TPU v7x, 512 devices: a whole 4x8x8 slice. The times are simulated.
512 devices in a mesh: section: 4 (over x), ctx: 64 (over z, y_lo, core), tp: 2 (over y_hi).
Axes of the slice: x: 4, y: 8 (y_hi: 2, y_lo: 4; y = y_hi * 4 + y_lo), z: 8, core: 2. Of those that a mesh axis runs over, the one named last changes fastest.
Arguments:
- teacher_hidden: bfloat16 [1024, 16384], P('ctx', ('section', 'tp')), may hold values from -21 to 21
- lm_head: bfloat16 [16384, 65536], P(('section', 'tp'), 'ctx'), may hold values from -2.5 to 2.5
- sampled_ids: int32 [1024], replicated, may hold values from 0 to 65535
- student_logprob: float32 [1024], replicated, may hold values from -24 to -4
- owner_map: int32 [1024], replicated, may hold values from 0 to 8191
- queries: bfloat16 [8192, 8192], P('ctx', ('section', 'tp')), may hold values from -108 to 108
- keys: bfloat16 [8192, 1024], P('ctx', ('section', 'tp')), may hold values from -6 to 6
- values: bfloat16 [8192, 1024], P('ctx', ('section', 'tp')), may hold values from -6 to 6
- grad_out: bfloat16 [8192, 8192], P('ctx', ('section', 'tp')), may hold values from -24 to 24
- segment_ids: int32 [8192], P('ctx'), may hold values from 0 to 15, never falling along the last dimension, each value on 1 to 1025 neighbouring positions
Outputs:
- advantage: float32 [1024], P(('section', 'tp'))
- d_queries: bfloat16 [8192, 8192], P('ctx', ('section', 'tp'))
- d_keys: bfloat16 [8192, 1024], P('ctx', ('section', 'tp'))
- d_values: bfloat16 [8192, 1024], P('ctx', ('section', 'tp'))
Inputs may be any that keep to these rules, and one draw needn't show every extreme that they name: `segment_ids`: segment numbers never fall along the sequence; a segment holds 1 to 1025 positions and one holds exactly 1025.
All inputs are finite; a program needn't handle non-finite values.
Results may differ from a plain program's by a relative error of at most 0.008.
Values may be sent and summed in bfloat16 or wider, within the bound.
No kernel may reach another device: no remote copies, remote signals or barrier semaphores. Data moves between devices by JAX's collectives and lax.ppermute only.
A program may use at most 128 MiB of HBM per device.

v0:
```python
import jax
import jax.numpy as jnp
from jax import lax
from jax.sharding import PartitionSpec as P

advantage_scale = 0.1
clip_bound = 8.0
masked_value = -1e30


def joined(shard, axis, combine):
    everything = jax.tree.map(lambda part: lax.all_gather(part, axis), shard)
    first = jax.tree.map(lambda part: part[0], everything)

    def hop(k, so_far):
        return combine(so_far, jax.tree.map(lambda part: part[k], everything))

    return lax.fori_loop(1, lax.axis_size(axis), hop, first)


def passed_along(block, axis, distance):
    devices = range(lax.axis_size(axis))
    route = [(i - distance, i) for i in devices if i - distance in devices]
    return lax.ppermute(block, axis, route)


def normalize(scores, allowed):
    masked = jnp.where(allowed, scores, masked_value)
    row_top = jnp.max(masked, axis=1, keepdims=True)
    row_total = jnp.sum(jnp.where(allowed, jnp.exp(masked - row_top), 0.0), axis=1, keepdims=True)
    log_norm = row_top + jnp.log(row_total)
    return jnp.where(allowed, jnp.exp(masked - log_norm), 0.0).astype(jnp.bfloat16)


def attend_block(query_rows, upstream, key_window, value_window, allowed, scaling):
    scores = jnp.dot(query_rows, key_window.T, preferred_element_type=jnp.float32) * scaling
    softmax = normalize(scores, allowed)
    context = jnp.dot(softmax, value_window, preferred_element_type=jnp.float32)
    row_delta = jnp.sum(upstream.astype(jnp.float32) * context, axis=1, keepdims=True)
    grad_prob = jnp.dot(upstream, value_window.T, preferred_element_type=jnp.float32)
    grad_score = (softmax.astype(jnp.float32) * (grad_prob - row_delta) * scaling).astype(
        jnp.bfloat16
    )
    grad_query = jnp.dot(grad_score, key_window, preferred_element_type=jnp.float32)
    grad_key = jnp.dot(grad_score.T, query_rows, preferred_element_type=jnp.float32)
    grad_value = jnp.dot(softmax.T, upstream, preferred_element_type=jnp.float32)
    return (grad_query, grad_key, grad_value)


def row_stats(logits, token_ids, vocab_start):
    columns = vocab_start + jnp.arange(logits.shape[1], dtype=jnp.int32)
    picked = jnp.sum(jnp.where(columns[None, :] == token_ids[:, None], logits, 0.0), axis=1)
    row_top = jnp.max(logits, axis=1)
    row_total = jnp.sum(jnp.exp(logits - row_top[:, None]), axis=1)

    def combine(earlier, later):
        highest = jnp.maximum(earlier[0], later[0])
        summed = earlier[1] * jnp.exp(earlier[0] - highest) + later[1] * jnp.exp(later[0] - highest)
        return (highest, summed, earlier[2] + later[2])

    row_top, row_total, picked = joined((row_top, row_total, picked), "ctx", combine)
    return picked - row_top - jnp.log(row_total)


def body(
    teacher_hidden,
    lm_head,
    sampled_ids,
    student_logprob,
    owner_map,
    queries,
    keys,
    values,
    grad_out,
    segment_ids,
):
    ctx_index = lax.axis_index("ctx")
    block_count = lax.axis_size(("section", "tp"))
    block_index = lax.axis_index(("section", "tp"))
    gathered = lax.all_gather(teacher_hidden, "ctx", axis=0, tiled=True)
    vocab_start = ctx_index * lm_head.shape[1]
    row_count = gathered.shape[0] // block_count
    logits = lax.psum_scatter(
        jnp.dot(gathered, lm_head, preferred_element_type=jnp.float32),
        ("section", "tp"),
        scatter_dimension=0,
        tiled=True,
    )
    first_row = block_index * row_count
    token_ids = lax.dynamic_slice_in_dim(sampled_ids, first_row, row_count, 0)
    student_rows = lax.dynamic_slice_in_dim(student_logprob, first_row, row_count, 0)
    teacher_logprob = row_stats(logits, token_ids, vocab_start)
    advantage = jnp.clip(teacher_logprob - student_rows, -clip_bound, clip_bound)
    advantage_all = lax.all_gather(advantage, ("section", "tp"), axis=0, tiled=True)
    seq_rows = queries.shape[0]
    query_position = ctx_index * seq_rows + jnp.arange(seq_rows, dtype=jnp.int32)
    routed = jnp.sum(
        jnp.where(owner_map[None, :] == query_position[:, None], advantage_all[None, :], 0.0),
        axis=1,
    )
    weight = 1.0 + advantage_scale * routed
    grad_rows = (weight[:, None] * grad_out.astype(jnp.float32)).astype(jnp.bfloat16)
    head_dim = keys.shape[1]
    queries_per_group = queries.shape[1] // head_dim
    farthest = min(8, lax.axis_size("ctx") - 1)
    scaling = head_dim ** (-0.5)
    local_block = (keys, values, segment_ids)
    arrivals = []
    carried = local_block
    for distance in range(farthest):
        carried = passed_along((carried[0], carried[1], carried[2]), "ctx", 1)
        arrivals.append(carried)
    window = arrivals[::-1] + [local_block]
    distances = list(range(farthest, -1, -1))
    key_segment = jnp.concatenate([member[2] for member in window], axis=0)
    key_position = jnp.concatenate(
        [
            (ctx_index - distance) * seq_rows + jnp.arange(seq_rows, dtype=jnp.int32)
            for distance in distances
        ],
        axis=0,
    )
    doc_mask = (
        (key_segment[None, :] == segment_ids[:, None])
        & (key_position[None, :] <= query_position[:, None])
        & (key_position[None, :] >= 0)
    )
    query_rows = (
        queries.reshape(seq_rows, queries_per_group, head_dim)
        .transpose(1, 0, 2)
        .reshape(queries_per_group * seq_rows, head_dim)
    )
    upstream_rows = (
        grad_rows.reshape(seq_rows, queries_per_group, head_dim)
        .transpose(1, 0, 2)
        .reshape(queries_per_group * seq_rows, head_dim)
    )
    key_window = jnp.concatenate([member[0] for member in window], axis=0)
    value_window = jnp.concatenate([member[1] for member in window], axis=0)
    grad_query, grad_key, grad_value = attend_block(
        query_rows,
        upstream_rows,
        key_window,
        value_window,
        jnp.tile(doc_mask, (queries_per_group, 1)),
        scaling,
    )
    key_list = jnp.split(grad_key, farthest + 1, axis=0)
    value_list = jnp.split(grad_value, farthest + 1, axis=0)
    carried_grads = (key_list[0], value_list[0])
    for distance in range(farthest, 0, -1):
        arrived = passed_along((carried_grads[0], carried_grads[1]), "ctx", -1)
        carried_grads = (
            arrived[0] + key_list[farthest - distance + 1],
            arrived[1] + value_list[farthest - distance + 1],
        )
    key_total, value_total = carried_grads
    d_queries = (
        grad_query.astype(jnp.bfloat16)
        .reshape(queries_per_group, seq_rows, head_dim)
        .transpose(1, 0, 2)
        .reshape(seq_rows, queries_per_group * head_dim)
    )
    return (advantage, d_queries, key_total.astype(jnp.bfloat16), value_total.astype(jnp.bfloat16))


def solution(mesh):
    in_specs = (
        P("ctx", ("section", "tp")),
        P(("section", "tp"), "ctx"),
        P(),
        P(),
        P(),
        P("ctx", ("section", "tp")),
        P("ctx", ("section", "tp")),
        P("ctx", ("section", "tp")),
        P("ctx", ("section", "tp")),
        P("ctx"),
    )
    out_specs = (
        P(("section", "tp")),
        P("ctx", ("section", "tp")),
        P("ctx", ("section", "tp")),
        P("ctx", ("section", "tp")),
    )
    return jax.shard_map(body, mesh=mesh, in_specs=in_specs, out_specs=out_specs, check_vma=False)
```

profile of v0, /device:TPU:217, one launch (start us, length us, event | category | flops | bytes accessed | tf_op | source)
XLA Modules:
  0.0 641.0 jit_solution(16636599793859464002)
XLA Ops:
  7.9 122.5 %all-gather.9.cloned.1.call-done = bf16[1024,2048]{1,0:T(8,128)(2,1)} async-done(((bf16[16,2048]{1,0:T(8,128)(2,1)}), bf16[1024,2048]{1,0:T(8,128)(2,1)}) %all-gather.9.cloned.1.call-update) | async-done | bytes 4194320 | tf_op jit(solution)/shard_map/all_gather | solution.py:80
  130.5 9.9 %fusion.21 = f32[1024,1024]{1,0:T(8,128)} fusion(bf16[1024,2048]{1,0:T(8,128)(2,1)} %all-gather.9.cloned.1.call-done, bf16[2048,1024]{1,0:T(8,128)(2,1)} %param.13), kind=kOutput, calls=%fused_computation.97 | convolution fusion | flops 4294967296 | bytes 12582912 | tf_op jit(solution)/shard_map/dot_general | solution.py:84
  141.1 3.8 collective-permute-start.16
  145.0 2.1 collective-permute-start.8
  147.2 3.0 collective-permute-start
  150.9 8.0 %collective-permute-start.1 = (s32[128]{0:T(128)S(1)}, s32[128]{0:T(128)S(1)}, u32[]{:S(2)}, u32[]{:S(2)}) collective-permute-start(s32[128]{0:T(128)S(1)} %collective-permute-done), channel_id=1, source_target_pairs={{0,2},{2,4},{4,6},{6,8},{8,10},{10,12},{12,14},{14,16},{16,18},{18... | collective-permute-start | bytes 1544 | tf_op jit(solution)/shard_map/ppermute | solution.py:24
  159.7 9.7 %collective-permute-start.2 = (s32[128]{0:T(128)S(1)}, s32[128]{0:T(128)S(1)}, u32[]{:S(2)}, u32[]{:S(2)}) collective-permute-start(s32[128]{0:T(128)S(1)} %collective-permute-done.1), channel_id=1, source_target_pairs={{0,2},{2,4},{4,6},{6,8},{8,10},{10,12},{12,14},{14,16},{16,18},{18... | collective-permute-start | bytes 1544 | tf_op jit(solution)/shard_map/ppermute | solution.py:24
  170.1 8.0 %collective-permute-start.3 = (s32[128]{0:T(128)S(1)}, s32[128]{0:T(128)S(1)}, u32[]{:S(2)}, u32[]{:S(2)}) collective-permute-start(s32[128]{0:T(128)S(1)} %collective-permute-done.2), channel_id=1, source_target_pairs={{0,2},{2,4},{4,6},{6,8},{8,10},{10,12},{12,14},{14,16},{16,18},{18... | collective-permute-start | bytes 1544 | tf_op jit(solution)/shard_map/ppermute | solution.py:24
  178.8 8.1 %collective-permute-start.4 = (s32[128]{0:T(128)S(1)}, s32[128]{0:T(128)S(1)}, u32[]{:S(2)}, u32[]{:S(2)}) collective-permute-start(s32[128]{0:T(128)S(1)} %collective-permute-done.3), channel_id=1, source_target_pairs={{0,2},{2,4},{4,6},{6,8},{8,10},{10,12},{12,14},{14,16},{16,18},{18... | collective-permute-start | bytes 1544 | tf_op jit(solution)/shard_map/ppermute | solution.py:24
  187.6 8.0 %collective-permute-start.5 = (s32[128]{0:T(128)S(1)}, s32[128]{0:T(128)S(1)}, u32[]{:S(2)}, u32[]{:S(2)}) collective-permute-start(s32[128]{0:T(128)S(1)} %collective-permute-done.4), channel_id=1, source_target_pairs={{0,2},{2,4},{4,6},{6,8},{8,10},{10,12},{12,14},{14,16},{16,18},{18... | collective-permute-start | bytes 1544 | tf_op jit(solution)/shard_map/ppermute | solution.py:24
  196.4 8.1 %collective-permute-start.6 = (s32[128]{0:T(128)S(1)}, s32[128]{0:T(128)S(1)}, u32[]{:S(2)}, u32[]{:S(2)}) collective-permute-start(s32[128]{0:T(128)S(1)} %collective-permute-done.5), channel_id=1, source_target_pairs={{0,2},{2,4},{4,6},{6,8},{8,10},{10,12},{12,14},{14,16},{16,18},{18... | collective-permute-start | bytes 1544 | tf_op jit(solution)/shard_map/ppermute | solution.py:24
  205.1 8.1 %collective-permute-start.7 = (s32[128]{0:T(128)S(1)}, s32[128]{0:T(128)S(1)}, u32[]{:S(2)}, u32[]{:S(2)}) collective-permute-start(s32[128]{0:T(128)S(1)} %collective-permute-done.6), channel_id=1, source_target_pairs={{0,2},{2,4},{4,6},{6,8},{8,10},{10,12},{12,14},{14,16},{16,18},{18... | collective-permute-start | bytes 1544 | tf_op jit(solution)/shard_map/ppermute | solution.py:24
  214.4 7.7 %collective-permute-start.17 = (bf16[128,128]{1,0:T(8,128)(2,1)S(1)}, bf16[128,128]{1,0:T(8,128)(2,1)S(1)}, u32[]{:S(2)}, u32[]{:S(2)}) collective-permute-start(bf16[128,128]{1,0:T(8,128)(2,1)S(1)} %collective-permute-done.16), channel_id=1, source_target_pairs={{0,2},{2,4},{4,6},{6,8},{8,10},{10,12},{12,14},{14,16},{16,18},{18... | collective-permute-start | bytes 98312 | tf_op jit(solution)/shard_map/ppermute | solution.py:24
  222.1 1.9 collective-permute-start.9
  224.0 7.2 %collective-permute-start.18 = (bf16[128,128]{1,0:T(8,128)(2,1)S(1)}, bf16[128,128]{1,0:T(8,128)(2,1)S(1)}, u32[]{:S(2)}, u32[]{:S(2)}) collective-permute-start(bf16[128,128]{1,0:T(8,128)(2,1)S(1)} %collective-permute-done.17), channel_id=1, source_target_pairs={{0,2},{2,4},{4,6},{6,8},{8,10},{10,12},{12,14},{14,16},{16,18},{18... | collective-permute-start | bytes 98312 | tf_op jit(solution)/shard_map/ppermute | solution.py:24
  231.2 1.9 collective-permute-start.10
  233.1 7.2 %collective-permute-start.19 = (bf16[128,128]{1,0:T(8,128)(2,1)S(1)}, bf16[128,128]{1,0:T(8,128)(2,1)S(1)}, u32[]{:S(2)}, u32[]{:S(2)}) collective-permute-start(bf16[128,128]{1,0:T(8,128)(2,1)S(1)} %collective-permute-done.18), channel_id=1, source_target_pairs={{0,2},{2,4},{4,6},{6,8},{8,10},{10,12},{12,14},{14,16},{16,18},{18... | collective-permute-start | bytes 98312 | tf_op jit(solution)/shard_map/ppermute | solution.py:24
  240.3 1.9 collective-permute-start.11
  242.3 7.2 %collective-permute-start.20 = (bf16[128,128]{1,0:T(8,128)(2,1)S(1)}, bf16[128,128]{1,0:T(8,128)(2,1)S(1)}, u32[]{:S(2)}, u32[]{:S(2)}) collective-permute-start(bf16[128,128]{1,0:T(8,128)(2,1)S(1)} %collective-permute-done.19), channel_id=1, source_target_pairs={{0,2},{2,4},{4,6},{6,8},{8,10},{10,12},{12,14},{14,16},{16,18},{18... | collective-permute-start | bytes 98312 | tf_op jit(solution)/shard_map/ppermute | solution.py:24
  249.4 2.0 collective-permute-start.12
  251.5 7.8 %collective-permute-start.21 = (bf16[128,128]{1,0:T(8,128)(2,1)S(1)}, bf16[128,128]{1,0:T(8,128)(2,1)S(1)}, u32[]{:S(2)}, u32[]{:S(2)}) collective-permute-start(bf16[128,128]{1,0:T(8,128)(2,1)S(1)} %collective-permute-done.20), channel_id=1, source_target_pairs={{0,2},{2,4},{4,6},{6,8},{8,10},{10,12},{12,14},{14,16},{16,18},{18... | collective-permute-start | bytes 98312 | tf_op jit(solution)/shard_map/ppermute | solution.py:24
  259.3 2.3 collective-permute-start.13
  261.6 6.8 %collective-permute-start.22 = (bf16[128,128]{1,0:T(8,128)(2,1)S(1)}, bf16[128,128]{1,0:T(8,128)(2,1)S(1)}, u32[]{:S(2)}, u32[]{:S(2)}) collective-permute-start(bf16[128,128]{1,0:T(8,128)(2,1)S(1)} %collective-permute-done.21), channel_id=1, source_target_pairs={{0,2},{2,4},{4,6},{6,8},{8,10},{10,12},{12,14},{14,16},{16,18},{18... | collective-permute-start | bytes 98312 | tf_op jit(solution)/shard_map/ppermute | solution.py:24
  268.4 2.3 collective-permute-start.14
  270.7 6.8 %collective-permute-start.23 = (bf16[128,128]{1,0:T(8,128)(2,1)S(1)}, bf16[128,128]{1,0:T(8,128)(2,1)S(1)}, u32[]{:S(2)}, u32[]{:S(2)}) collective-permute-start(bf16[128,128]{1,0:T(8,128)(2,1)S(1)} %collective-permute-done.22), channel_id=1, source_target_pairs={{0,2},{2,4},{4,6},{6,8},{8,10},{10,12},{12,14},{14,16},{16,18},{18... | collective-permute-start | bytes 98312 | tf_op jit(solution)/shard_map/ppermute | solution.py:24
  278.6 1.9 collective-permute-start.15
  287.3 75.6 %all-gather.3 = f32[64,1,128]{2,1,0:T(1,128)S(1)} all-gather(f32[1,1,128]{2,1,0:T(1,128)S(1)} %bitcast.94), channel_id=2, replica_groups=mesh['section'=4,'ctx'=64,'tp'=2] {'ctx'}, dimensions={0}, use_global_device_ids=true | all-gather | bytes 33280 | tf_op jit(solution)/shard_map/all_gather | solution.py:12
  362.9 1.3 select_reduce_fusion.2
  364.2 73.3 %all-gather.4 = f32[64,1,128]{2,1,0:T(1,128)S(1)} all-gather(f32[1,1,128]{2,1,0:T(1,128)S(1)} %bitcast.97), channel_id=3, replica_groups=mesh['section'=4,'ctx'=64,'tp'=2] {'ctx'}, dimensions={0}, use_global_device_ids=true | all-gather | bytes 33280 | tf_op jit(solution)/shard_map/all_gather | solution.py:12
  437.5 75.2 %all-gather.5 = f32[64,1,128]{2,1,0:T(1,128)S(1)} all-gather(f32[1,1,128]{2,1,0:T(1,128)S(1)} %bitcast.96), channel_id=4, replica_groups=mesh['section'=4,'ctx'=64,'tp'=2] {'ctx'}, dimensions={0}, use_global_device_ids=true | all-gather | bytes 33280 | tf_op jit(solution)/shard_map/all_gather | solution.py:12
  512.8 3.0 while.19
  516.5 29.8 %all-gather.6 = f32[8,1,128]{2,1,0:T(1,128)S(1)} all-gather(f32[1,1,128]{2,1,0:T(1,128)S(1)} %bitcast.95), channel_id=1, replica_groups=mesh['section'=4,'ctx'=64,'tp'=2] {'section','tp'}, dimensions={0}, use_global_device_ids=true | all-gather | bytes 4608 | tf_op jit(solution)/shard_map/all_gather | solution.py:94
  550.0 5.9 collective-permute-start.24
  557.5 1.9 collective-permute-start.32
  559.4 2.2 collective-permute-done.24
  561.7 1.9 collective-permute-start.25
  563.6 3.4 collective-permute-done.32
  567.0 1.9 collective-permute-start.33
  568.9 2.2 collective-permute-done.25
  571.2 1.9 collective-permute-start.26
  573.1 3.4 collective-permute-done.33
  576.5 1.9 collective-permute-start.34
  578.5 2.2 collective-permute-done.26
  580.7 1.9 collective-permute-start.27
  582.6 3.4 collective-permute-done.34
  586.0 1.9 collective-permute-start.35
  588.0 2.2 collective-permute-done.27
  590.2 1.9 collective-permute-start.28
  592.1 3.4 collective-permute-done.35
  595.5 1.9 collective-permute-start.36
  597.5 2.2 collective-permute-done.28
  599.7 1.9 collective-permute-start.29
  601.6 3.4 collective-permute-done.36
  605.0 1.9 collective-permute-start.37
  607.0 2.2 collective-permute-done.29
  609.2 1.9 collective-permute-start.30
  611.1 3.4 collective-permute-done.37
  614.5 1.9 collective-permute-start.38
  616.5 2.2 collective-permute-done.30
  618.7 1.9 collective-permute-start.31
  620.6 3.4 collective-permute-done.38
  624.0 1.9 collective-permute-start.39
  626.0 2.2 collective-permute-done.31
  628.8 4.7 collective-permute-done.39
  (194 shorter events, 24.3 us)
Async XLA Ops:
  7.2 123.3 %all-gather.9.cloned.1.call-start = ((), (), s32[]{:S(2)}) async-start(), calls=%async_computation.1 | async-start | bytes 4259840 | tf_op jit(solution)/shard_map/all_gather | solution.py:80
  7.9 278.2 %reduce-scatter.2.cloned.1.call-start = ((), (), s32[]{:S(2)}) async-start(), calls=%async_computation.2 | async-start | bytes 4718592 | tf_op jit(solution)/shard_map/reduce_scatter | solution.py:83
  140.4 0.8 copy-start.2
  140.4 4.6 copy-start.3
  140.4 6.8 %copy-start.8 = (s32[128]{0:T(128)S(1)}, s32[128]{0:T(128)}, u32[]{:S(2)}) copy-start(s32[128]{0:T(128)} %param.21) | copy-start | bytes 1540
  140.4 72.8 %copy-start.1 = (bf16[128,1024]{1,0:T(8,128)(2,1)S(1)}, bf16[128,1024]{1,0:T(8,128)(2,1)}, u32[]{:S(2)}) copy-start(bf16[128,1024]{1,0:T(8,128)(2,1)} %param.17) | copy-start | bytes 786436
  141.1 73.2 %collective-permute-start.16 = (bf16[128,128]{1,0:T(8,128)(2,1)S(1)}, bf16[128,128]{1,0:T(8,128)(2,1)S(1)}, u32[]{:S(2)}, u32[]{:S(2)}) collective-permute-start(bf16[128,128]{1,0:T(8,128)(2,1)S(1)} %copy-done.2), channel_id=1, source_target_pairs={{0,2},{2,4},{4,6},{6,8},{8,10},{10,12},{12,14},{14,16},{16,18},{18... | collective-permute-start | bytes 98312 | tf_op jit(solution)/shard_map/ppermute | solution.py:24
  145.0 77.0 %collective-permute-start.8 = (bf16[128,128]{1,0:T(8,128)(2,1)S(1)}, bf16[128,128]{1,0:T(8,128)(2,1)S(1)}, u32[]{:S(2)}, u32[]{:S(2)}) collective-permute-start(bf16[128,128]{1,0:T(8,128)(2,1)S(1)} %copy-done.3), channel_id=1, source_target_pairs={{0,2},{2,4},{4,6},{6,8},{8,10},{10,12},{12,14},{14,16},{16,18},{18... | collective-permute-start | bytes 98312 | tf_op jit(solution)/shard_map/ppermute | solution.py:24
  147.2 3.7 collective-permute-start
  150.9 8.8 %collective-permute-start.1 = (s32[128]{0:T(128)S(1)}, s32[128]{0:T(128)S(1)}, u32[]{:S(2)}, u32[]{:S(2)}) collective-permute-start(s32[128]{0:T(128)S(1)} %collective-permute-done), channel_id=1, source_target_pairs={{0,2},{2,4},{4,6},{6,8},{8,10},{10,12},{12,14},{14,16},{16,18},{18... | collective-permute-start | bytes 1544 | tf_op jit(solution)/shard_map/ppermute | solution.py:24
  159.7 10.4 %collective-permute-start.2 = (s32[128]{0:T(128)S(1)}, s32[128]{0:T(128)S(1)}, u32[]{:S(2)}, u32[]{:S(2)}) collective-permute-start(s32[128]{0:T(128)S(1)} %collective-permute-done.1), channel_id=1, source_target_pairs={{0,2},{2,4},{4,6},{6,8},{8,10},{10,12},{12,14},{14,16},{16,18},{18... | collective-permute-start | bytes 1544 | tf_op jit(solution)/shard_map/ppermute | solution.py:24
  170.1 8.8 %collective-permute-start.3 = (s32[128]{0:T(128)S(1)}, s32[128]{0:T(128)S(1)}, u32[]{:S(2)}, u32[]{:S(2)}) collective-permute-start(s32[128]{0:T(128)S(1)} %collective-permute-done.2), channel_id=1, source_target_pairs={{0,2},{2,4},{4,6},{6,8},{8,10},{10,12},{12,14},{14,16},{16,18},{18... | collective-permute-start | bytes 1544 | tf_op jit(solution)/shard_map/ppermute | solution.py:24
  178.8 8.8 %collective-permute-start.4 = (s32[128]{0:T(128)S(1)}, s32[128]{0:T(128)S(1)}, u32[]{:S(2)}, u32[]{:S(2)}) collective-permute-start(s32[128]{0:T(128)S(1)} %collective-permute-done.3), channel_id=1, source_target_pairs={{0,2},{2,4},{4,6},{6,8},{8,10},{10,12},{12,14},{14,16},{16,18},{18... | collective-permute-start | bytes 1544 | tf_op jit(solution)/shard_map/ppermute | solution.py:24
  187.6 8.8 %collective-permute-start.5 = (s32[128]{0:T(128)S(1)}, s32[128]{0:T(128)S(1)}, u32[]{:S(2)}, u32[]{:S(2)}) collective-permute-start(s32[128]{0:T(128)S(1)} %collective-permute-done.4), channel_id=1, source_target_pairs={{0,2},{2,4},{4,6},{6,8},{8,10},{10,12},{12,14},{14,16},{16,18},{18... | collective-permute-start | bytes 1544 | tf_op jit(solution)/shard_map/ppermute | solution.py:24
  196.4 8.8 %collective-permute-start.6 = (s32[128]{0:T(128)S(1)}, s32[128]{0:T(128)S(1)}, u32[]{:S(2)}, u32[]{:S(2)}) collective-permute-start(s32[128]{0:T(128)S(1)} %collective-permute-done.5), channel_id=1, source_target_pairs={{0,2},{2,4},{4,6},{6,8},{8,10},{10,12},{12,14},{14,16},{16,18},{18... | collective-permute-start | bytes 1544 | tf_op jit(solution)/shard_map/ppermute | solution.py:24
  205.1 9.2 %collective-permute-start.7 = (s32[128]{0:T(128)S(1)}, s32[128]{0:T(128)S(1)}, u32[]{:S(2)}, u32[]{:S(2)}) collective-permute-start(s32[128]{0:T(128)S(1)} %collective-permute-done.6), channel_id=1, source_target_pairs={{0,2},{2,4},{4,6},{6,8},{8,10},{10,12},{12,14},{14,16},{16,18},{18... | collective-permute-start | bytes 1544 | tf_op jit(solution)/shard_map/ppermute | solution.py:24
  214.4 9.6 %collective-permute-start.17 = (bf16[128,128]{1,0:T(8,128)(2,1)S(1)}, bf16[128,128]{1,0:T(8,128)(2,1)S(1)}, u32[]{:S(2)}, u32[]{:S(2)}) collective-permute-start(bf16[128,128]{1,0:T(8,128)(2,1)S(1)} %collective-permute-done.16), channel_id=1, source_target_pairs={{0,2},{2,4},{4,6},{6,8},{8,10},{10,12},{12,14},{14,16},{16,18},{18... | collective-permute-start | bytes 98312 | tf_op jit(solution)/shard_map/ppermute | solution.py:24
  222.1 9.1 %collective-permute-start.9 = (bf16[128,128]{1,0:T(8,128)(2,1)S(1)}, bf16[128,128]{1,0:T(8,128)(2,1)S(1)}, u32[]{:S(2)}, u32[]{:S(2)}) collective-permute-start(bf16[128,128]{1,0:T(8,128)(2,1)S(1)} %collective-permute-done.8), channel_id=1, source_target_pairs={{0,2},{2,4},{4,6},{6,8},{8,10},{10,12},{12,14},{14,16},{16,18},{18... | collective-permute-start | bytes 98312 | tf_op jit(solution)/shard_map/ppermute | solution.py:24
  224.0 9.1 %collective-permute-start.18 = (bf16[128,128]{1,0:T(8,128)(2,1)S(1)}, bf16[128,128]{1,0:T(8,128)(2,1)S(1)}, u32[]{:S(2)}, u32[]{:S(2)}) collective-permute-start(bf16[128,128]{1,0:T(8,128)(2,1)S(1)} %collective-permute-done.17), channel_id=1, source_target_pairs={{0,2},{2,4},{4,6},{6,8},{8,10},{10,12},{12,14},{14,16},{16,18},{18... | collective-permute-start | bytes 98312 | tf_op jit(solution)/shard_map/ppermute | solution.py:24
  231.2 9.1 %collective-permute-start.10 = (bf16[128,128]{1,0:T(8,128)(2,1)S(1)}, bf16[128,128]{1,0:T(8,128)(2,1)S(1)}, u32[]{:S(2)}, u32[]{:S(2)}) collective-permute-start(bf16[128,128]{1,0:T(8,128)(2,1)S(1)} %collective-permute-done.9), channel_id=1, source_target_pairs={{0,2},{2,4},{4,6},{6,8},{8,10},{10,12},{12,14},{14,16},{16,18},{18... | collective-permute-start | bytes 98312 | tf_op jit(solution)/shard_map/ppermute | solution.py:24
  233.1 9.1 %collective-permute-start.19 = (bf16[128,128]{1,0:T(8,128)(2,1)S(1)}, bf16[128,128]{1,0:T(8,128)(2,1)S(1)}, u32[]{:S(2)}, u32[]{:S(2)}) collective-permute-start(bf16[128,128]{1,0:T(8,128)(2,1)S(1)} %collective-permute-done.18), channel_id=1, source_target_pairs={{0,2},{2,4},{4,6},{6,8},{8,10},{10,12},{12,14},{14,16},{16,18},{18... | collective-permute-start | bytes 98312 | tf_op jit(solution)/shard_map/ppermute | solution.py:24
  240.3 9.1 %collective-permute-start.11 = (bf16[128,128]{1,0:T(8,128)(2,1)S(1)}, bf16[128,128]{1,0:T(8,128)(2,1)S(1)}, u32[]{:S(2)}, u32[]{:S(2)}) collective-permute-start(bf16[128,128]{1,0:T(8,128)(2,1)S(1)} %collective-permute-done.10), channel_id=1, source_target_pairs={{0,2},{2,4},{4,6},{6,8},{8,10},{10,12},{12,14},{14,16},{16,18},{18... | collective-permute-start | bytes 98312 | tf_op jit(solution)/shard_map/ppermute | solution.py:24
  242.3 9.2 %collective-permute-start.20 = (bf16[128,128]{1,0:T(8,128)(2,1)S(1)}, bf16[128,128]{1,0:T(8,128)(2,1)S(1)}, u32[]{:S(2)}, u32[]{:S(2)}) collective-permute-start(bf16[128,128]{1,0:T(8,128)(2,1)S(1)} %collective-permute-done.19), channel_id=1, source_target_pairs={{0,2},{2,4},{4,6},{6,8},{8,10},{10,12},{12,14},{14,16},{16,18},{18... | collective-permute-start | bytes 98312 | tf_op jit(solution)/shard_map/ppermute | solution.py:24
  249.4 9.8 %collective-permute-start.12 = (bf16[128,128]{1,0:T(8,128)(2,1)S(1)}, bf16[128,128]{1,0:T(8,128)(2,1)S(1)}, u32[]{:S(2)}, u32[]{:S(2)}) collective-permute-start(bf16[128,128]{1,0:T(8,128)(2,1)S(1)} %collective-permute-done.11), channel_id=1, source_target_pairs={{0,2},{2,4},{4,6},{6,8},{8,10},{10,12},{12,14},{14,16},{16,18},{18... | collective-permute-start | bytes 98312 | tf_op jit(solution)/shard_map/ppermute | solution.py:24
  251.5 10.1 %collective-permute-start.21 = (bf16[128,128]{1,0:T(8,128)(2,1)S(1)}, bf16[128,128]{1,0:T(8,128)(2,1)S(1)}, u32[]{:S(2)}, u32[]{:S(2)}) collective-permute-start(bf16[128,128]{1,0:T(8,128)(2,1)S(1)} %collective-permute-done.20), channel_id=1, source_target_pairs={{0,2},{2,4},{4,6},{6,8},{8,10},{10,12},{12,14},{14,16},{16,18},{18... | collective-permute-start | bytes 98312 | tf_op jit(solution)/shard_map/ppermute | solution.py:24
  259.3 9.1 %collective-permute-start.13 = (bf16[128,128]{1,0:T(8,128)(2,1)S(1)}, bf16[128,128]{1,0:T(8,128)(2,1)S(1)}, u32[]{:S(2)}, u32[]{:S(2)}) collective-permute-start(bf16[128,128]{1,0:T(8,128)(2,1)S(1)} %collective-permute-done.12), channel_id=1, source_target_pairs={{0,2},{2,4},{4,6},{6,8},{8,10},{10,12},{12,14},{14,16},{16,18},{18... | collective-permute-start | bytes 98312 | tf_op jit(solution)/shard_map/ppermute | solution.py:24
  261.6 9.1 %collective-permute-start.22 = (bf16[128,128]{1,0:T(8,128)(2,1)S(1)}, bf16[128,128]{1,0:T(8,128)(2,1)S(1)}, u32[]{:S(2)}, u32[]{:S(2)}) collective-permute-start(bf16[128,128]{1,0:T(8,128)(2,1)S(1)} %collective-permute-done.21), channel_id=1, source_target_pairs={{0,2},{2,4},{4,6},{6,8},{8,10},{10,12},{12,14},{14,16},{16,18},{18... | collective-permute-start | bytes 98312 | tf_op jit(solution)/shard_map/ppermute | solution.py:24
  268.4 10.2 %collective-permute-start.14 = (bf16[128,128]{1,0:T(8,128)(2,1)S(1)}, bf16[128,128]{1,0:T(8,128)(2,1)S(1)}, u32[]{:S(2)}, u32[]{:S(2)}) collective-permute-start(bf16[128,128]{1,0:T(8,128)(2,1)S(1)} %collective-permute-done.13), channel_id=1, source_target_pairs={{0,2},{2,4},{4,6},{6,8},{8,10},{10,12},{12,14},{14,16},{16,18},{18... | collective-permute-start | bytes 98312 | tf_op jit(solution)/shard_map/ppermute | solution.py:24
  270.7 9.8 %collective-permute-start.23 = (bf16[128,128]{1,0:T(8,128)(2,1)S(1)}, bf16[128,128]{1,0:T(8,128)(2,1)S(1)}, u32[]{:S(2)}, u32[]{:S(2)}) collective-permute-start(bf16[128,128]{1,0:T(8,128)(2,1)S(1)} %collective-permute-done.22), channel_id=1, source_target_pairs={{0,2},{2,4},{4,6},{6,8},{8,10},{10,12},{12,14},{14,16},{16,18},{18... | collective-permute-start | bytes 98312 | tf_op jit(solution)/shard_map/ppermute | solution.py:24
  278.6 3.1 collective-permute-start.15
  281.8 1.7 copy-start.5
  284.8 261.6 %copy-start.4 = (s32[1024]{0:T(1024)S(1)}, s32[1024]{0:T(1024)}, u32[]{:S(2)}) copy-start(s32[1024]{0:T(1024)} %param.16) | copy-start | bytes 12292
  284.8 261.7 %copy-start = (bf16[128,1024]{1,0:T(8,128)(2,1)S(1)}, bf16[128,1024]{1,0:T(8,128)(2,1)}, u32[]{:S(2)}) copy-start(bf16[128,1024]{1,0:T(8,128)(2,1)} %param.20) | copy-start | bytes 786436
  516.5 31.8 %copy-start.7 = (f32[128]{0:T(128)}, f32[128]{0:T(128)S(1)}, u32[]{:S(2)}) copy-start(f32[128]{0:T(128)S(1)} %subtract_clamp_fusion) | copy-start | bytes 1540
  548.4 7.5 %copy-start.6 = (bf16[1152,128]{1,0:T(8,128)(2,1)S(1)}, bf16[1152,128]{1,0:T(8,128)(2,1)}, u32[]{:S(2)}) copy-start(bf16[1152,128]{1,0:T(8,128)(2,1)} %copy-done.5) | copy-start | bytes 884740
  550.0 11.6 %collective-permute-start.24 = (f32[128,128]{1,0:T(8,128)S(1)}, f32[128,128]{1,0:T(8,128)S(1)}, u32[]{:S(2)}, u32[]{:S(2)}) collective-permute-start(f32[128,128]{1,0:T(8,128)S(1)} %split.72), channel_id=1, source_target_pairs={{2,0},{4,2},{6,4},{8,6},{10,8},{12,10},{14,12},{16,14},{18,16},{20... | collective-permute-start | bytes 196616 | tf_op jit(solution)/shard_map/ppermute | solution.py:24
  557.5 9.5 %collective-permute-start.32 = (f32[128,128]{1,0:T(8,128)S(1)}, f32[128,128]{1,0:T(8,128)S(1)}, u32[]{:S(2)}, u32[]{:S(2)}) collective-permute-start(f32[128,128]{1,0:T(8,128)S(1)} %split.81), channel_id=1, source_target_pairs={{2,0},{4,2},{6,4},{8,6},{10,8},{12,10},{14,12},{16,14},{18,16},{20... | collective-permute-start | bytes 196616 | tf_op jit(solution)/shard_map/ppermute | solution.py:24
  561.7 9.5 %collective-permute-start.25 = (f32[128,128]{1,0:T(8,128)S(1)}, f32[128,128]{1,0:T(8,128)S(1)}, u32[]{:S(2)}, u32[]{:S(2)}) collective-permute-start(f32[128,128]{1,0:T(8,128)S(1)} %slice_add_fusion.15), channel_id=1, source_target_pairs={{2,0},{4,2},{6,4},{8,6},{10,8},{12,10},{14,12},{16,14},{18,16},{20... | collective-permute-start | bytes 196616 | tf_op jit(solution)/shard_map/ppermute | solution.py:24
  567.0 9.5 %collective-permute-start.33 = (f32[128,128]{1,0:T(8,128)S(1)}, f32[128,128]{1,0:T(8,128)S(1)}, u32[]{:S(2)}, u32[]{:S(2)}) collective-permute-start(f32[128,128]{1,0:T(8,128)S(1)} %slice_add_fusion.7), channel_id=1, source_target_pairs={{2,0},{4,2},{6,4},{8,6},{10,8},{12,10},{14,12},{16,14},{18,16},{20... | collective-permute-start | bytes 196616 | tf_op jit(solution)/shard_map/ppermute | solution.py:24
  571.2 9.5 %collective-permute-start.26 = (f32[128,128]{1,0:T(8,128)S(1)}, f32[128,128]{1,0:T(8,128)S(1)}, u32[]{:S(2)}, u32[]{:S(2)}) collective-permute-start(f32[128,128]{1,0:T(8,128)S(1)} %slice_add_fusion.14), channel_id=1, source_target_pairs={{2,0},{4,2},{6,4},{8,6},{10,8},{12,10},{14,12},{16,14},{18,16},{20... | collective-permute-start | bytes 196616 | tf_op jit(solution)/shard_map/ppermute | solution.py:24
  576.5 9.5 %collective-permute-start.34 = (f32[128,128]{1,0:T(8,128)S(1)}, f32[128,128]{1,0:T(8,128)S(1)}, u32[]{:S(2)}, u32[]{:S(2)}) collective-permute-start(f32[128,128]{1,0:T(8,128)S(1)} %slice_add_fusion.6), channel_id=1, source_target_pairs={{2,0},{4,2},{6,4},{8,6},{10,8},{12,10},{14,12},{16,14},{18,16},{20... | collective-permute-start | bytes 196616 | tf_op jit(solution)/shard_map/ppermute | solution.py:24
  580.7 9.5 %collective-permute-start.27 = (f32[128,128]{1,0:T(8,128)S(1)}, f32[128,128]{1,0:T(8,128)S(1)}, u32[]{:S(2)}, u32[]{:S(2)}) collective-permute-start(f32[128,128]{1,0:T(8,128)S(1)} %slice_add_fusion.13), channel_id=1, source_target_pairs={{2,0},{4,2},{6,4},{8,6},{10,8},{12,10},{14,12},{16,14},{18,16},{20... | collective-permute-start | bytes 196616 | tf_op jit(solution)/shard_map/ppermute | solution.py:24
  586.0 9.5 %collective-permute-start.35 = (f32[128,128]{1,0:T(8,128)S(1)}, f32[128,128]{1,0:T(8,128)S(1)}, u32[]{:S(2)}, u32[]{:S(2)}) collective-permute-start(f32[128,128]{1,0:T(8,128)S(1)} %slice_add_fusion.5), channel_id=1, source_target_pairs={{2,0},{4,2},{6,4},{8,6},{10,8},{12,10},{14,12},{16,14},{18,16},{20... | collective-permute-start | bytes 196616 | tf_op jit(solution)/shard_map/ppermute | solution.py:24
  590.2 9.5 %collective-permute-start.28 = (f32[128,128]{1,0:T(8,128)S(1)}, f32[128,128]{1,0:T(8,128)S(1)}, u32[]{:S(2)}, u32[]{:S(2)}) collective-permute-start(f32[128,128]{1,0:T(8,128)S(1)} %slice_add_fusion.12), channel_id=1, source_target_pairs={{2,0},{4,2},{6,4},{8,6},{10,8},{12,10},{14,12},{16,14},{18,16},{20... | collective-permute-start | bytes 196616 | tf_op jit(solution)/shard_map/ppermute | solution.py:24
  595.5 9.5 %collective-permute-start.36 = (f32[128,128]{1,0:T(8,128)S(1)}, f32[128,128]{1,0:T(8,128)S(1)}, u32[]{:S(2)}, u32[]{:S(2)}) collective-permute-start(f32[128,128]{1,0:T(8,128)S(1)} %slice_add_fusion.4), channel_id=1, source_target_pairs={{2,0},{4,2},{6,4},{8,6},{10,8},{12,10},{14,12},{16,14},{18,16},{20... | collective-permute-start | bytes 196616 | tf_op jit(solution)/shard_map/ppermute | solution.py:24
  599.7 9.5 %collective-permute-start.29 = (f32[128,128]{1,0:T(8,128)S(1)}, f32[128,128]{1,0:T(8,128)S(1)}, u32[]{:S(2)}, u32[]{:S(2)}) collective-permute-start(f32[128,128]{1,0:T(8,128)S(1)} %slice_add_fusion.11), channel_id=1, source_target_pairs={{2,0},{4,2},{6,4},{8,6},{10,8},{12,10},{14,12},{16,14},{18,16},{20... | collective-permute-start | bytes 196616 | tf_op jit(solution)/shard_map/ppermute | solution.py:24
  605.0 9.5 %collective-permute-start.37 = (f32[128,128]{1,0:T(8,128)S(1)}, f32[128,128]{1,0:T(8,128)S(1)}, u32[]{:S(2)}, u32[]{:S(2)}) collective-permute-start(f32[128,128]{1,0:T(8,128)S(1)} %slice_add_fusion.3), channel_id=1, source_target_pairs={{2,0},{4,2},{6,4},{8,6},{10,8},{12,10},{14,12},{16,14},{18,16},{20... | collective-permute-start | bytes 196616 | tf_op jit(solution)/shard_map/ppermute | solution.py:24
  609.2 9.5 %collective-permute-start.30 = (f32[128,128]{1,0:T(8,128)S(1)}, f32[128,128]{1,0:T(8,128)S(1)}, u32[]{:S(2)}, u32[]{:S(2)}) collective-permute-start(f32[128,128]{1,0:T(8,128)S(1)} %slice_add_fusion.10), channel_id=1, source_target_pairs={{2,0},{4,2},{6,4},{8,6},{10,8},{12,10},{14,12},{16,14},{18,16},{20... | collective-permute-start | bytes 196616 | tf_op jit(solution)/shard_map/ppermute | solution.py:24
  614.5 9.5 %collective-permute-start.38 = (f32[128,128]{1,0:T(8,128)S(1)}, f32[128,128]{1,0:T(8,128)S(1)}, u32[]{:S(2)}, u32[]{:S(2)}) collective-permute-start(f32[128,128]{1,0:T(8,128)S(1)} %slice_add_fusion.2), channel_id=1, source_target_pairs={{2,0},{4,2},{6,4},{8,6},{10,8},{12,10},{14,12},{16,14},{18,16},{20... | collective-permute-start | bytes 196616 | tf_op jit(solution)/shard_map/ppermute | solution.py:24
  618.7 9.5 %collective-permute-start.31 = (f32[128,128]{1,0:T(8,128)S(1)}, f32[128,128]{1,0:T(8,128)S(1)}, u32[]{:S(2)}, u32[]{:S(2)}) collective-permute-start(f32[128,128]{1,0:T(8,128)S(1)} %slice_add_fusion.9), channel_id=1, source_target_pairs={{2,0},{4,2},{6,4},{8,6},{10,8},{12,10},{14,12},{16,14},{18,16},{20... | collective-permute-start | bytes 196616 | tf_op jit(solution)/shard_map/ppermute | solution.py:24
  624.0 9.5 %collective-permute-start.39 = (f32[128,128]{1,0:T(8,128)S(1)}, f32[128,128]{1,0:T(8,128)S(1)}, u32[]{:S(2)}, u32[]{:S(2)}) collective-permute-start(f32[128,128]{1,0:T(8,128)S(1)} %slice_add_fusion.1), channel_id=1, source_target_pairs={{2,0},{4,2},{6,4},{8,6},{10,8},{12,10},{14,12},{16,14},{18,16},{20... | collective-permute-start | bytes 196616 | tf_op jit(solution)/shard_map/ppermute | solution.py:24
Sparse Core Ops, SparseCore 0:
  10.2 120.2 all-gather.8
  140.5 123.3 reduce-scatter.1
where the time goes:
time: 642 us; the launch traced here: 641 us
  blocking collectives  254 us (40%)
  waiting for transfers between devices  175 us (27%)
  starting transfers between devices  167 us (26%)
  between operations  15 us (2%)
  matrix products  14.9 us (2%)
  other arithmetic  10.4 us (2%)
    all_gather x3, blocking collectives, joined(): everything = jax.tree.map(lambda part: lax.all_gather(part, axis), shard)  224 us
    ppermute x40, starting transfers between devices, passed_along(): return lax.ppermute(block, axis, route)  166 us
    all_gather x1, waiting for transfers between devices, body(): gathered = lax.all_gather(teacher_hidden, 'ctx', axis=0, tiled=True)  123 us
    ppermute x40, waiting for transfers between devices, passed_along(): return lax.ppermute(block, axis, route)  52 us
    all_gather x1, blocking collectives, body(): lax.all_gather(advantage, ('section', 'tp'), axis=0, tiled=True)  29.8 us
  transfers between devices with their start and end apart: 42, of which 25 were waited for; matrix products, arithmetic and copies ran while one was open for 1% of the time, Pallas kernels for 0%

commit v1 on v0

v1 whole, which is shorter than its diff:
```python
import jax
import jax.numpy as jnp
from jax import lax
from jax.sharding import PartitionSpec as P

advantage_scale = 0.1
clip_bound = 8.0
masked_value = -1e30

Z, Y, CORES = 8, 4, 2
SECTIONS, TPS = 4, 2
PIECE = 16
FARTHEST = 8


def ctx_move(block, target):
    route = []
    for z in range(Z):
        for y in range(Y):
            for core in range(CORES):
                z2, y2, core2 = target(z, y, core)
                route.append(
                    (z * 8 + y * 2 + core, (z2 % Z) * 8 + (y2 % Y) * 2 + core2 % CORES)
                )
    return lax.ppermute(block, "ctx", route)


def over_y(block, bits):
    return ctx_move(block, lambda z, y, core: (z, y ^ bits, core))


def along_all_z(block):
    groups = [[z * 8 + rest for z in range(Z)] for rest in range(Y * CORES)]
    return lax.all_gather(block, "ctx", axis_index_groups=groups)


def other_core(block):
    return ctx_move(block, lambda z, y, core: (z, y, core + 1))


def passed_along(block, distance):
    count = Z * Y * CORES
    route = [(i - distance, i) for i in range(count) if 0 <= i - distance < count]
    return lax.ppermute(block, "ctx", route)


def along_section(block, step):
    return lax.ppermute(block, "section", [(s, (s + step) % SECTIONS) for s in range(SECTIONS)])


def to_other_tp(block):
    return lax.ppermute(block, "tp", [(0, 1), (1, 0)])


def section_parts(gathered, heads, section):
    rows = gathered.shape[1]
    parts = []
    for head in heads:
        part = jnp.dot(
            gathered.reshape(Z * rows, -1), head, preferred_element_type=jnp.float32
        )
        parts.append(part.reshape(SECTIONS, 2, rows // PIECE, PIECE, head.shape[1]))

    def rows_for(step):
        place = lax.rem(section + step, SECTIONS)
        return jnp.stack(
            [lax.dynamic_index_in_dim(part, place, 0, keepdims=False) for part in parts]
        )

    return [rows_for(0)] + [rows_for(step).astype(jnp.bfloat16) for step in (1, 2, 3)]


def section_sums(parts):
    total = parts[0]
    for step in (1, 2, 3):
        total = total + along_section(parts[step], step).astype(jnp.float32)
    return total


def tp_halves(total, tp):
    halves = total.reshape(total.shape[:3] + (TPS, PIECE // TPS) + total.shape[4:])
    keep = lax.dynamic_index_in_dim(halves, tp, 3, keepdims=False)
    give = lax.dynamic_index_in_dim(halves, 1 - tp, 3, keepdims=False)
    return keep, give.astype(jnp.bfloat16)


def tp_sums(keep, give):
    return keep + to_other_tp(give).astype(jnp.float32)


def row_stats(logits, columns, ids):
    picked = jnp.sum(jnp.where(columns == ids[None, ..., None], logits, 0.0), axis=(0, 4))
    row_top = jnp.max(logits, axis=(0, 4))
    row_total = jnp.sum(jnp.exp(logits - row_top[None, ..., None]), axis=(0, 4))
    return jnp.stack([row_top, row_total, picked])


def y_exchanged(array, axis, y):
    shape = array.shape
    pairs = array.reshape(shape[:axis] + (2, 2) + shape[axis + 1 :])
    pairs = jnp.where(y % 2 == 1, jnp.flip(pairs, axis + 1), pairs)
    pairs = jnp.where(y // 2 == 1, jnp.flip(pairs, axis), pairs)
    return pairs.reshape(shape)


def key_value_window(keys, values, segment_ids):
    id_row = jnp.concatenate([segment_ids, jnp.zeros_like(segment_ids)])[None, :]
    own = jnp.concatenate(
        [
            jnp.concatenate([keys, values], axis=1),
            jnp.broadcast_to(id_row.astype(jnp.bfloat16), (16, 2 * keys.shape[1])),
        ],
        axis=0,
    )[None]
    two = jnp.concatenate([passed_along(own, 1), own], axis=0)
    four = jnp.concatenate([passed_along(two, 2), two], axis=0)
    return jnp.concatenate([passed_along(own, 8), passed_along(four, 4), four], axis=0)


def body(
    teacher_hidden,
    lm_head,
    sampled_ids,
    student_logprob,
    owner_map,
    queries,
    keys,
    values,
    grad_out,
    segment_ids,
):
    ctx_index = lax.axis_index("ctx")
    section = lax.axis_index("section")
    tp = lax.axis_index("tp")
    y, core = lax.rem(ctx_index // 2, 4), lax.rem(ctx_index, 2)

    near = jnp.concatenate([teacher_hidden, over_y(teacher_hidden, 1)], axis=0)
    far = over_y(near, 2)
    far, segment_ids = lax.optimization_barrier((far, segment_ids))
    window = key_value_window(keys, values, segment_ids)
    near_all, far, other_head, window = lax.optimization_barrier(
        (along_all_z(near), far, other_core(lm_head), window)
    )
    far_all = along_all_z(far)
    heads = (lm_head, other_head)
    keep, give = tp_halves(section_sums(section_parts(near_all, heads, section)), tp)
    give, far_all, window = lax.optimization_barrier((give, far_all, window))
    near_logits = tp_sums(keep, give)
    far_parts = section_parts(far_all, heads, section)
    far_logits = tp_sums(*tp_halves(section_sums(far_parts), tp))

    def kept(array, axis):
        return lax.dynamic_index_in_dim(
            lax.dynamic_index_in_dim(array, section, 0, keepdims=False), tp, axis, keepdims=False
        )

    token_ids = kept(sampled_ids.reshape(SECTIONS, 2, Y, CORES, TPS, PIECE // TPS), 3)
    token_ids = lax.dynamic_index_in_dim(token_ids, core, 2, keepdims=False)
    relative_ids = y_exchanged(token_ids, 1, y)
    vocab = lm_head.shape[1]
    starts = jnp.stack([ctx_index, ctx_index + 1 - 2 * core]) * vocab
    columns = starts[:, None, None, None, None] + jnp.arange(vocab, dtype=jnp.int32)
    stats = jnp.concatenate(
        [
            row_stats(near_logits, columns, relative_ids[:, :2]),
            row_stats(far_logits, columns, relative_ids[:, 2:]),
        ],
        axis=2,
    )
    stats = y_exchanged(stats, 2, y).reshape(3, -1)
    everywhere = lax.all_to_all(
        jnp.broadcast_to(stats, (Z * Y * CORES,) + stats.shape), "ctx", 0, 0
    ).reshape(Z * Y, CORES, 3, -1)
    highest = jnp.max(everywhere[:, :, 0], axis=0)
    summed = jnp.sum(everywhere[:, :, 1] * jnp.exp(everywhere[:, :, 0] - highest), axis=0)
    teacher_logprob = jnp.sum(everywhere[:, :, 2], axis=0) - highest - jnp.log(summed)
    student_rows = kept(student_logprob.reshape(SECTIONS, 2, Y, CORES, TPS, PIECE // TPS), 3)
    student_rows = student_rows.transpose(2, 0, 1, 3).reshape(CORES, -1)
    advantage = jnp.clip(teacher_logprob - student_rows, -clip_bound, clip_bound).reshape(-1)
    count = SECTIONS * TPS
    everything = lax.all_to_all(
        jnp.broadcast_to(advantage, (count,) + advantage.shape), ("section", "tp"), 0, 0
    )
    owners = owner_map.reshape(SECTIONS, 2, Y, CORES, TPS, PIECE // TPS)
    owners = owners.transpose(0, 4, 3, 1, 2, 5).reshape(-1)
    advantage_own = everything.reshape(SECTIONS, TPS, CORES, 2, Y, PIECE // TPS)
    advantage_own = kept(advantage_own, 2).transpose(2, 1, 0, 3).reshape(-1)
    everything = everything.reshape(-1)

    seq_rows = queries.shape[0]
    head_dim = keys.shape[1]
    group = queries.shape[1] // head_dim
    scaling = head_dim ** (-0.5)
    query_position = ctx_index * seq_rows + jnp.arange(seq_rows, dtype=jnp.int32)
    routed = jnp.sum(
        jnp.where(owners[None, :] == query_position[:, None], everything[None, :], 0.0), axis=1
    )
    weight = 1.0 + advantage_scale * routed

    key_window = window[:, :seq_rows, :head_dim].reshape(-1, head_dim)
    value_window = window[:, :seq_rows, head_dim:].reshape(-1, head_dim)
    key_segment = window[:, seq_rows, :seq_rows].reshape(-1)
    key_position = (ctx_index - FARTHEST) * seq_rows + jnp.arange(
        (FARTHEST + 1) * seq_rows, dtype=jnp.int32
    )
    allowed = (
        (key_segment[None, :] == segment_ids.astype(jnp.bfloat16)[:, None])
        & (key_position[None, :] <= query_position[:, None])
        & (key_position[None, :] >= 0)
    )
    allowed = jnp.tile(allowed, (group, 1))

    def by_head(array):
        return (
            array.reshape(seq_rows, group, head_dim)
            .transpose(1, 0, 2)
            .reshape(group * seq_rows, head_dim)
        )

    query_rows, grad_rows = by_head(queries), by_head(grad_out)
    scores = jnp.dot(query_rows, key_window.T, preferred_element_type=jnp.float32) * scaling
    masked = jnp.where(allowed, scores, masked_value)
    top = jnp.max(masked, axis=1, keepdims=True)
    raised = jnp.where(allowed, jnp.exp(masked - top), 0.0)
    softmax = (raised / jnp.sum(raised, axis=1, keepdims=True)).astype(jnp.bfloat16)
    context = jnp.dot(softmax, value_window, preferred_element_type=jnp.float32)
    row_delta = jnp.sum(grad_rows.astype(jnp.float32) * context, axis=1, keepdims=True)
    grad_prob = jnp.dot(grad_rows, value_window.T, preferred_element_type=jnp.float32)
    grad_score = (softmax.astype(jnp.float32) * (grad_prob - row_delta) * scaling).astype(
        jnp.bfloat16
    )
    grad_query = jnp.dot(grad_score, key_window, preferred_element_type=jnp.float32)

    row_weight = jnp.tile(weight, (group,))[:, None]
    grad_query = (row_weight * grad_query).astype(jnp.bfloat16)
    weighted_query = (row_weight * query_rows.astype(jnp.float32)).astype(jnp.bfloat16)
    weighted_grad = (row_weight * grad_rows.astype(jnp.float32)).astype(jnp.bfloat16)
    grad_key = jnp.dot(grad_score.T, weighted_query, preferred_element_type=jnp.float32)
    grad_value = jnp.dot(softmax.T, weighted_grad, preferred_element_type=jnp.float32)
    both = jnp.concatenate([grad_key, grad_value], axis=1).reshape(
        FARTHEST + 1, seq_rows, 2 * head_dim
    )
    total = both[FARTHEST]
    for distance in range(1, FARTHEST + 1):
        given = both[FARTHEST - distance].astype(jnp.bfloat16)
        total = total + passed_along(given, -distance).astype(jnp.float32)
    total = total.astype(jnp.bfloat16)
    d_queries = (
        grad_query.reshape(group, seq_rows, head_dim)
        .transpose(1, 0, 2)
        .reshape(seq_rows, group * head_dim)
    )
    return (advantage_own, d_queries, total[:, :head_dim], total[:, head_dim:])


def solution(mesh):
    in_specs = (
        P("ctx", ("section", "tp")),
        P(("section", "tp"), "ctx"),
        P(),
        P(),
        P(),
        P("ctx", ("section", "tp")),
        P("ctx", ("section", "tp")),
        P("ctx", ("section", "tp")),
        P("ctx", ("section", "tp")),
        P("ctx"),
    )
    out_specs = (
        P(("section", "tp")),
        P("ctx", ("section", "tp")),
        P("ctx", ("section", "tp")),
        P("ctx", ("section", "tp")),
    )
    return jax.shard_map(body, mesh=mesh, in_specs=in_specs, out_specs=out_specs, check_vma=False)
```

time: 642 us -> 228 us (0.36)
  blocking collectives: 254 us -> 0 us
  waiting for transfers between devices: 175 us -> 67.7 us
  starting transfers between devices: 167 us -> 95.1 us
  local copies, waits for them, and re-layouts: 3.76 us -> 17.1 us
    all_gather x4 -> x0, blocking collectives: 254 us -> none  [the longest x3 224 us: joined(): everything = jax.tree.map(lambda part: lax.all_gather(part, axis), shard)]
    all_gather x1 -> x2, waiting for transfers between devices: 123 us -> 13.5 us  [along_all_z(): return lax.all_gather(block, 'ctx', axis_index_groups=groups)]
    ppermute x40 -> x23, starting transfers between devices: 166 us -> 74.4 us  [the longest x12 39.8 us: passed_along(): return lax.ppermute(block, 'ctx', route)]
    all_to_all x0 -> x2, starting transfers between devices: none -> 20.6 us  [the longest x1 17 us: body(): lax.all_to_all(jnp.broadcast_to(stats, (Z * Y * CORES,) + stats.shape), '...]
    all_to_all x0 -> x2, waiting for transfers between devices: none -> 8.9 us  [the longest x1 5.61 us: body(): lax.all_to_all(jnp.broadcast_to(advantage, (count,) + advantage.shape), (...]
    ppermute x40 -> x23, waiting for transfers between devices: 52 us -> 45.2 us  [the longest x12 21.2 us: passed_along(): return lax.ppermute(block, 'ctx', route)]
    dot_general x7 -> x10, matrix products: 14.9 us -> 18.5 us  [the longest x4 10.3 us: section_parts(): jnp.dot(gathered.reshape(Z * rows, -1), head, preferred_element_type=jnp....]
  transfers between devices with their start and end apart: 42 -> 27, of which waited for: 25 -> 15; matrix products, arithmetic and copies ran while one was open for 1% -> 15% of each run, Pallas kernels for 0% -> 0%
where the time goes in v1:
time: 228 us; the launch traced here: 227 us
  starting transfers between devices  95.1 us (42%)
  waiting for transfers between devices  67.7 us (30%)
  matrix products  18.5 us (8%)
  local copies, waits for them, and re-layouts  17.1 us (8%)
  between operations  15.1 us (7%)
  other arithmetic  13.5 us (6%)
    ppermute x12, starting transfers between devices, passed_along(): return lax.ppermute(block, 'ctx', route)  39.8 us
    ppermute x12, waiting for transfers between devices, passed_along(): return lax.ppermute(block, 'ctx', route)  21.2 us
    ppermute x6, starting transfers between devices, along_section(): lax.ppermute(block, 'section', [(s, (s + step) % SECTIONS) for s in range...  18.8 us
    all_to_all x1, starting transfers between devices, body(): lax.all_to_all(jnp.broadcast_to(stats, (Z * Y * CORES,) + stats.shape), '...  17 us
    all_gather x2, waiting for transfers between devices, along_all_z(): return lax.all_gather(block, 'ctx', axis_index_groups=groups)  13.5 us
    ppermute x3, waiting for transfers between devices, ctx_move(): return lax.ppermute(block, 'ctx', route)  10.9 us
    dot_general x4, matrix products, section_parts(): jnp.dot(gathered.reshape(Z * rows, -1), head, preferred_element_type=jnp....  10.3 us
    ppermute x2, starting transfers between devices, to_other_tp(): return lax.ppermute(block, 'tp', [(0, 1), (1, 0)])  9.2 us
  transfers between devices with their start and end apart: 27, of which 15 were waited for; matrix products, arithmetic and copies ran while one was open for 15% of the time, Pallas kernels for 0%

profile of v1, /device:TPU:217, one launch (start us, length us, event | category | flops | bytes accessed | tf_op | source)
XLA Modules:
  0.0 227.0 jit_solution(12507558644679657938)
XLA Ops:
  7.2 2.6 %collective-permute-start.2 = (bf16[2048,1024]{1,0:T(8,128)(2,1)}, bf16[2048,1024]{1,0:T(8,128)(2,1)}, u32[]{:S(2)}, u32[]{:S(2)}) collective-permute-start(bf16[2048,1024]{1,0:T(8,128)(2,1)} %param.11), channel_id=1, source_target_pairs={{0,2},{2,0},{4,6},{6,4},{8,10},{10,8},{12,14},{14,12},{16,18},{18,... | collective-permute-start | bytes 12582920 | tf_op jit(solution)/shard_map/ppermute | solution.py:25
  9.8 2.1 collective-permute-start
  11.9 0.8 reshape.271
  12.9 0.8 constant_dynamic-update-slice_fusion.1
  13.8 1.8 collective-permute-done
  16.4 2.0 collective-permute-start.1
  18.4 9.1 %collective-permute-done.1 = bf16[32,2048]{1,0:T(8,128)(2,1)S(1)} collective-permute-done((bf16[32,2048]{1,0:T(8,128)(2,1)}, bf16[32,2048]{1,0:T(8,128)(2,1)S(1)}, u32[]{:S(2)}, u32[]{:S(2)}) %collective-permute-start.1) | collective-permute-done | bytes 131104 | tf_op jit(solution)/shard_map/ppermute | solution.py:25
  28.2 0.8 maximum_bitcast_fusion
  28.9 5.4 %collective-permute-start.4 = (bf16[1,144,256]{2,1,0:T(8,128)(2,1)S(1)}, bf16[1,144,256]{2,1,0:T(8,128)(2,1)S(1)}, u32[]{:S(2)}, u32[]{:S(2)}) collective-permute-start(bf16[1,144,256]{2,1,0:T(8,128)(2,1)S(1)} %maximum_bitcast_fusion), channel_id=1, source_target_pairs={{0,2},{2,4},{4,6},{6,8},{8,10},{10,12},{12,14},{14,16},{16,18},{18... | collective-permute-start | bytes 221192 | tf_op jit(solution)/shard_map/ppermute | solution.py:44
  34.3 1.4 collective-permute-done.4
  35.7 2.4 %collective-permute-start.5 = (bf16[2,144,256]{2,1,0:T(8,128)(2,1)S(1)}, bf16[2,144,256]{2,1,0:T(8,128)(2,1)S(1)}, u32[]{:S(2)}, u32[]{:S(2)}) collective-permute-start(bf16[2,144,256]{2,1,0:T(8,128)(2,1)S(1)} %pad_maximum_fusion.8), channel_id=1, source_target_pairs={{0,4},{2,6},{4,8},{6,10},{8,12},{10,14},{12,16},{14,18},{16,20},{1... | collective-permute-start | bytes 442376 | tf_op jit(solution)/shard_map/ppermute | solution.py:44
  38.7 0.8 reshape.277
  39.6 3.8 %collective-permute-done.5 = bf16[2,144,256]{2,1,0:T(8,128)(2,1)S(1)} collective-permute-done((bf16[2,144,256]{2,1,0:T(8,128)(2,1)S(1)}, bf16[2,144,256]{2,1,0:T(8,128)(2,1)S(1)}, u32[]{:S(2)}, u32[]{:S(2)}) %collective-permute-start.5) | collective-permute-done | bytes 147488 | tf_op jit(solution)/shard_map/ppermute | solution.py:44
  43.5 1.9 collective-permute-start.6
  46.0 2.9 %collective-permute-start.3 = (bf16[1,144,256]{2,1,0:T(8,128)(2,1)S(1)}, bf16[1,144,256]{2,1,0:T(8,128)(2,1)S(1)}, u32[]{:S(2)}, u32[]{:S(2)}) collective-permute-start(bf16[1,144,256]{2,1,0:T(8,128)(2,1)S(1)} %maximum_bitcast_fusion), channel_id=1, source_target_pairs={{0,16},{2,18},{4,20},{6,22},{8,24},{10,26},{12,28},{14,30},{16,32}... | collective-permute-start | bytes 221192 | tf_op jit(solution)/shard_map/ppermute | solution.py:44
  49.5 2.7 %collective-permute-done.3 = bf16[1,144,256]{2,1,0:T(8,128)(2,1)S(1)} collective-permute-done((bf16[1,144,256]{2,1,0:T(8,128)(2,1)S(1)}, bf16[1,144,256]{2,1,0:T(8,128)(2,1)S(1)}, u32[]{:S(2)}, u32[]{:S(2)}) %collective-permute-start.3) | collective-permute-done | bytes 73760 | tf_op jit(solution)/shard_map/ppermute | solution.py:44
  52.3 8.2 %collective-permute-done.6 = bf16[4,144,256]{2,1,0:T(8,128)(2,1)S(1)} collective-permute-done((bf16[4,144,256]{2,1,0:T(8,128)(2,1)S(1)}, bf16[4,144,256]{2,1,0:T(8,128)(2,1)S(1)}, u32[]{:S(2)}, u32[]{:S(2)}) %collective-permute-start.6) | collective-permute-done | bytes 294944 | tf_op jit(solution)/shard_map/ppermute | solution.py:44
  60.6 0.8 constant_dynamic-update-slice_fusion.2
  61.5 3.9 %fusion.5 = f32[4,2,2,16,1024]{4,3,2,1,0:T(8,128)S(1)} fusion(bf16[4,2,2,16,2048]{4,3,2,1,0:T(8,128)(2,1)} %bitcast.206, bf16[2048,1024]{1,0:T(8,128)(2,1)} %collective-permute-done.2), kind=kOutput, calls=%fused_computation.11 | convolution fusion | flops 1073741824 | bytes 6291456 | tf_op jit(solution)/shard_map/dot_general | solution.py:59
  65.5 1.3 fusion.9
  66.9 4.4 %collective-permute-start.9 = (bf16[2,2,2,16,1024]{4,3,2,1,0:T(8,128)(2,1)S(1)}, bf16[2,2,2,16,1024]{4,3,2,1,0:T(8,128)(2,1)S(1)}, u32[]{:S(2)}, u32[]{:S(2)}) collective-permute-start(bf16[2,2,2,16,1024]{4,3,2,1,0:T(8,128)(2,1)S(1)} %pad_maximum_fusion.4), channel_id=1, source_target_pairs={{0,384},{128,0},{256,128},{384,256},{1,385},{129,1},{257,129},{385... | collective-permute-start | bytes 786440 | tf_op jit(solution)/shard_map/ppermute | solution.py:48
  72.0 2.4 %collective-permute-start.8 = (bf16[2,2,2,16,1024]{4,3,2,1,0:T(8,128)(2,1)}, bf16[2,2,2,16,1024]{4,3,2,1,0:T(8,128)(2,1)S(1)}, u32[]{:S(2)}, u32[]{:S(2)}) collective-permute-start(bf16[2,2,2,16,1024]{4,3,2,1,0:T(8,128)(2,1)} %pad_maximum_fusion.3), channel_id=1, source_target_pairs={{0,256},{128,384},{256,0},{384,128},{1,257},{129,385},{257,1},{385... | collective-permute-start | bytes 786440 | tf_op jit(solution)/shard_map/ppermute | solution.py:48
  74.4 0.7 pad_maximum_fusion.2
  75.2 2.5 %collective-permute-start.7 = (bf16[2,2,2,16,1024]{4,3,2,1,0:T(8,128)(2,1)}, bf16[2,2,2,16,1024]{4,3,2,1,0:T(8,128)(2,1)}, u32[]{:S(2)}, u32[]{:S(2)}) collective-permute-start(bf16[2,2,2,16,1024]{4,3,2,1,0:T(8,128)(2,1)} %pad_maximum_fusion.2), channel_id=1, source_target_pairs={{0,128},{128,256},{256,384},{384,0},{1,129},{129,257},{257,385},{3... | collective-permute-start | bytes 786440 | tf_op jit(solution)/shard_map/ppermute | solution.py:48
  79.5 0.8 reshape.281
  81.1 1.0 constant_dynamic-slice_fusion.5
  83.5 6.1 %collective-permute-done.7 = bf16[2,2,2,16,1024]{4,3,2,1,0:T(8,128)(2,1)} collective-permute-done((bf16[2,2,2,16,1024]{4,3,2,1,0:T(8,128)(2,1)}, bf16[2,2,2,16,1024]{4,3,2,1,0:T(8,128)(2,1)}, u32[]{:S(2)}, u32[]{:S(2)}) %collective-permute-start.7) | collective-permute-done | bytes 262176 | tf_op jit(solution)/shard_map/ppermute | solution.py:48
  89.5 1.3 fusion.19
  90.8 13.5 %all-gather.7.cloned.1.call-done = bf16[256,2048]{1,0:T(8,128)(2,1)} async-done(((bf16[32,2048]{1,0:T(8,128)(2,1)}), bf16[256,2048]{1,0:T(8,128)(2,1)}) %all-gather.7.cloned.1.call-update) | async-done | bytes 1048592 | tf_op jit(solution)/shard_map/all_gather | solution.py:34
  104.4 3.9 %fusion.3 = f32[4,2,2,16,1024]{4,3,2,1,0:T(8,128)S(1)} fusion(bf16[4,2,2,16,2048]{4,3,2,1,0:T(8,128)(2,1)} %bitcast.208, bf16[2048,1024]{1,0:T(8,128)(2,1)} %collective-permute-done.2), kind=kOutput, calls=%fused_computation.9 | convolution fusion | flops 1073741824 | bytes 6291456 | tf_op jit(solution)/shard_map/dot_general | solution.py:59
  108.4 1.3 fusion.7
  109.7 0.8 fusion.53
  110.5 4.2 %collective-permute-start.10 = (bf16[2,2,2,8,1024]{4,3,2,1,0:T(8,128)(2,1)S(1)}, bf16[2,2,2,8,1024]{4,3,2,1,0:T(8,128)(2,1)S(1)}, u32[]{:S(2)}, u32[]{:S(2)}) collective-permute-start(bf16[2,2,2,8,1024]{4,3,2,1,0:T(8,128)(2,1)S(1)} %fusion.36), channel_id=1, source_target_pairs={{0,1},{1,0},{2,3},{3,2},{4,5},{5,4},{6,7},{7,6},{8,9},{9,8},{10,11... | collective-permute-start | bytes 393224 | tf_op jit(solution)/shard_map/ppermute | solution.py:52
  114.9 4.5 %collective-permute-start.13 = (bf16[2,2,2,16,1024]{4,3,2,1,0:T(8,128)(2,1)S(1)}, bf16[2,2,2,16,1024]{4,3,2,1,0:T(8,128)(2,1)S(1)}, u32[]{:S(2)}, u32[]{:S(2)}) collective-permute-start(bf16[2,2,2,16,1024]{4,3,2,1,0:T(8,128)(2,1)S(1)} %pad_maximum_fusion.7), channel_id=1, source_target_pairs={{0,384},{128,0},{256,128},{384,256},{1,385},{129,1},{257,129},{385... | collective-permute-start | bytes 786440 | tf_op jit(solution)/shard_map/ppermute | solution.py:48
  119.5 2.5 %collective-permute-start.12 = (bf16[2,2,2,16,1024]{4,3,2,1,0:T(8,128)(2,1)S(1)}, bf16[2,2,2,16,1024]{4,3,2,1,0:T(8,128)(2,1)S(1)}, u32[]{:S(2)}, u32[]{:S(2)}) collective-permute-start(bf16[2,2,2,16,1024]{4,3,2,1,0:T(8,128)(2,1)S(1)} %pad_maximum_fusion.6), channel_id=1, source_target_pairs={{0,256},{128,384},{256,0},{384,128},{1,257},{129,385},{257,1},{385... | collective-permute-start | bytes 786440 | tf_op jit(solution)/shard_map/ppermute | solution.py:48
  122.0 2.5 %collective-permute-start.11 = (bf16[2,2,2,16,1024]{4,3,2,1,0:T(8,128)(2,1)S(1)}, bf16[2,2,2,16,1024]{4,3,2,1,0:T(8,128)(2,1)S(1)}, u32[]{:S(2)}, u32[]{:S(2)}) collective-permute-start(bf16[2,2,2,16,1024]{4,3,2,1,0:T(8,128)(2,1)S(1)} %pad_maximum_fusion.5), channel_id=1, source_target_pairs={{0,128},{128,256},{256,384},{384,0},{1,129},{129,257},{257,385},{3... | collective-permute-start | bytes 786440 | tf_op jit(solution)/shard_map/ppermute | solution.py:48
  124.5 1.1 and_and_fusion
  126.2 1.1 fusion.2
  127.4 1.3 fusion.11
  128.8 2.1 collective-permute-done.11
  131.1 5.0 %collective-permute-start.14 = (bf16[2,2,2,8,1024]{4,3,2,1,0:T(8,128)(2,1)S(1)}, bf16[2,2,2,8,1024]{4,3,2,1,0:T(8,128)(2,1)S(1)}, u32[]{:S(2)}, u32[]{:S(2)}) collective-permute-start(bf16[2,2,2,8,1024]{4,3,2,1,0:T(8,128)(2,1)S(1)} %fusion.37), channel_id=1, source_target_pairs={{0,1},{1,0},{2,3},{3,2},{4,5},{5,4},{6,7},{7,6},{8,9},{9,8},{10,11... | collective-permute-start | bytes 393224 | tf_op jit(solution)/shard_map/ppermute | solution.py:52
  136.1 1.4 divide_convert_fusion
  137.7 4.4 %collective-permute-done.14 = bf16[2,2,2,8,1024]{4,3,2,1,0:T(8,128)(2,1)S(1)} collective-permute-done((bf16[2,2,2,8,1024]{4,3,2,1,0:T(8,128)(2,1)S(1)}, bf16[2,2,2,8,1024]{4,3,2,1,0:T(8,128)(2,1)S(1)}, u32[]{:S(2)}, u32[]{:S(2)}) %collective-permute-start.14) | collective-permute-done | bytes 131104 | tf_op jit(solution)/shard_map/ppermute | solution.py:52
  142.8 0.8 reshape.304
  143.5 17.0 %all-to-all-start = ((f32[64,1,192]{2,1,0:T(1,128)}), f32[64,1,192]{2,1,0:T(1,128)S(1)}, u32[]{:S(2)}, u32[]{:S(2)}) async-start(f32[64,1,192]{2,1,0:T(1,128)} %reshape.304), calls=%async_computation | async-start | bytes 131072 | tf_op jit(solution)/shard_map/all_to_all | solution.py:171
  160.5 1.5 fusion.14
  162.1 3.3 %all-to-all-done = f32[64,1,192]{2,1,0:T(1,128)S(1)} async-done(((f32[64,1,192]{2,1,0:T(1,128)}), f32[64,1,192]{2,1,0:T(1,128)S(1)}, u32[]{:S(2)}, u32[]{:S(2)}) %all-to-all-start) | async-done | bytes 49184 | tf_op jit(solution)/shard_map/all_to_all | solution.py:171
  165.9 0.8 reduce.8
  167.6 3.6 %all-to-all-start.1 = ((f32[8,1,128]{2,1,0:T(1,128)}), f32[8,1,128]{2,1,0:T(1,128)S(1)}, u32[]{:S(2)}, u32[]{:S(2)}) async-start(f32[8,1,128]{2,1,0:T(1,128)} %broadcast_in_dim.61), calls=%async_computation.1 | async-start | bytes 8192 | tf_op jit(solution)/shard_map/all_to_all | solution.py:181
  171.2 3.2 %fusion.1 = bf16[1024,1152]{0,1:T(8,128)(2,1)} fusion(bf16[1024,1152]{0,1:T(8,128)(2,1)S(1)} %divide_convert_fusion, bf16[1152,128]{1,0:T(8,128)(2,1)} %bitcast.187, f32[1024]{0:T(1024)S(1)} %fusion.14, bf16[16,8,8,128]{3,2,1,0:T(8,128)(2,1)S(1)} %bitcast.176), kind=kOutput, calls=%fused_computation.4 | convolution fusion | flops 307888128 | bytes 5279744 | tf_op jit(solution)/shard_map/dot_general | solution.py:228
  174.4 5.6 %all-to-all-done.1 = f32[8,1,128]{2,1,0:T(1,128)S(1)} async-done(((f32[8,1,128]{2,1,0:T(1,128)}), f32[8,1,128]{2,1,0:T(1,128)S(1)}, u32[]{:S(2)}, u32[]{:S(2)}) %all-to-all-start.1) | async-done | bytes 4128 | tf_op jit(solution)/shard_map/all_to_all | solution.py:181
  180.2 0.9 fusion.24
  181.7 0.9 fusion.23
  182.7 3.1 %collective-permute-start.22 = (bf16[128,256]{0,1:T(8,128)(2,1)S(1)}, bf16[128,256]{0,1:T(8,128)(2,1)S(1)}, u32[]{:S(2)}, u32[]{:S(2)}) collective-permute-start(bf16[128,256]{0,1:T(8,128)(2,1)S(1)} %get-tuple-element.71), channel_id=1, source_target_pairs={{16,0},{18,2},{20,4},{22,6},{24,8},{26,10},{28,12},{30,14},{32,16}... | collective-permute-start | bytes 196616 | tf_op jit(solution)/shard_map/ppermute | solution.py:44
  185.9 6.5 %collective-permute-start.21 = (bf16[128,256]{0,1:T(8,128)(2,1)S(1)}, bf16[128,256]{0,1:T(8,128)(2,1)S(1)}, u32[]{:S(2)}, u32[]{:S(2)}) collective-permute-start(bf16[128,256]{0,1:T(8,128)(2,1)S(1)} %get-tuple-element.72), channel_id=1, source_target_pairs={{14,0},{16,2},{18,4},{20,6},{22,8},{24,10},{26,12},{28,14},{30,16}... | collective-permute-start | bytes 196616 | tf_op jit(solution)/shard_map/ppermute | solution.py:44
  192.4 3.1 %collective-permute-start.20 = (bf16[128,256]{0,1:T(8,128)(2,1)S(1)}, bf16[128,256]{0,1:T(8,128)(2,1)S(1)}, u32[]{:S(2)}, u32[]{:S(2)}) collective-permute-start(bf16[128,256]{0,1:T(8,128)(2,1)S(1)} %get-tuple-element.73), channel_id=1, source_target_pairs={{12,0},{14,2},{16,4},{18,6},{20,8},{22,10},{24,12},{26,14},{28,16}... | collective-permute-start | bytes 196616 | tf_op jit(solution)/shard_map/ppermute | solution.py:44
  197.4 1.9 collective-permute-start.19
  199.3 4.2 %collective-permute-start.18 = (bf16[128,256]{0,1:T(8,128)(2,1)S(1)}, bf16[128,256]{0,1:T(8,128)(2,1)S(1)}, u32[]{:S(2)}, u32[]{:S(2)}) collective-permute-start(bf16[128,256]{0,1:T(8,128)(2,1)S(1)} %get-tuple-element.75), channel_id=1, source_target_pairs={{8,0},{10,2},{12,4},{14,6},{16,8},{18,10},{20,12},{22,14},{24,16},... | collective-permute-start | bytes 196616 | tf_op jit(solution)/shard_map/ppermute | solution.py:44
  203.5 2.2 collective-permute-start.17
  205.7 3.4 %collective-permute-start.16 = (bf16[128,256]{0,1:T(8,128)(2,1)S(1)}, bf16[128,256]{0,1:T(8,128)(2,1)S(1)}, u32[]{:S(2)}, u32[]{:S(2)}) collective-permute-start(bf16[128,256]{0,1:T(8,128)(2,1)S(1)} %get-tuple-element.77), channel_id=1, source_target_pairs={{4,0},{6,2},{8,4},{10,6},{12,8},{14,10},{16,12},{18,14},{20,16},{2... | collective-permute-start | bytes 196616 | tf_op jit(solution)/shard_map/ppermute | solution.py:44
  209.1 2.8 %collective-permute-start.15 = (bf16[128,256]{0,1:T(8,128)(2,1)S(1)}, bf16[128,256]{0,1:T(8,128)(2,1)S(1)}, u32[]{:S(2)}, u32[]{:S(2)}) collective-permute-start(bf16[128,256]{0,1:T(8,128)(2,1)S(1)} %get-tuple-element.70), channel_id=1, source_target_pairs={{2,0},{4,2},{6,4},{8,6},{10,8},{12,10},{14,12},{16,14},{18,16},{20... | collective-permute-start | bytes 196616 | tf_op jit(solution)/shard_map/ppermute | solution.py:44
  212.9 0.8 copy.135
  213.7 2.6 %collective-permute-done.16 = bf16[128,256]{0,1:T(8,128)(2,1)S(1)} collective-permute-done((bf16[128,256]{0,1:T(8,128)(2,1)S(1)}, bf16[128,256]{0,1:T(8,128)(2,1)S(1)}, u32[]{:S(2)}, u32[]{:S(2)}) %collective-permute-start.16) | collective-permute-done | bytes 65568 | tf_op jit(solution)/shard_map/ppermute | solution.py:44
  216.2 2.4 %collective-permute-done.15 = bf16[128,256]{0,1:T(8,128)(2,1)S(1)} collective-permute-done((bf16[128,256]{0,1:T(8,128)(2,1)S(1)}, bf16[128,256]{0,1:T(8,128)(2,1)S(1)}, u32[]{:S(2)}, u32[]{:S(2)}) %collective-permute-start.15) | collective-permute-done | bytes 65568 | tf_op jit(solution)/shard_map/ppermute | solution.py:44
  (145 shorter events, 17.1 us)
Async XLA Ops:
  7.2 54.2 %all-gather.5.cloned.1.call-start = ((), (), s32[]{:S(2)}) async-start(), calls=%async_computation.2 | async-start | bytes 1179648 | tf_op jit(solution)/shard_map/all_gather | solution.py:34
  7.2 54.2 %collective-permute-start.2 = (bf16[2048,1024]{1,0:T(8,128)(2,1)}, bf16[2048,1024]{1,0:T(8,128)(2,1)}, u32[]{:S(2)}, u32[]{:S(2)}) collective-permute-start(bf16[2048,1024]{1,0:T(8,128)(2,1)} %param.11), channel_id=1, source_target_pairs={{0,2},{2,0},{4,6},{6,4},{8,10},{10,8},{12,14},{14,12},{16,18},{18,... | collective-permute-start | bytes 12582920 | tf_op jit(solution)/shard_map/ppermute | solution.py:25
  9.8 5.8 %collective-permute-start = (bf16[16,2048]{1,0:T(8,128)(2,1)}, bf16[16,2048]{1,0:T(8,128)(2,1)S(1)}, u32[]{:S(2)}, u32[]{:S(2)}) collective-permute-start(bf16[16,2048]{1,0:T(8,128)(2,1)} %param.10), channel_id=1, source_target_pairs={{0,4},{2,6},{4,0},{6,2},{8,12},{10,14},{12,8},{14,10},{16,20},{18,... | collective-permute-start | bytes 196616 | tf_op jit(solution)/shard_map/ppermute | solution.py:25
  15.6 0.7 copy-start.2
  16.3 88.0 %all-gather.7.cloned.1.call-start = ((), (), s32[]{:S(2)}) async-start(), calls=%async_computation.3 | async-start | bytes 1179648 | tf_op jit(solution)/shard_map/all_gather | solution.py:34
  16.4 11.1 %collective-permute-start.1 = (bf16[32,2048]{1,0:T(8,128)(2,1)}, bf16[32,2048]{1,0:T(8,128)(2,1)S(1)}, u32[]{:S(2)}, u32[]{:S(2)}) collective-permute-start(bf16[32,2048]{1,0:T(8,128)(2,1)} %copy-done.2), channel_id=1, source_target_pairs={{0,8},{2,10},{4,12},{6,14},{8,0},{10,2},{12,4},{14,6},{16,24},{18,... | collective-permute-start | bytes 393224 | tf_op jit(solution)/shard_map/ppermute | solution.py:25
  27.5 33.9 %copy-start.9 = (bf16[32,2048]{1,0:T(8,128)(2,1)}, bf16[32,2048]{1,0:T(8,128)(2,1)S(1)}, u32[]{:S(2)}) copy-start(bf16[32,2048]{1,0:T(8,128)(2,1)S(1)} %collective-permute-done.1) | copy-start | bytes 393220
  28.1 7.6 %copy-start.17 = (bf16[128]{0:T(256)(128)(2,1)}, bf16[128]{0:T(256)(128)(2,1)S(1)}, u32[]{:S(2)}) copy-start(bf16[128]{0:T(256)(128)(2,1)S(1)} %convert.50) | copy-start | bytes 772
  28.9 6.8 %collective-permute-start.4 = (bf16[1,144,256]{2,1,0:T(8,128)(2,1)S(1)}, bf16[1,144,256]{2,1,0:T(8,128)(2,1)S(1)}, u32[]{:S(2)}, u32[]{:S(2)}) collective-permute-start(bf16[1,144,256]{2,1,0:T(8,128)(2,1)S(1)} %maximum_bitcast_fusion), channel_id=1, source_target_pairs={{0,2},{2,4},{4,6},{6,8},{8,10},{10,12},{12,14},{14,16},{16,18},{18... | collective-permute-start | bytes 221192 | tf_op jit(solution)/shard_map/ppermute | solution.py:44
  35.7 7.7 %collective-permute-start.5 = (bf16[2,144,256]{2,1,0:T(8,128)(2,1)S(1)}, bf16[2,144,256]{2,1,0:T(8,128)(2,1)S(1)}, u32[]{:S(2)}, u32[]{:S(2)}) collective-permute-start(bf16[2,144,256]{2,1,0:T(8,128)(2,1)S(1)} %pad_maximum_fusion.8), channel_id=1, source_target_pairs={{0,4},{2,6},{4,8},{6,10},{8,12},{10,14},{12,16},{14,18},{16,20},{1... | collective-permute-start | bytes 442376 | tf_op jit(solution)/shard_map/ppermute | solution.py:44
  43.5 17.0 %collective-permute-start.6 = (bf16[4,144,256]{2,1,0:T(8,128)(2,1)S(1)}, bf16[4,144,256]{2,1,0:T(8,128)(2,1)S(1)}, u32[]{:S(2)}, u32[]{:S(2)}) collective-permute-start(bf16[4,144,256]{2,1,0:T(8,128)(2,1)S(1)} %pad_maximum_fusion.1), channel_id=1, source_target_pairs={{0,8},{2,10},{4,12},{6,14},{8,16},{10,18},{12,20},{14,22},{16,24},... | collective-permute-start | bytes 884744 | tf_op jit(solution)/shard_map/ppermute | solution.py:44
  46.0 6.2 %collective-permute-start.3 = (bf16[1,144,256]{2,1,0:T(8,128)(2,1)S(1)}, bf16[1,144,256]{2,1,0:T(8,128)(2,1)S(1)}, u32[]{:S(2)}, u32[]{:S(2)}) collective-permute-start(bf16[1,144,256]{2,1,0:T(8,128)(2,1)S(1)} %maximum_bitcast_fusion), channel_id=1, source_target_pairs={{0,16},{2,18},{4,20},{6,22},{8,24},{10,26},{12,28},{14,30},{16,32}... | collective-permute-start | bytes 221192 | tf_op jit(solution)/shard_map/ppermute | solution.py:44
  61.4 4.0 %copy-start.20 = (bf16[2048,1024]{1,0:T(8,128)(2,1)S(1)}, bf16[2048,1024]{1,0:T(8,128)(2,1)}, u32[]{:S(2)}) copy-start(bf16[2048,1024]{1,0:T(8,128)(2,1)} %param.11) | copy-start | bytes 12582916
  61.4 4.0 %copy-start.22 = (bf16[256,2048]{1,0:T(8,128)(2,1)S(1)}, bf16[256,2048]{1,0:T(8,128)(2,1)}, u32[]{:S(2)}) copy-start(bf16[256,2048]{1,0:T(8,128)(2,1)} %all-gather.5.cloned.1.call-done) | copy-start | bytes 3145732
  65.5 13.4 %copy-start.7 = (bf16[128,1024]{1,0:T(8,128)(2,1)S(1)}, bf16[128,1024]{1,0:T(8,128)(2,1)}, u32[]{:S(2)}) copy-start(bf16[128,1024]{1,0:T(8,128)(2,1)} %param.15) | copy-start | bytes 786436
  65.5 13.7 %copy-start.8 = (bf16[128,1024]{1,0:T(8,128)(2,1)S(1)}, bf16[128,1024]{1,0:T(8,128)(2,1)}, u32[]{:S(2)}) copy-start(bf16[128,1024]{1,0:T(8,128)(2,1)} %param.18) | copy-start | bytes 786436
  66.8 8.4 %copy-start.1 = (f32[4,2,2,16,1024]{4,3,2,1,0:T(8,128)}, f32[4,2,2,16,1024]{4,3,2,1,0:T(8,128)S(1)}, u32[]{:S(2)}) copy-start(f32[4,2,2,16,1024]{4,3,2,1,0:T(8,128)S(1)} %fusion.9) | copy-start | bytes 3145732
  66.9 15.2 %collective-permute-start.9 = (bf16[2,2,2,16,1024]{4,3,2,1,0:T(8,128)(2,1)S(1)}, bf16[2,2,2,16,1024]{4,3,2,1,0:T(8,128)(2,1)S(1)}, u32[]{:S(2)}, u32[]{:S(2)}) collective-permute-start(bf16[2,2,2,16,1024]{4,3,2,1,0:T(8,128)(2,1)S(1)} %pad_maximum_fusion.4), channel_id=1, source_target_pairs={{0,384},{128,0},{256,128},{384,256},{1,385},{129,1},{257,129},{385... | collective-permute-start | bytes 786440 | tf_op jit(solution)/shard_map/ppermute | solution.py:48
  72.0 10.7 %collective-permute-start.8 = (bf16[2,2,2,16,1024]{4,3,2,1,0:T(8,128)(2,1)}, bf16[2,2,2,16,1024]{4,3,2,1,0:T(8,128)(2,1)S(1)}, u32[]{:S(2)}, u32[]{:S(2)}) collective-permute-start(bf16[2,2,2,16,1024]{4,3,2,1,0:T(8,128)(2,1)} %pad_maximum_fusion.3), channel_id=1, source_target_pairs={{0,256},{128,384},{256,0},{384,128},{1,257},{129,385},{257,1},{385... | collective-permute-start | bytes 786440 | tf_op jit(solution)/shard_map/ppermute | solution.py:48
  75.2 14.4 %collective-permute-start.7 = (bf16[2,2,2,16,1024]{4,3,2,1,0:T(8,128)(2,1)}, bf16[2,2,2,16,1024]{4,3,2,1,0:T(8,128)(2,1)}, u32[]{:S(2)}, u32[]{:S(2)}) collective-permute-start(bf16[2,2,2,16,1024]{4,3,2,1,0:T(8,128)(2,1)} %pad_maximum_fusion.2), channel_id=1, source_target_pairs={{0,128},{128,256},{256,384},{384,0},{1,129},{129,257},{257,385},{3... | collective-permute-start | bytes 786440 | tf_op jit(solution)/shard_map/ppermute | solution.py:48
  82.1 0.7 copy-start.5
  82.8 0.7 copy-start.6
  104.4 3.9 %copy-start.21 = (bf16[2048,1024]{1,0:T(8,128)(2,1)S(1)}, bf16[2048,1024]{1,0:T(8,128)(2,1)}, u32[]{:S(2)}) copy-start(bf16[2048,1024]{1,0:T(8,128)(2,1)} %param.11) | copy-start | bytes 12582916
  104.4 4.0 %copy-start.23 = (bf16[256,2048]{1,0:T(8,128)(2,1)S(1)}, bf16[256,2048]{1,0:T(8,128)(2,1)}, u32[]{:S(2)}) copy-start(bf16[256,2048]{1,0:T(8,128)(2,1)} %all-gather.7.cloned.1.call-done) | copy-start | bytes 3145732
  108.4 16.1 %copy-start.10 = (s32[1152]{0:T(1024)S(1)}, s32[1152]{0:T(1024)}, u32[]{:S(2)}) copy-start(s32[1152]{0:T(1024)} %iota_add_fusion) | copy-start | bytes 13828
  108.4 16.1 %copy-start.12 = (pred[1152]{0:T(1024)(128)(4,1)S(1)}, pred[1152]{0:T(1024)(128)(4,1)}, u32[]{:S(2)}) copy-start(pred[1152]{0:T(1024)(128)(4,1)} %broadcast_compare_fusion) | copy-start | bytes 3460
  108.4 16.1 %copy-start.15 = (s32[128]{0:T(128)S(1)}, s32[128]{0:T(128)}, u32[]{:S(2)}) copy-start(s32[128]{0:T(128)} %iota_add_fusion.2) | copy-start | bytes 1540
  108.4 16.1 %copy-start.18 = (bf16[128]{0:T(256)(128)(2,1)S(1)}, bf16[128]{0:T(256)(128)(2,1)}, u32[]{:S(2)}) copy-start(bf16[128]{0:T(256)(128)(2,1)} %copy-done.17) | copy-start | bytes 772
  110.5 16.8 %copy-start.3 = (bf16[9,128,128]{2,1,0:T(8,128)(2,1)}, bf16[9,128,128]{2,1,0:T(8,128)(2,1)S(1)}, u32[]{:S(2)}) copy-start(bf16[9,128,128]{2,1,0:T(8,128)(2,1)S(1)} %get-tuple-element.69) | copy-start | bytes 884740
  110.5 27.0 %collective-permute-start.10 = (bf16[2,2,2,8,1024]{4,3,2,1,0:T(8,128)(2,1)S(1)}, bf16[2,2,2,8,1024]{4,3,2,1,0:T(8,128)(2,1)S(1)}, u32[]{:S(2)}, u32[]{:S(2)}) collective-permute-start(bf16[2,2,2,8,1024]{4,3,2,1,0:T(8,128)(2,1)S(1)} %fusion.36), channel_id=1, source_target_pairs={{0,1},{1,0},{2,3},{3,2},{4,5},{5,4},{6,7},{7,6},{8,9},{9,8},{10,11... | collective-permute-start | bytes 393224 | tf_op jit(solution)/shard_map/ppermute | solution.py:52
  114.9 13.8 %collective-permute-start.13 = (bf16[2,2,2,16,1024]{4,3,2,1,0:T(8,128)(2,1)S(1)}, bf16[2,2,2,16,1024]{4,3,2,1,0:T(8,128)(2,1)S(1)}, u32[]{:S(2)}, u32[]{:S(2)}) collective-permute-start(bf16[2,2,2,16,1024]{4,3,2,1,0:T(8,128)(2,1)S(1)} %pad_maximum_fusion.7), channel_id=1, source_target_pairs={{0,384},{128,0},{256,128},{384,256},{1,385},{129,1},{257,129},{385... | collective-permute-start | bytes 786440 | tf_op jit(solution)/shard_map/ppermute | solution.py:48
  119.5 9.3 %collective-permute-start.12 = (bf16[2,2,2,16,1024]{4,3,2,1,0:T(8,128)(2,1)S(1)}, bf16[2,2,2,16,1024]{4,3,2,1,0:T(8,128)(2,1)S(1)}, u32[]{:S(2)}, u32[]{:S(2)}) collective-permute-start(bf16[2,2,2,16,1024]{4,3,2,1,0:T(8,128)(2,1)S(1)} %pad_maximum_fusion.6), channel_id=1, source_target_pairs={{0,256},{128,384},{256,0},{384,128},{1,257},{129,385},{257,1},{385... | collective-permute-start | bytes 786440 | tf_op jit(solution)/shard_map/ppermute | solution.py:48
  122.0 8.9 %collective-permute-start.11 = (bf16[2,2,2,16,1024]{4,3,2,1,0:T(8,128)(2,1)S(1)}, bf16[2,2,2,16,1024]{4,3,2,1,0:T(8,128)(2,1)S(1)}, u32[]{:S(2)}, u32[]{:S(2)}) collective-permute-start(bf16[2,2,2,16,1024]{4,3,2,1,0:T(8,128)(2,1)S(1)} %pad_maximum_fusion.5), channel_id=1, source_target_pairs={{0,128},{128,256},{256,384},{384,0},{1,129},{129,257},{257,385},{3... | collective-permute-start | bytes 786440 | tf_op jit(solution)/shard_map/ppermute | solution.py:48
  131.1 11.2 %copy-start.13 = (s32[2,2,8]{2,1,0:T(2,128)S(1)}, s32[2,2,8]{2,1,0:T(2,128)}, u32[]{:S(2)}) copy-start(s32[2,2,8]{2,1,0:T(2,128)} %get-tuple-element.82) | copy-start | bytes 388
  131.1 11.2 %copy-start.14 = (s32[2,2,8]{2,1,0:T(2,128)S(1)}, s32[2,2,8]{2,1,0:T(2,128)}, u32[]{:S(2)}) copy-start(s32[2,2,8]{2,1,0:T(2,128)} %get-tuple-element.83) | copy-start | bytes 388
  131.1 11.0 %collective-permute-start.14 = (bf16[2,2,2,8,1024]{4,3,2,1,0:T(8,128)(2,1)S(1)}, bf16[2,2,2,8,1024]{4,3,2,1,0:T(8,128)(2,1)S(1)}, u32[]{:S(2)}, u32[]{:S(2)}) collective-permute-start(bf16[2,2,2,8,1024]{4,3,2,1,0:T(8,128)(2,1)S(1)} %fusion.37), channel_id=1, source_target_pairs={{0,1},{1,0},{2,3},{3,2},{4,5},{5,4},{6,7},{7,6},{8,9},{9,8},{10,11... | collective-permute-start | bytes 393224 | tf_op jit(solution)/shard_map/ppermute | solution.py:52
  137.5 29.5 %copy-start.19 = (f32[128]{0:T(128)S(1)}, f32[128]{0:T(128)}, u32[]{:S(2)}) copy-start(f32[128]{0:T(128)} %reshape.278) | copy-start | bytes 1540
  143.5 21.9 %all-to-all-start = ((f32[64,1,192]{2,1,0:T(1,128)}), f32[64,1,192]{2,1,0:T(1,128)S(1)}, u32[]{:S(2)}, u32[]{:S(2)}) async-start(f32[64,1,192]{2,1,0:T(1,128)} %reshape.304), calls=%async_computation | async-start | bytes 131072 | tf_op jit(solution)/shard_map/all_to_all | solution.py:171
  160.5 19.5 %copy-start.11 = (s32[1024]{0:T(1024)S(1)}, s32[1024]{0:T(1024)}, u32[]{:S(2)}) copy-start(s32[1024]{0:T(1024)} %eq.76) | copy-start | bytes 12292
  160.5 19.5 %copy-start.16 = (s32[128]{0:T(128)S(1)}, s32[128]{0:T(128)}, u32[]{:S(2)}) copy-start(s32[128]{0:T(128)} %iota_add_fusion.2) | copy-start | bytes 1540
  167.6 12.4 %all-to-all-start.1 = ((f32[8,1,128]{2,1,0:T(1,128)}), f32[8,1,128]{2,1,0:T(1,128)S(1)}, u32[]{:S(2)}, u32[]{:S(2)}) async-start(f32[8,1,128]{2,1,0:T(1,128)} %broadcast_in_dim.61), calls=%async_computation.1 | async-start | bytes 8192 | tf_op jit(solution)/shard_map/all_to_all | solution.py:181
  180.0 1.7 copy-start
  181.7 13.8 %copy-start.4 = (bf16[9,128,128]{2,1,0:T(8,128)(2,1)S(1)}, bf16[9,128,128]{2,1,0:T(8,128)(2,1)}, u32[]{:S(2)}) copy-start(bf16[9,128,128]{2,1,0:T(8,128)(2,1)} %copy-done.3) | copy-start | bytes 884740
  182.7 20.7 %collective-permute-start.22 = (bf16[128,256]{0,1:T(8,128)(2,1)S(1)}, bf16[128,256]{0,1:T(8,128)(2,1)S(1)}, u32[]{:S(2)}, u32[]{:S(2)}) collective-permute-start(bf16[128,256]{0,1:T(8,128)(2,1)S(1)} %get-tuple-element.71), channel_id=1, source_target_pairs={{16,0},{18,2},{20,4},{22,6},{24,8},{26,10},{28,12},{30,14},{32,16}... | collective-permute-start | bytes 196616 | tf_op jit(solution)/shard_map/ppermute | solution.py:44
  185.9 19.8 %collective-permute-start.21 = (bf16[128,256]{0,1:T(8,128)(2,1)S(1)}, bf16[128,256]{0,1:T(8,128)(2,1)S(1)}, u32[]{:S(2)}, u32[]{:S(2)}) collective-permute-start(bf16[128,256]{0,1:T(8,128)(2,1)S(1)} %get-tuple-element.72), channel_id=1, source_target_pairs={{14,0},{16,2},{18,4},{20,6},{22,8},{24,10},{26,12},{28,14},{30,16}... | collective-permute-start | bytes 196616 | tf_op jit(solution)/shard_map/ppermute | solution.py:44
  192.4 16.7 %collective-permute-start.20 = (bf16[128,256]{0,1:T(8,128)(2,1)S(1)}, bf16[128,256]{0,1:T(8,128)(2,1)S(1)}, u32[]{:S(2)}, u32[]{:S(2)}) collective-permute-start(bf16[128,256]{0,1:T(8,128)(2,1)S(1)} %get-tuple-element.73), channel_id=1, source_target_pairs={{12,0},{14,2},{16,4},{18,6},{20,8},{22,10},{24,12},{26,14},{28,16}... | collective-permute-start | bytes 196616 | tf_op jit(solution)/shard_map/ppermute | solution.py:44
  197.4 16.3 %collective-permute-start.19 = (bf16[128,256]{0,1:T(8,128)(2,1)S(1)}, bf16[128,256]{0,1:T(8,128)(2,1)S(1)}, u32[]{:S(2)}, u32[]{:S(2)}) collective-permute-start(bf16[128,256]{0,1:T(8,128)(2,1)S(1)} %get-tuple-element.74), channel_id=1, source_target_pairs={{10,0},{12,2},{14,4},{16,6},{18,8},{20,10},{22,12},{24,14},{26,16}... | collective-permute-start | bytes 196616 | tf_op jit(solution)/shard_map/ppermute | solution.py:44
  199.3 14.4 %collective-permute-start.18 = (bf16[128,256]{0,1:T(8,128)(2,1)S(1)}, bf16[128,256]{0,1:T(8,128)(2,1)S(1)}, u32[]{:S(2)}, u32[]{:S(2)}) collective-permute-start(bf16[128,256]{0,1:T(8,128)(2,1)S(1)} %get-tuple-element.75), channel_id=1, source_target_pairs={{8,0},{10,2},{12,4},{14,6},{16,8},{18,10},{20,12},{22,14},{24,16},... | collective-permute-start | bytes 196616 | tf_op jit(solution)/shard_map/ppermute | solution.py:44
  203.5 10.2 %collective-permute-start.17 = (bf16[128,256]{0,1:T(8,128)(2,1)S(1)}, bf16[128,256]{0,1:T(8,128)(2,1)S(1)}, u32[]{:S(2)}, u32[]{:S(2)}) collective-permute-start(bf16[128,256]{0,1:T(8,128)(2,1)S(1)} %get-tuple-element.76), channel_id=1, source_target_pairs={{6,0},{8,2},{10,4},{12,6},{14,8},{16,10},{18,12},{20,14},{22,16},{... | collective-permute-start | bytes 196616 | tf_op jit(solution)/shard_map/ppermute | solution.py:44
  205.7 10.5 %collective-permute-start.16 = (bf16[128,256]{0,1:T(8,128)(2,1)S(1)}, bf16[128,256]{0,1:T(8,128)(2,1)S(1)}, u32[]{:S(2)}, u32[]{:S(2)}) collective-permute-start(bf16[128,256]{0,1:T(8,128)(2,1)S(1)} %get-tuple-element.77), channel_id=1, source_target_pairs={{4,0},{6,2},{8,4},{10,6},{12,8},{14,10},{16,12},{18,14},{20,16},{2... | collective-permute-start | bytes 196616 | tf_op jit(solution)/shard_map/ppermute | solution.py:44
  209.1 9.5 %collective-permute-start.15 = (bf16[128,256]{0,1:T(8,128)(2,1)S(1)}, bf16[128,256]{0,1:T(8,128)(2,1)S(1)}, u32[]{:S(2)}, u32[]{:S(2)}) collective-permute-start(bf16[128,256]{0,1:T(8,128)(2,1)S(1)} %get-tuple-element.70), channel_id=1, source_target_pairs={{2,0},{4,2},{6,4},{8,6},{10,8},{12,10},{14,12},{16,14},{18,16},{20... | collective-permute-start | bytes 196616 | tf_op jit(solution)/shard_map/ppermute | solution.py:44
Sparse Core Ops, SparseCore 0:
  16.4 38.1 all-gather.4
  61.5 42.7 all-gather.6

commit v2 on v1

--- a/solution.py
+++ b/solution.py
@@ -25,13 +25,16 @@
     return lax.ppermute(block, "ctx", route)
 
 
-def over_y(block, bits):
-    return ctx_move(block, lambda z, y, core: (z, y ^ bits, core))
-
-
-def along_all_z(block):
-    groups = [[z * 8 + rest for z in range(Z)] for rest in range(Y * CORES)]
-    return lax.all_gather(block, "ctx", axis_index_groups=groups)
+def across_chips(block):
+    groups = [[chip * CORES + core for chip in range(Z * Y)] for core in range(CORES)]
+    copies = jnp.broadcast_to(block, (Z * Y,) + block.shape)
+    return lax.all_to_all(copies, "ctx", 0, 0, axis_index_groups=groups)
+
+
+def across_row(blocks):
+    row = Y * CORES
+    groups = [[z * row + place for place in range(row)] for z in range(Z)]
+    return lax.all_to_all(blocks, "ctx", 0, 0, axis_index_groups=groups)
 
 
 def other_core(block):
@@ -52,14 +55,12 @@
     return lax.ppermute(block, "tp", [(0, 1), (1, 0)])
 
 
-def section_parts(gathered, heads, section):
-    rows = gathered.shape[1]
+def section_parts(gathered, weight, section):
+    mine = gathered.reshape(-1, gathered.shape[2])
     parts = []
-    for head in heads:
-        part = jnp.dot(
-            gathered.reshape(Z * rows, -1), head, preferred_element_type=jnp.float32
-        )
-        parts.append(part.reshape(SECTIONS, 2, rows // PIECE, PIECE, head.shape[1]))
+    for rows in (mine, other_core(mine)):
+        part = jnp.dot(rows, weight, preferred_element_type=jnp.float32)
+        parts.append(part.reshape(SECTIONS, 2, Y, PIECE, weight.shape[1]))
 
     def rows_for(step):
         place = lax.rem(section + step, SECTIONS)
@@ -89,18 +90,14 @@
 
 
 def row_stats(logits, columns, ids):
-    picked = jnp.sum(jnp.where(columns == ids[None, ..., None], logits, 0.0), axis=(0, 4))
-    row_top = jnp.max(logits, axis=(0, 4))
-    row_total = jnp.sum(jnp.exp(logits - row_top[None, ..., None]), axis=(0, 4))
+    picked = jnp.sum(jnp.where(columns == ids[..., None], logits, 0.0), axis=-1)
+    row_top = jnp.max(logits, axis=-1)
+    row_total = jnp.sum(jnp.exp(logits - row_top[..., None]), axis=-1)
     return jnp.stack([row_top, row_total, picked])
 
 
-def y_exchanged(array, axis, y):
-    shape = array.shape
-    pairs = array.reshape(shape[:axis] + (2, 2) + shape[axis + 1 :])
-    pairs = jnp.where(y % 2 == 1, jnp.flip(pairs, axis + 1), pairs)
-    pairs = jnp.where(y // 2 == 1, jnp.flip(pairs, axis), pairs)
-    return pairs.reshape(shape)
+def cores_exchanged(array, axis, core):
+    return jnp.where(core == 1, jnp.flip(array, axis), array)
 
 
 def key_value_window(keys, values, segment_ids):
@@ -132,51 +129,33 @@
     ctx_index = lax.axis_index("ctx")
     section = lax.axis_index("section")
     tp = lax.axis_index("tp")
-    y, core = lax.rem(ctx_index // 2, 4), lax.rem(ctx_index, 2)
-
-    near = jnp.concatenate([teacher_hidden, over_y(teacher_hidden, 1)], axis=0)
-    far = over_y(near, 2)
-    far, segment_ids = lax.optimization_barrier((far, segment_ids))
+    place, core = lax.rem(ctx_index, Y * CORES), lax.rem(ctx_index, CORES)
+
+    gathered = across_chips(teacher_hidden)
     window = key_value_window(keys, values, segment_ids)
-    near_all, far, other_head, window = lax.optimization_barrier(
-        (along_all_z(near), far, other_core(lm_head), window)
-    )
-    far_all = along_all_z(far)
-    heads = (lm_head, other_head)
-    keep, give = tp_halves(section_sums(section_parts(near_all, heads, section)), tp)
-    give, far_all, window = lax.optimization_barrier((give, far_all, window))
-    near_logits = tp_sums(keep, give)
-    far_parts = section_parts(far_all, heads, section)
-    far_logits = tp_sums(*tp_halves(section_sums(far_parts), tp))
+    gathered, window = lax.optimization_barrier((gathered, window))
+    logits = tp_sums(*tp_halves(section_sums(section_parts(gathered, lm_head, section)), tp))
 
     def kept(array, axis):
         return lax.dynamic_index_in_dim(
             lax.dynamic_index_in_dim(array, section, 0, keepdims=False), tp, axis, keepdims=False
         )
 
-    token_ids = kept(sampled_ids.reshape(SECTIONS, 2, Y, CORES, TPS, PIECE // TPS), 3)
-    token_ids = lax.dynamic_index_in_dim(token_ids, core, 2, keepdims=False)
-    relative_ids = y_exchanged(token_ids, 1, y)
-    vocab = lm_head.shape[1]
-    starts = jnp.stack([ctx_index, ctx_index + 1 - 2 * core]) * vocab
-    columns = starts[:, None, None, None, None] + jnp.arange(vocab, dtype=jnp.int32)
-    stats = jnp.concatenate(
-        [
-            row_stats(near_logits, columns, relative_ids[:, :2]),
-            row_stats(far_logits, columns, relative_ids[:, 2:]),
-        ],
-        axis=2,
-    )
-    stats = y_exchanged(stats, 2, y).reshape(3, -1)
+    def kept_rows(array):
+        rows = kept(array.reshape(SECTIONS, 2, Y, CORES, TPS, PIECE // TPS), 3)
+        return rows.transpose(2, 0, 1, 3)
+
+    columns = ctx_index * lm_head.shape[1] + jnp.arange(lm_head.shape[1], dtype=jnp.int32)
+    stats = row_stats(logits, columns, cores_exchanged(kept_rows(sampled_ids), 0, core))
+    stats = cores_exchanged(stats, 1, core).reshape(3, -1)
     everywhere = lax.all_to_all(
         jnp.broadcast_to(stats, (Z * Y * CORES,) + stats.shape), "ctx", 0, 0
-    ).reshape(Z * Y, CORES, 3, -1)
-    highest = jnp.max(everywhere[:, :, 0], axis=0)
-    summed = jnp.sum(everywhere[:, :, 1] * jnp.exp(everywhere[:, :, 0] - highest), axis=0)
-    teacher_logprob = jnp.sum(everywhere[:, :, 2], axis=0) - highest - jnp.log(summed)
-    student_rows = kept(student_logprob.reshape(SECTIONS, 2, Y, CORES, TPS, PIECE // TPS), 3)
-    student_rows = student_rows.transpose(2, 0, 1, 3).reshape(CORES, -1)
-    advantage = jnp.clip(teacher_logprob - student_rows, -clip_bound, clip_bound).reshape(-1)
+    )
+    highest = jnp.max(everywhere[:, 0], axis=0)
+    summed = jnp.sum(everywhere[:, 1] * jnp.exp(everywhere[:, 0] - highest), axis=0)
+    teacher_logprob = jnp.sum(everywhere[:, 2], axis=0) - highest - jnp.log(summed)
+    student_rows = kept_rows(student_logprob).reshape(-1)
+    advantage = jnp.clip(teacher_logprob - student_rows, -clip_bound, clip_bound)
     count = SECTIONS * TPS
     everything = lax.all_to_all(
         jnp.broadcast_to(advantage, (count,) + advantage.shape), ("section", "tp"), 0, 0
@@ -240,10 +219,14 @@
     both = jnp.concatenate([grad_key, grad_value], axis=1).reshape(
         FARTHEST + 1, seq_rows, 2 * head_dim
     )
-    total = both[FARTHEST]
-    for distance in range(1, FARTHEST + 1):
-        given = both[FARTHEST - distance].astype(jnp.bfloat16)
-        total = total + passed_along(given, -distance).astype(jnp.float32)
+    cyclic = both[1:].astype(jnp.bfloat16)
+    cyclic = jnp.concatenate([cyclic, cyclic], axis=0)
+    given = lax.dynamic_slice_in_dim(cyclic, Y * CORES - 1 - place, Y * CORES, 0)
+    arrived = across_row(given).astype(jnp.float32)
+    sender = jnp.arange(Y * CORES, dtype=jnp.int32)[:, None, None]
+    back = both[0] + jnp.sum(jnp.where(sender < place, arrived, 0.0), axis=0)
+    back = passed_along(back.astype(jnp.bfloat16), -Y * CORES).astype(jnp.float32)
+    total = both[FARTHEST] + jnp.sum(jnp.where(sender > place, arrived, 0.0), axis=0) + back
     total = total.astype(jnp.bfloat16)
     d_queries = (
         grad_query.reshape(group, seq_rows, head_dim)

time: 228 us -> 221 us (0.969)
  the two profiles are of different devices: /device:TPU:217 before, /device:TPU:1 now
where the time goes in v2:
time: 221 us; the launch traced here: 220 us
  starting transfers between devices  93 us (42%)
  waiting for transfers between devices  89.3 us (40%)
  local copies, waits for them, and re-layouts  15.6 us (7%)
  matrix products  12.6 us (6%)
  other arithmetic  8.45 us (4%)
    ppermute x5, waiting for transfers between devices, passed_along(): return lax.ppermute(block, 'ctx', route)  32.7 us
    ppermute x5, starting transfers between devices, passed_along(): return lax.ppermute(block, 'ctx', route)  26.6 us
    ppermute x3, waiting for transfers between devices, along_section(): lax.ppermute(block, 'section', [(s, (s + step) % SECTIONS) for s in range...  22.1 us
    all_to_all x1, starting transfers between devices, body(): lax.all_to_all(jnp.broadcast_to(stats, (Z * Y * CORES,) + stats.shape), '...  22.1 us
    all_to_all x1, starting transfers between devices, across_chips(): return lax.all_to_all(copies, 'ctx', 0, 0, axis_index_groups=groups)  14.4 us
    all_to_all x1, waiting for transfers between devices, across_row(): return lax.all_to_all(blocks, 'ctx', 0, 0, axis_index_groups=groups)  11 us
    all_to_all x1, waiting for transfers between devices, body(): lax.all_to_all(jnp.broadcast_to(stats, (Z * Y * CORES,) + stats.shape), '...  10.2 us
    ppermute x3, starting transfers between devices, along_section(): lax.ppermute(block, 'section', [(s, (s + step) % SECTIONS) for s in range...  9.33 us
  transfers between devices with their start and end apart: 14, of which 9 were waited for; matrix products, arithmetic and copies ran while one was open for 10% of the time, Pallas kernels for 0%

profile of v2, /device:TPU:1, one launch (start us, length us, event | category | flops | bytes accessed | tf_op | source)
XLA Modules:
  0.0 220.4 jit_solution(4450065397889947888)
XLA Ops:
  0.6 2.4 %broadcast_in_dim.75 = bf16[32,16,2048]{2,1,0:T(8,128)(2,1)} broadcast(bf16[16,2048]{1,0:T(8,128)(2,1)} %param.10), dimensions={1,2} | broadcast | bytes 2162688 | tf_op jit(solution)/shard_map/broadcast_in_dim | solution.py:30
  3.1 14.4 %all-to-all-start = ((bf16[32,16,2048]{2,1,0:T(8,128)(2,1)}), bf16[32,16,2048]{2,1,0:T(8,128)(2,1)S(1)}, u32[]{:S(2)}, u32[]{:S(2)}) async-start(bf16[32,16,2048]{2,1,0:T(8,128)(2,1)} %broadcast_in_dim.75), calls=%async_computation | async-start | bytes 4194304 | tf_op jit(solution)/shard_map/all_to_all | solution.py:31
  17.7 3.8 %collective-permute-start = (bf16[1,144,256]{2,1,0:T(8,128)(2,1)S(1)}, bf16[1,144,256]{2,1,0:T(8,128)(2,1)}, u32[]{:S(2)}, u32[]{:S(2)}) collective-permute-start(bf16[1,144,256]{2,1,0:T(8,128)(2,1)S(1)} %maximum_bitcast_fusion), channel_id=1, source_target_pairs={{0,16},{2,18},{4,20},{6,22},{8,24},{10,26},{12,28},{14,30},{16,32}... | collective-permute-start | bytes 221192 | tf_op jit(solution)/shard_map/ppermute | solution.py:47
  21.4 4.5 %collective-permute-start.1 = (bf16[1,144,256]{2,1,0:T(8,128)(2,1)S(1)}, bf16[1,144,256]{2,1,0:T(8,128)(2,1)S(1)}, u32[]{:S(2)}, u32[]{:S(2)}) collective-permute-start(bf16[1,144,256]{2,1,0:T(8,128)(2,1)S(1)} %maximum_bitcast_fusion), channel_id=1, source_target_pairs={{0,2},{2,4},{4,6},{6,8},{8,10},{10,12},{12,14},{14,16},{16,18},{18... | collective-permute-start | bytes 221192 | tf_op jit(solution)/shard_map/ppermute | solution.py:47
  25.9 0.1 reshape.205
  26.4 28.0 %collective-permute-done.1 = bf16[1,144,256]{2,1,0:T(8,128)(2,1)S(1)} collective-permute-done((bf16[1,144,256]{2,1,0:T(8,128)(2,1)S(1)}, bf16[1,144,256]{2,1,0:T(8,128)(2,1)S(1)}, u32[]{:S(2)}, u32[]{:S(2)}) %collective-permute-start.1) | collective-permute-done | bytes 73760 | tf_op jit(solution)/shard_map/ppermute | solution.py:47
  54.4 0.7 pad_maximum_fusion.4
  55.0 14.0 %collective-permute-start.2 = (bf16[2,144,256]{2,1,0:T(8,128)(2,1)}, bf16[2,144,256]{2,1,0:T(8,128)(2,1)S(1)}, u32[]{:S(2)}, u32[]{:S(2)}) collective-permute-start(bf16[2,144,256]{2,1,0:T(8,128)(2,1)} %pad_maximum_fusion.4), channel_id=1, source_target_pairs={{0,4},{2,6},{4,8},{6,10},{8,12},{10,14},{12,16},{14,18},{16,20},{1... | collective-permute-start | bytes 442376 | tf_op jit(solution)/shard_map/ppermute | solution.py:47
  69.0 0.6 iota_add_fusion.1
  69.6 0.6 reshape.206
  70.3 0.2 copy.76
  70.6 0.2 copy.77
  71.0 0.7 eq.55
  71.8 3.1 %collective-permute-start.3 = (bf16[4,144,256]{2,1,0:T(8,128)(2,1)S(1)}, bf16[4,144,256]{2,1,0:T(8,128)(2,1)S(1)}, u32[]{:S(2)}, u32[]{:S(2)}) collective-permute-start(bf16[4,144,256]{2,1,0:T(8,128)(2,1)S(1)} %pad_maximum_fusion.3), channel_id=1, source_target_pairs={{0,8},{2,10},{4,12},{6,14},{8,16},{10,18},{12,20},{14,22},{16,24},... | collective-permute-start | bytes 884744 | tf_op jit(solution)/shard_map/ppermute | solution.py:47
  74.9 0.9 constant_dynamic-update-slice_fusion.4
  75.8 2.7 %collective-permute-done.3 = bf16[4,144,256]{2,1,0:T(8,128)(2,1)S(1)} collective-permute-done((bf16[4,144,256]{2,1,0:T(8,128)(2,1)S(1)}, bf16[4,144,256]{2,1,0:T(8,128)(2,1)S(1)}, u32[]{:S(2)}, u32[]{:S(2)}) %collective-permute-start.3) | collective-permute-done | bytes 294944 | tf_op jit(solution)/shard_map/ppermute | solution.py:47
  78.6 0.9 constant_dynamic-update-slice_fusion.2
  79.6 6.5 %collective-permute-start.4 = (bf16[512,2048]{1,0:T(8,128)(2,1)S(1)}, bf16[512,2048]{1,0:T(8,128)(2,1)S(1)}, u32[]{:S(2)}, u32[]{:S(2)}) collective-permute-start(bf16[512,2048]{1,0:T(8,128)(2,1)S(1)} %bitcast.141), channel_id=1, source_target_pairs={{0,2},{2,0},{4,6},{6,4},{8,10},{10,8},{12,14},{14,12},{16,18},{18,... | collective-permute-start | bytes 6291464 | tf_op jit(solution)/shard_map/ppermute | solution.py:25
  86.1 0.8 fusion.40
  86.9 1.1 and_and_fusion
  88.0 0.6 tile.7
  88.6 1.1 fusion.2
  89.7 1.0 copy-done.19
  90.8 2.4 %fusion.3 = f32[4,2,4,16,1024]{4,3,2,1,0:T(8,128)S(1)} fusion(bf16[4,2,4,16,2048]{4,3,2,1,0:T(8,128)(2,1)S(1)} %bitcast.142, bf16[2048,1024]{1,0:T(8,128)(2,1)S(1)} %copy-done.19), kind=kOutput, calls=%fused_computation.9 | convolution fusion | flops 2147483648 | bytes 8388608 | tf_op jit(solution)/shard_map/dot_general | solution.py:62
  93.1 2.3 %fusion.43 = f32[512,1024]{1,0:T(8,128)S(1)} fusion(bf16[512,2048]{1,0:T(8,128)(2,1)S(1)} %collective-permute-done.4, bf16[2048,1024]{1,0:T(8,128)(2,1)S(1)} %copy-done.19), kind=kOutput, calls=%fused_computation.106 | convolution fusion | flops 2147483648 | bytes 8388608 | tf_op jit(solution)/shard_map/dot_general | solution.py:62
  95.5 0.2 dynamic-slice_convert_fusion.5
  95.8 4.4 %collective-permute-start.7 = (bf16[2,2,4,16,1024]{4,3,2,1,0:T(8,128)(2,1)S(1)}, bf16[2,2,4,16,1024]{4,3,2,1,0:T(8,128)(2,1)S(1)}, u32[]{:S(2)}, u32[]{:S(2)}) collective-permute-start(bf16[2,2,4,16,1024]{4,3,2,1,0:T(8,128)(2,1)S(1)} %pad_maximum_fusion.2), channel_id=1, source_target_pairs={{0,384},{128,0},{256,128},{384,256},{1,385},{129,1},{257,129},{385... | collective-permute-start | bytes 1572872 | tf_op jit(solution)/shard_map/ppermute | solution.py:51
  100.3 2.4 %collective-permute-start.6 = (bf16[2,2,4,16,1024]{4,3,2,1,0:T(8,128)(2,1)S(1)}, bf16[2,2,4,16,1024]{4,3,2,1,0:T(8,128)(2,1)S(1)}, u32[]{:S(2)}, u32[]{:S(2)}) collective-permute-start(bf16[2,2,4,16,1024]{4,3,2,1,0:T(8,128)(2,1)S(1)} %pad_maximum_fusion.1), channel_id=1, source_target_pairs={{0,256},{128,384},{256,0},{384,128},{1,257},{129,385},{257,1},{385... | collective-permute-start | bytes 1572872 | tf_op jit(solution)/shard_map/ppermute | solution.py:51
  102.8 2.5 %collective-permute-start.5 = (bf16[2,2,4,16,1024]{4,3,2,1,0:T(8,128)(2,1)S(1)}, bf16[2,2,4,16,1024]{4,3,2,1,0:T(8,128)(2,1)S(1)}, u32[]{:S(2)}, u32[]{:S(2)}) collective-permute-start(bf16[2,2,4,16,1024]{4,3,2,1,0:T(8,128)(2,1)S(1)} %pad_maximum_fusion), channel_id=1, source_target_pairs={{0,128},{128,256},{256,384},{384,0},{1,129},{129,257},{257,385},{3... | collective-permute-start | bytes 1572872 | tf_op jit(solution)/shard_map/ppermute | solution.py:51
  105.3 1.3 fusion.5
  106.7 15.9 %collective-permute-done.7 = bf16[2,2,4,16,1024]{4,3,2,1,0:T(8,128)(2,1)S(1)} collective-permute-done((bf16[2,2,4,16,1024]{4,3,2,1,0:T(8,128)(2,1)S(1)}, bf16[2,2,4,16,1024]{4,3,2,1,0:T(8,128)(2,1)S(1)}, u32[]{:S(2)}, u32[]{:S(2)}) %collective-permute-start.7) | collective-permute-done | bytes 524320 | tf_op jit(solution)/shard_map/ppermute | solution.py:51
  122.6 6.1 %collective-permute-done.5 = bf16[2,2,4,16,1024]{4,3,2,1,0:T(8,128)(2,1)S(1)} collective-permute-done((bf16[2,2,4,16,1024]{4,3,2,1,0:T(8,128)(2,1)S(1)}, bf16[2,2,4,16,1024]{4,3,2,1,0:T(8,128)(2,1)S(1)}, u32[]{:S(2)}, u32[]{:S(2)}) %collective-permute-start.5) | collective-permute-done | bytes 524320 | tf_op jit(solution)/shard_map/ppermute | solution.py:51
  128.7 0.3 fusion.15
  129.1 5.1 %collective-permute-start.8 = (bf16[2,2,4,8,1024]{4,3,2,1,0:T(8,128)(2,1)S(1)}, bf16[2,2,4,8,1024]{4,3,2,1,0:T(8,128)(2,1)S(1)}, u32[]{:S(2)}, u32[]{:S(2)}) collective-permute-start(bf16[2,2,4,8,1024]{4,3,2,1,0:T(8,128)(2,1)S(1)} %fusion.19), channel_id=1, source_target_pairs={{0,1},{1,0},{2,3},{3,2},{4,5},{5,4},{6,7},{7,6},{8,9},{9,8},{10,11... | collective-permute-start | bytes 786440 | tf_op jit(solution)/shard_map/ppermute | solution.py:55
  134.3 1.4 divide_convert_fusion
  135.7 6.7 %collective-permute-done.8 = bf16[2,2,4,8,1024]{4,3,2,1,0:T(8,128)(2,1)S(1)} collective-permute-done((bf16[2,2,4,8,1024]{4,3,2,1,0:T(8,128)(2,1)S(1)}, bf16[2,2,4,8,1024]{4,3,2,1,0:T(8,128)(2,1)S(1)}, u32[]{:S(2)}, u32[]{:S(2)}) %collective-permute-start.8) | collective-permute-done | bytes 262176 | tf_op jit(solution)/shard_map/ppermute | solution.py:55
  142.5 0.1 fusion.33
  142.6 0.3 exponential_reduce_fusion
  143.0 0.7 broadcast_in_dim.79
  143.7 22.1 %all-to-all-start.1 = ((f32[64,3,128]{2,1,0:T(4,128)}), f32[64,3,128]{2,1,0:T(4,128)S(1)}, u32[]{:S(2)}, u32[]{:S(2)}) async-start(f32[64,3,128]{2,1,0:T(4,128)} %broadcast_in_dim.79), calls=%async_computation.1 | async-start | bytes 262144 | tf_op jit(solution)/shard_map/all_to_all | solution.py:151
  165.8 0.6 fusion.7
  166.4 10.2 %all-to-all-done.1 = f32[64,3,128]{2,1,0:T(4,128)S(1)} async-done(((f32[64,3,128]{2,1,0:T(4,128)}), f32[64,3,128]{2,1,0:T(4,128)S(1)}, u32[]{:S(2)}, u32[]{:S(2)}) %all-to-all-start.1) | async-done | bytes 98336 | tf_op jit(solution)/shard_map/all_to_all | solution.py:151
  176.8 0.6 broadcast_in_dim.80
  177.4 3.8 %all-to-all-start.2 = ((f32[8,1,128]{2,1,0:T(1,128)}), f32[8,1,128]{2,1,0:T(1,128)S(1)}, u32[]{:S(2)}, u32[]{:S(2)}) async-start(f32[8,1,128]{2,1,0:T(1,128)} %broadcast_in_dim.80), calls=%async_computation.2 | async-start | bytes 8192 | tf_op jit(solution)/shard_map/all_to_all | solution.py:160
  181.2 2.3 %fusion.1 = bf16[1024,1152]{0,1:T(8,128)(2,1)} fusion(bf16[1024,1152]{0,1:T(8,128)(2,1)S(1)} %divide_convert_fusion, bf16[1152,128]{1,0:T(8,128)(2,1)S(1)} %bitcast.159, f32[1024]{0:T(1024)S(1)} %fusion.7, bf16[16,8,8,128]{3,2,1,0:T(8,128)(2,1)S(1)} %bitcast.146), kind=kOutput, calls=%fused_computation.4 | convolution fusion | flops 307888128 | bytes 5279744 | tf_op jit(solution)/shard_map/dot_general | solution.py:207
  183.4 6.6 %all-to-all-done.2 = f32[8,1,128]{2,1,0:T(1,128)S(1)} async-done(((f32[8,1,128]{2,1,0:T(1,128)}), f32[8,1,128]{2,1,0:T(1,128)S(1)}, u32[]{:S(2)}, u32[]{:S(2)}) %all-to-all-start.2) | async-done | bytes 4128 | tf_op jit(solution)/shard_map/all_to_all | solution.py:160
  190.0 0.2 select_reduce_fusion
  190.2 0.9 fusion.21
  191.1 0.8 copy-done
  191.9 0.9 fusion.20
  192.8 1.0 fusion.17
  193.8 5.2 %all-to-all-start.3 = ((bf16[8,128,256]{1,2,0:T(8,128)(2,1)}), bf16[8,128,256]{1,2,0:T(8,128)(2,1)S(1)}, u32[]{:S(2)}, u32[]{:S(2)}) async-start(bf16[8,128,256]{1,2,0:T(8,128)(2,1)} %fusion.17), calls=%async_computation.3 | async-start | bytes 1048576 | tf_op jit(solution)/shard_map/all_to_all | solution.py:37
  199.1 0.5 broadcast.123
  199.6 0.7 reduce.7
  200.4 2.2 %fusion.8 = bf16[16,8,8,128]{3,1,2,0:T(8,128)(2,1)S(1)} fusion(bf16[1024,1152]{0,1:T(8,128)(2,1)} %fusion.1, bf16[1152,128]{1,0:T(8,128)(2,1)S(1)} %bitcast.157, f32[1024]{0:T(1024)S(1)} %broadcast_bitcast_fusion), kind=kOutput, calls=%fused_computation.22 | convolution fusion | flops 302252032 | bytes 2920448 | tf_op jit(solution)/shard_map/dot_general | solution.py:211
  202.6 11.0 %all-to-all-done.3 = bf16[8,128,256]{1,2,0:T(8,128)(2,1)S(1)} async-done(((bf16[8,128,256]{1,2,0:T(8,128)(2,1)}), bf16[8,128,256]{1,2,0:T(8,128)(2,1)S(1)}, u32[]{:S(2)}, u32[]{:S(2)}) %all-to-all-start.3) | async-done | bytes 524320 | tf_op jit(solution)/shard_map/all_to_all | solution.py:37
  213.6 0.3 fusion.9
  213.9 1.3 collective-permute-start.9
  215.2 0.6 reshape.208
  215.9 0.2 copy.79
  216.1 0.8 copy.122
  216.9 2.0 collective-permute-done.9
  218.9 0.7 copy.82
  219.6 0.7 copy.83
  (92 shorter events, 1.6 us)
Async XLA Ops:
  3.1 14.5 %copy-start.20 = (s32[128]{0:T(128)S(1)}, s32[128]{0:T(128)}, u32[]{:S(2)}) copy-start(s32[128]{0:T(128)} %param.19) | copy-start | bytes 1540
  3.1 14.6 %copy-start.7 = (bf16[128,128]{1,0:T(8,128)(2,1)S(1)}, bf16[128,128]{1,0:T(8,128)(2,1)}, u32[]{:S(2)}) copy-start(bf16[128,128]{1,0:T(8,128)(2,1)} %param.17) | copy-start | bytes 98308
  3.1 14.6 %copy-start.8 = (bf16[128,128]{1,0:T(8,128)(2,1)S(1)}, bf16[128,128]{1,0:T(8,128)(2,1)}, u32[]{:S(2)}) copy-start(bf16[128,128]{1,0:T(8,128)(2,1)} %param.16) | copy-start | bytes 98308
  3.1 22.9 %copy-start.11 = (f32[1024]{0:T(1024)S(1)}, f32[1024]{0:T(1024)}, u32[]{:S(2)}) copy-start(f32[1024]{0:T(1024)} %param.13) | copy-start | bytes 12292
  3.1 23.0 %copy-start.12 = (s32[1024]{0:T(1024)S(1)}, s32[1024]{0:T(1024)}, u32[]{:S(2)}) copy-start(s32[1024]{0:T(1024)} %param.12) | copy-start | bytes 12292
  3.1 67.1 %copy-start.5 = (bf16[128,1024]{1,0:T(8,128)(2,1)S(1)}, bf16[128,1024]{1,0:T(8,128)(2,1)}, u32[]{:S(2)}) copy-start(bf16[128,1024]{1,0:T(8,128)(2,1)} %param.15) | copy-start | bytes 786436
  3.1 67.4 %copy-start.6 = (bf16[128,1024]{1,0:T(8,128)(2,1)S(1)}, bf16[128,1024]{1,0:T(8,128)(2,1)}, u32[]{:S(2)}) copy-start(bf16[128,1024]{1,0:T(8,128)(2,1)} %param.18) | copy-start | bytes 786436
  3.1 76.4 %all-to-all-start = ((bf16[32,16,2048]{2,1,0:T(8,128)(2,1)}), bf16[32,16,2048]{2,1,0:T(8,128)(2,1)S(1)}, u32[]{:S(2)}, u32[]{:S(2)}) async-start(bf16[32,16,2048]{2,1,0:T(8,128)(2,1)} %broadcast_in_dim.75), calls=%async_computation | async-start | bytes 4194304 | tf_op jit(solution)/shard_map/all_to_all | solution.py:31
  17.6 53.3 %copy-start.13 = (s32[1024]{0:T(1024)S(1)}, s32[1024]{0:T(1024)}, u32[]{:S(2)}) copy-start(s32[1024]{0:T(1024)} %param.14) | copy-start | bytes 12292
  17.6 8.7 %copy-start.17 = (bf16[128]{0:T(256)(128)(2,1)}, bf16[128]{0:T(256)(128)(2,1)S(1)}, u32[]{:S(2)}) copy-start(bf16[128]{0:T(256)(128)(2,1)S(1)} %convert.25) | copy-start | bytes 772
  17.7 57.3 %collective-permute-start = (bf16[1,144,256]{2,1,0:T(8,128)(2,1)S(1)}, bf16[1,144,256]{2,1,0:T(8,128)(2,1)}, u32[]{:S(2)}, u32[]{:S(2)}) collective-permute-start(bf16[1,144,256]{2,1,0:T(8,128)(2,1)S(1)} %maximum_bitcast_fusion), channel_id=1, source_target_pairs={{0,16},{2,18},{4,20},{6,22},{8,24},{10,26},{12,28},{14,30},{16,32}... | collective-permute-start | bytes 221192 | tf_op jit(solution)/shard_map/ppermute | solution.py:47
  21.4 32.9 %collective-permute-start.1 = (bf16[1,144,256]{2,1,0:T(8,128)(2,1)S(1)}, bf16[1,144,256]{2,1,0:T(8,128)(2,1)S(1)}, u32[]{:S(2)}, u32[]{:S(2)}) collective-permute-start(bf16[1,144,256]{2,1,0:T(8,128)(2,1)S(1)} %maximum_bitcast_fusion), channel_id=1, source_target_pairs={{0,2},{2,4},{4,6},{6,8},{8,10},{10,12},{12,14},{14,16},{16,18},{18... | collective-permute-start | bytes 221192 | tf_op jit(solution)/shard_map/ppermute | solution.py:47
  55.0 16.7 %collective-permute-start.2 = (bf16[2,144,256]{2,1,0:T(8,128)(2,1)}, bf16[2,144,256]{2,1,0:T(8,128)(2,1)S(1)}, u32[]{:S(2)}, u32[]{:S(2)}) collective-permute-start(bf16[2,144,256]{2,1,0:T(8,128)(2,1)} %pad_maximum_fusion.4), channel_id=1, source_target_pairs={{0,4},{2,6},{4,8},{6,10},{8,12},{10,14},{12,16},{14,18},{16,20},{1... | collective-permute-start | bytes 442376 | tf_op jit(solution)/shard_map/ppermute | solution.py:47
  70.5 16.4 %copy-start.18 = (bf16[128]{0:T(256)(128)(2,1)S(1)}, bf16[128]{0:T(256)(128)(2,1)}, u32[]{:S(2)}) copy-start(bf16[128]{0:T(256)(128)(2,1)} %copy-done.17) | copy-start | bytes 772
  71.7 3.2 %copy-start.1 = (bf16[2,144,256]{2,1,0:T(8,128)(2,1)}, bf16[2,144,256]{2,1,0:T(8,128)(2,1)S(1)}, u32[]{:S(2)}) copy-start(bf16[2,144,256]{2,1,0:T(8,128)(2,1)S(1)} %collective-permute-done.2) | copy-start | bytes 442372
  71.8 6.8 %collective-permute-start.3 = (bf16[4,144,256]{2,1,0:T(8,128)(2,1)S(1)}, bf16[4,144,256]{2,1,0:T(8,128)(2,1)S(1)}, u32[]{:S(2)}, u32[]{:S(2)}) collective-permute-start(bf16[4,144,256]{2,1,0:T(8,128)(2,1)S(1)} %pad_maximum_fusion.3), channel_id=1, source_target_pairs={{0,8},{2,10},{4,12},{6,14},{8,16},{10,18},{12,20},{14,22},{16,24},... | collective-permute-start | bytes 884744 | tf_op jit(solution)/shard_map/ppermute | solution.py:47
  74.9 14.8 %copy-start.14 = (s32[128]{0:T(128)}, s32[128]{0:T(128)S(1)}, u32[]{:S(2)}) copy-start(s32[128]{0:T(128)S(1)} %iota_add_fusion.2) | copy-start | bytes 1540
  79.6 13.6 %collective-permute-start.4 = (bf16[512,2048]{1,0:T(8,128)(2,1)S(1)}, bf16[512,2048]{1,0:T(8,128)(2,1)S(1)}, u32[]{:S(2)}, u32[]{:S(2)}) collective-permute-start(bf16[512,2048]{1,0:T(8,128)(2,1)S(1)} %bitcast.141), channel_id=1, source_target_pairs={{0,2},{2,0},{4,6},{6,4},{8,10},{10,8},{12,14},{14,12},{16,18},{18,... | collective-permute-start | bytes 6291464 | tf_op jit(solution)/shard_map/ppermute | solution.py:25
  86.9 2.9 %copy-start.2 = (bf16[9,128,128]{2,1,0:T(8,128)(2,1)}, bf16[9,128,128]{2,1,0:T(8,128)(2,1)S(1)}, u32[]{:S(2)}) copy-start(bf16[9,128,128]{2,1,0:T(8,128)(2,1)S(1)} %get-tuple-element.43) | copy-start | bytes 884740
  88.6 2.2 copy-start.19
  95.8 26.8 %collective-permute-start.7 = (bf16[2,2,4,16,1024]{4,3,2,1,0:T(8,128)(2,1)S(1)}, bf16[2,2,4,16,1024]{4,3,2,1,0:T(8,128)(2,1)S(1)}, u32[]{:S(2)}, u32[]{:S(2)}) collective-permute-start(bf16[2,2,4,16,1024]{4,3,2,1,0:T(8,128)(2,1)S(1)} %pad_maximum_fusion.2), channel_id=1, source_target_pairs={{0,384},{128,0},{256,128},{384,256},{1,385},{129,1},{257,129},{385... | collective-permute-start | bytes 1572872 | tf_op jit(solution)/shard_map/ppermute | solution.py:51
  100.3 22.4 %collective-permute-start.6 = (bf16[2,2,4,16,1024]{4,3,2,1,0:T(8,128)(2,1)S(1)}, bf16[2,2,4,16,1024]{4,3,2,1,0:T(8,128)(2,1)S(1)}, u32[]{:S(2)}, u32[]{:S(2)}) collective-permute-start(bf16[2,2,4,16,1024]{4,3,2,1,0:T(8,128)(2,1)S(1)} %pad_maximum_fusion.1), channel_id=1, source_target_pairs={{0,256},{128,384},{256,0},{384,128},{1,257},{129,385},{257,1},{385... | collective-permute-start | bytes 1572872 | tf_op jit(solution)/shard_map/ppermute | solution.py:51
  102.8 26.0 %collective-permute-start.5 = (bf16[2,2,4,16,1024]{4,3,2,1,0:T(8,128)(2,1)S(1)}, bf16[2,2,4,16,1024]{4,3,2,1,0:T(8,128)(2,1)S(1)}, u32[]{:S(2)}, u32[]{:S(2)}) collective-permute-start(bf16[2,2,4,16,1024]{4,3,2,1,0:T(8,128)(2,1)S(1)} %pad_maximum_fusion), channel_id=1, source_target_pairs={{0,128},{128,256},{256,384},{384,0},{1,129},{129,257},{257,385},{3... | collective-permute-start | bytes 1572872 | tf_op jit(solution)/shard_map/ppermute | solution.py:51
  129.1 13.5 %copy-start.9 = (s32[1024]{0:T(1024)S(1)}, s32[1024]{0:T(1024)}, u32[]{:S(2)}) copy-start(s32[1024]{0:T(1024)} %iota_add_fusion.1) | copy-start | bytes 12292
  129.1 36.6 %copy-start.4 = (bf16[9,128,128]{2,1,0:T(8,128)(2,1)S(1)}, bf16[9,128,128]{2,1,0:T(8,128)(2,1)}, u32[]{:S(2)}) copy-start(bf16[9,128,128]{2,1,0:T(8,128)(2,1)} %get-tuple-element.42) | copy-start | bytes 884740
  129.1 13.3 %collective-permute-start.8 = (bf16[2,2,4,8,1024]{4,3,2,1,0:T(8,128)(2,1)S(1)}, bf16[2,2,4,8,1024]{4,3,2,1,0:T(8,128)(2,1)S(1)}, u32[]{:S(2)}, u32[]{:S(2)}) collective-permute-start(bf16[2,2,4,8,1024]{4,3,2,1,0:T(8,128)(2,1)S(1)} %fusion.19), channel_id=1, source_target_pairs={{0,1},{1,0},{2,3},{3,2},{4,5},{5,4},{6,7},{7,6},{8,9},{9,8},{10,11... | collective-permute-start | bytes 786440 | tf_op jit(solution)/shard_map/ppermute | solution.py:55
  143.7 33.1 %copy-start.16 = (f32[128]{0:T(128)S(1)}, f32[128]{0:T(128)}, u32[]{:S(2)}) copy-start(f32[128]{0:T(128)} %reshape.206) | copy-start | bytes 1540
  143.7 32.9 %all-to-all-start.1 = ((f32[64,3,128]{2,1,0:T(4,128)}), f32[64,3,128]{2,1,0:T(4,128)S(1)}, u32[]{:S(2)}, u32[]{:S(2)}) async-start(f32[64,3,128]{2,1,0:T(4,128)} %broadcast_in_dim.79), calls=%async_computation.1 | async-start | bytes 262144 | tf_op jit(solution)/shard_map/all_to_all | solution.py:151
  177.4 12.6 %all-to-all-start.2 = ((f32[8,1,128]{2,1,0:T(1,128)}), f32[8,1,128]{2,1,0:T(1,128)S(1)}, u32[]{:S(2)}, u32[]{:S(2)}) async-start(f32[8,1,128]{2,1,0:T(1,128)} %broadcast_in_dim.80), calls=%async_computation.2 | async-start | bytes 8192 | tf_op jit(solution)/shard_map/all_to_all | solution.py:160
  181.2 8.8 %copy-start.10 = (s32[1024]{0:T(1024)S(1)}, s32[1024]{0:T(1024)}, u32[]{:S(2)}) copy-start(s32[1024]{0:T(1024)} %eq.55) | copy-start | bytes 12292
  181.2 8.8 %copy-start.15 = (s32[128]{0:T(128)S(1)}, s32[128]{0:T(128)}, u32[]{:S(2)}) copy-start(s32[128]{0:T(128)} %copy-done.14) | copy-start | bytes 1540
  190.2 1.7 copy-start
  192.8 7.6 %copy-start.3 = (bf16[9,128,128]{2,1,0:T(8,128)(2,1)S(1)}, bf16[9,128,128]{2,1,0:T(8,128)(2,1)}, u32[]{:S(2)}) copy-start(bf16[9,128,128]{2,1,0:T(8,128)(2,1)} %copy-done.2) | copy-start | bytes 884740
  193.8 19.7 %all-to-all-start.3 = ((bf16[8,128,256]{1,2,0:T(8,128)(2,1)}), bf16[8,128,256]{1,2,0:T(8,128)(2,1)S(1)}, u32[]{:S(2)}, u32[]{:S(2)}) async-start(bf16[8,128,256]{1,2,0:T(8,128)(2,1)} %fusion.17), calls=%async_computation.3 | async-start | bytes 1048576 | tf_op jit(solution)/shard_map/all_to_all | solution.py:37
  213.9 5.0 %collective-permute-start.9 = (bf16[128,256]{0,1:T(8,128)(2,1)S(1)}, bf16[128,256]{0,1:T(8,128)(2,1)S(1)}, u32[]{:S(2)}, u32[]{:S(2)}) collective-permute-start(bf16[128,256]{0,1:T(8,128)(2,1)S(1)} %fusion.38), channel_id=1, source_target_pairs={{16,0},{18,2},{20,4},{22,6},{24,8},{26,10},{28,12},{30,14},{32,16}... | collective-permute-start | bytes 196616 | tf_op jit(solution)/shard_map/ppermute | solution.py:47

commit v3 on v2

--- a/solution.py
+++ b/solution.py
@@ -1,6 +1,10 @@
+import functools
+
 import jax
 import jax.numpy as jnp
 from jax import lax
+from jax.experimental import pallas as pl
+from jax.experimental.pallas import tpu as pltpu
 from jax.sharding import PartitionSpec as P
 
 advantage_scale = 0.1
@@ -25,9 +29,12 @@
     return lax.ppermute(block, "ctx", route)
 
 
-def across_chips(block):
+def copies_for_chips(block):
+    return jnp.broadcast_to(block, (Z * Y,) + block.shape)
+
+
+def across_chips(copies):
     groups = [[chip * CORES + core for chip in range(Z * Y)] for core in range(CORES)]
-    copies = jnp.broadcast_to(block, (Z * Y,) + block.shape)
     return lax.all_to_all(copies, "ctx", 0, 0, axis_index_groups=groups)
 
 
@@ -55,33 +62,57 @@
     return lax.ppermute(block, "tp", [(0, 1), (1, 0)])
 
 
+def logits_kernel(section_ref, mine_ref, theirs_ref, head_ref, *refs):
+    outs, logits = refs[:SECTIONS], refs[SECTIONS]
+    count = outs[0].shape[1]
+    for part, rows in enumerate((mine_ref, theirs_ref)):
+        logits[part] = jnp.dot(rows[...], head_ref[...], preferred_element_type=jnp.float32)
+        for step, out in enumerate(outs):
+            place = lax.rem(section_ref[0] + step, SECTIONS)
+            kept = logits[part, pl.ds(pl.multiple_of(place * count, count), count), :]
+            out[part] = kept.astype(out.dtype)
+
+
 def section_parts(gathered, weight, section):
     mine = gathered.reshape(-1, gathered.shape[2])
-    parts = []
-    for rows in (mine, other_core(mine)):
-        part = jnp.dot(rows, weight, preferred_element_type=jnp.float32)
-        parts.append(part.reshape(SECTIONS, 2, Y, PIECE, weight.shape[1]))
-
-    def rows_for(step):
-        place = lax.rem(section + step, SECTIONS)
-        return jnp.stack(
-            [lax.dynamic_index_in_dim(part, place, 0, keepdims=False) for part in parts]
-        )
-
-    return [rows_for(0)] + [rows_for(step).astype(jnp.bfloat16) for step in (1, 2, 3)]
-
-
-def section_sums(parts):
-    total = parts[0]
-    for step in (1, 2, 3):
-        total = total + along_section(parts[step], step).astype(jnp.float32)
-    return total
+    rows, depth = mine.shape
+    vocab, tile = weight.shape[1], 256
+    count = rows // SECTIONS
+    whole = pl.BlockSpec((rows, depth), lambda n: (0, 0))
+    kinds = [jnp.float32] + [jnp.bfloat16] * (SECTIONS - 1)
+    return pl.pallas_call(
+        logits_kernel,
+        grid=(vocab // tile,),
+        in_specs=[
+            pl.BlockSpec(memory_space=pltpu.SMEM),
+            whole,
+            whole,
+            pl.BlockSpec((depth, tile), lambda n: (0, n)),
+        ],
+        out_specs=[pl.BlockSpec((2, count, tile), lambda n: (0, 0, n))] * SECTIONS,
+        out_shape=[jax.ShapeDtypeStruct((2, count, vocab), kind) for kind in kinds],
+        scratch_shapes=[pltpu.VMEM((2, rows, tile), jnp.float32)],
+        compiler_params=pltpu.CompilerParams(vmem_limit_bytes=24 * 1024 * 1024),
+        cost_estimate=pl.CostEstimate(
+            flops=4 * rows * depth * vocab,
+            bytes_accessed=2 * depth * vocab + 4 * rows * depth + 5 * rows * vocab,
+            transcendentals=0,
+        ),
+    )(jnp.reshape(section, (1,)), mine, other_core(mine), weight)
+
+
+def section_arrivals(parts):
+    return [along_section(parts[step], step) for step in (1, 2, 3)]
+
+
+def section_sums(own, arrivals):
+    return functools.reduce(lambda total, part: total + part.astype(jnp.float32), arrivals, own)
 
 
 def tp_halves(total, tp):
-    halves = total.reshape(total.shape[:3] + (TPS, PIECE // TPS) + total.shape[4:])
-    keep = lax.dynamic_index_in_dim(halves, tp, 3, keepdims=False)
-    give = lax.dynamic_index_in_dim(halves, 1 - tp, 3, keepdims=False)
+    halves = total.reshape(2, TPS, -1, total.shape[2])
+    keep = lax.dynamic_index_in_dim(halves, tp, 1, keepdims=False)
+    give = lax.dynamic_index_in_dim(halves, 1 - tp, 1, keepdims=False)
     return keep, give.astype(jnp.bfloat16)
 
 
@@ -100,18 +131,15 @@
     return jnp.where(core == 1, jnp.flip(array, axis), array)
 
 
-def key_value_window(keys, values, segment_ids):
+def packed_window(keys, values, segment_ids):
     id_row = jnp.concatenate([segment_ids, jnp.zeros_like(segment_ids)])[None, :]
-    own = jnp.concatenate(
+    return jnp.concatenate(
         [
             jnp.concatenate([keys, values], axis=1),
             jnp.broadcast_to(id_row.astype(jnp.bfloat16), (16, 2 * keys.shape[1])),
         ],
         axis=0,
     )[None]
-    two = jnp.concatenate([passed_along(own, 1), own], axis=0)
-    four = jnp.concatenate([passed_along(two, 2), two], axis=0)
-    return jnp.concatenate([passed_along(own, 8), passed_along(four, 4), four], axis=0)
 
 
 def body(
@@ -131,20 +159,39 @@
     tp = lax.axis_index("tp")
     place, core = lax.rem(ctx_index, Y * CORES), lax.rem(ctx_index, CORES)
 
-    gathered = across_chips(teacher_hidden)
-    window = key_value_window(keys, values, segment_ids)
-    gathered, window = lax.optimization_barrier((gathered, window))
-    logits = tp_sums(*tp_halves(section_sums(section_parts(gathered, lm_head, section)), tp))
-
-    def kept(array, axis):
+    half = teacher_hidden.shape[0] // 2
+    first = across_chips(copies_for_chips(teacher_hidden[:half]))
+    copies = copies_for_chips(teacher_hidden[half:])
+    own_window = packed_window(keys, values, segment_ids)
+    eighth = passed_along(own_window, 8)
+    two_windows = jnp.concatenate([passed_along(own_window, 1), own_window], axis=0)
+    first, copies, eighth, two_windows = lax.optimization_barrier(
+        (first, copies, eighth, two_windows)
+    )
+    last = across_chips(copies)
+    first = section_parts(first, lm_head, section)
+    arrivals = section_arrivals(first)
+    arrivals[2], two_windows = lax.optimization_barrier((arrivals[2], two_windows))
+    four_windows = jnp.concatenate([passed_along(two_windows, 2), two_windows], axis=0)
+    first, last = lax.optimization_barrier((section_sums(first[0], arrivals), last))
+    keep, give = tp_halves(first, tp)
+    last = section_parts(last, lm_head, section)
+    give, last = lax.optimization_barrier((give, last))
+    arrivals = section_arrivals(last)
+    first = tp_sums(keep, give)
+    last, four_windows = lax.optimization_barrier((section_sums(last[0], arrivals), four_windows))
+    last = tp_sums(*tp_halves(last, tp))
+    window = jnp.concatenate([eighth, passed_along(four_windows, 4), four_windows], axis=0)
+
+    def kept_rows(array):
+        rows = array.reshape(SECTIONS * TPS, Y, CORES, 2, half)
         return lax.dynamic_index_in_dim(
-            lax.dynamic_index_in_dim(array, section, 0, keepdims=False), tp, axis, keepdims=False
-        )
-
-    def kept_rows(array):
-        rows = kept(array.reshape(SECTIONS, 2, Y, CORES, TPS, PIECE // TPS), 3)
-        return rows.transpose(2, 0, 1, 3)
-
+            rows, section * TPS + tp, 0, keepdims=False
+        ).transpose(1, 0, 2, 3)
+
+    logits = jnp.stack(
+        [part.reshape(CORES, Y, half, -1) for part in (first, last)], axis=2
+    )
     columns = ctx_index * lm_head.shape[1] + jnp.arange(lm_head.shape[1], dtype=jnp.int32)
     stats = row_stats(logits, columns, cores_exchanged(kept_rows(sampled_ids), 0, core))
     stats = cores_exchanged(stats, 1, core).reshape(3, -1)
@@ -160,10 +207,8 @@
     everything = lax.all_to_all(
         jnp.broadcast_to(advantage, (count,) + advantage.shape), ("section", "tp"), 0, 0
     )
-    owners = owner_map.reshape(SECTIONS, 2, Y, CORES, TPS, PIECE // TPS)
-    owners = owners.transpose(0, 4, 3, 1, 2, 5).reshape(-1)
-    advantage_own = everything.reshape(SECTIONS, TPS, CORES, 2, Y, PIECE // TPS)
-    advantage_own = kept(advantage_own, 2).transpose(2, 1, 0, 3).reshape(-1)
+    owners = owner_map.reshape(SECTIONS * TPS, Y, CORES, PIECE).transpose(0, 2, 1, 3).reshape(-1)
+    advantage_own = advantage.reshape(CORES, Y, PIECE).transpose(1, 0, 2).reshape(-1)
     everything = everything.reshape(-1)
 
     seq_rows = queries.shape[0]
@@ -219,21 +264,23 @@
     both = jnp.concatenate([grad_key, grad_value], axis=1).reshape(
         FARTHEST + 1, seq_rows, 2 * head_dim
     )
-    cyclic = both[1:].astype(jnp.bfloat16)
-    cyclic = jnp.concatenate([cyclic, cyclic], axis=0)
-    given = lax.dynamic_slice_in_dim(cyclic, Y * CORES - 1 - place, Y * CORES, 0)
-    arrived = across_row(given).astype(jnp.float32)
-    sender = jnp.arange(Y * CORES, dtype=jnp.int32)[:, None, None]
-    back = both[0] + jnp.sum(jnp.where(sender < place, arrived, 0.0), axis=0)
-    back = passed_along(back.astype(jnp.bfloat16), -Y * CORES).astype(jnp.float32)
-    total = both[FARTHEST] + jnp.sum(jnp.where(sender > place, arrived, 0.0), axis=0) + back
-    total = total.astype(jnp.bfloat16)
     d_queries = (
         grad_query.reshape(group, seq_rows, head_dim)
         .transpose(1, 0, 2)
         .reshape(seq_rows, group * head_dim)
     )
-    return (advantage_own, d_queries, total[:, :head_dim], total[:, head_dim:])
+    cyclic = both[1:].astype(jnp.bfloat16)
+    cyclic = jnp.concatenate([cyclic, cyclic], axis=0)
+    given = lax.dynamic_slice_in_dim(cyclic, Y * CORES - 1 - place, Y * CORES, 0)
+    arrived, d_queries = lax.optimization_barrier((across_row(given), d_queries))
+    arrived = arrived.astype(jnp.float32)
+    sender = jnp.arange(Y * CORES, dtype=jnp.int32)[:, None, None]
+    back = both[0] + jnp.sum(jnp.where(sender < place, arrived, 0.0), axis=0)
+    back = passed_along(back.astype(jnp.bfloat16), -Y * CORES).astype(jnp.float32)
+    here = both[FARTHEST] + jnp.sum(jnp.where(sender > place, arrived, 0.0), axis=0)
+    d_keys = (here[:, :head_dim] + back[:, :head_dim]).astype(jnp.bfloat16)
+    d_values = (here[:, head_dim:] + back[:, head_dim:]).astype(jnp.bfloat16)
+    return (advantage_own, d_queries, d_keys, d_values)
 
 
 def solution(mesh):

time: 221 us -> 212 us (0.959)
  waiting for transfers between devices: 89.3 us -> 58.3 us
  local copies, waits for them, and re-layouts: 15.6 us -> 23.2 us
  Pallas kernels: 0 us -> 7.46 us
  other arithmetic: 8.45 us -> 14.6 us
  matrix products: 12.6 us -> 10 us
    ppermute x5, waiting for transfers between devices: 32.7 us -> 17.3 us  [passed_along(): return lax.ppermute(block, 'ctx', route)]
    all_to_all x1, starting transfers between devices: 22.1 us -> 9.68 us  [body(): lax.all_to_all(jnp.broadcast_to(stats, (Z * Y * CORES,) + stats.shape), '...]
    ppermute x3 -> x6, waiting for transfers between devices: 22.1 us -> 12.3 us  [along_section(): lax.ppermute(block, 'section', [(s, (s + step) % SECTIONS) for s in range...]
    all_to_all x1 -> x2, starting transfers between devices: 14.4 us -> 22.9 us  [across_chips(): return lax.all_to_all(copies, 'ctx', 0, 0, axis_index_groups=groups)]
    ppermute x5, starting transfers between devices: 26.6 us -> 19 us  [passed_along(): return lax.ppermute(block, 'ctx', route)]
    pallas_call x0 -> x2, Pallas kernels: none -> 7.46 us  [section_parts(): pl.pallas_call(logits_kernel, grid=(vocab // tile,), in_specs=[pl.BlockSp...]
    ppermute x3 -> x6, starting transfers between devices: 9.33 us -> 16.7 us  [along_section(): lax.ppermute(block, 'section', [(s, (s + step) % SECTIONS) for s in range...]
    all_to_all x1, waiting for transfers between devices: 10.2 us -> 3.32 us  [body(): lax.all_to_all(jnp.broadcast_to(stats, (Z * Y * CORES,) + stats.shape), '...]
  transfers between devices with their start and end apart: 14 -> 20, of which waited for: 9 -> 11; matrix products, arithmetic and copies ran while one was open for 10% -> 16% of each run, Pallas kernels for 0% -> 4%
where the time goes in v3:
time: 212 us; the launch traced here: 210 us
  starting transfers between devices  95.2 us (45%)
  waiting for transfers between devices  58.3 us (28%)
  local copies, waits for them, and re-layouts  23.2 us (11%)
  other arithmetic  14.6 us (7%)
  matrix products  10 us (5%)
  Pallas kernels  7.46 us (4%)
    all_to_all x2, starting transfers between devices, across_chips(): return lax.all_to_all(copies, 'ctx', 0, 0, axis_index_groups=groups)  22.9 us
    ppermute x5, starting transfers between devices, passed_along(): return lax.ppermute(block, 'ctx', route)  19 us
    ppermute x5, waiting for transfers between devices, passed_along(): return lax.ppermute(block, 'ctx', route)  17.3 us
    ppermute x6, starting transfers between devices, along_section(): lax.ppermute(block, 'section', [(s, (s + step) % SECTIONS) for s in range...  16.7 us
    ppermute x6, waiting for transfers between devices, along_section(): lax.ppermute(block, 'section', [(s, (s + step) % SECTIONS) for s in range...  12.3 us
    all_to_all x1, waiting for transfers between devices, across_row(): return lax.all_to_all(blocks, 'ctx', 0, 0, axis_index_groups=groups)  11 us
    unnamed x48, local copies, waits for them, and re-layouts  10.8 us
    all_to_all x1, starting transfers between devices, body(): lax.all_to_all(jnp.broadcast_to(stats, (Z * Y * CORES,) + stats.shape), '...  9.68 us
  transfers between devices with their start and end apart: 20, of which 11 were waited for; matrix products, arithmetic and copies ran while one was open for 16% of the time, Pallas kernels for 4%

profile of v3, /device:TPU:1, one launch (start us, length us, event | category | flops | bytes accessed | tf_op | source)
XLA Modules:
  0.0 210.1 jit_solution(4419471482079946092)
XLA Ops:
  0.6 0.8 fusion.42
  1.4 1.1 broadcast_in_dim.78
  2.5 14.3 %all-to-all-start = ((bf16[32,8,2048]{2,1,0:T(8,128)(2,1)}), bf16[32,8,2048]{2,1,0:T(8,128)(2,1)S(1)}, u32[]{:S(2)}, u32[]{:S(2)}) async-start(bf16[32,8,2048]{2,1,0:T(8,128)(2,1)} %broadcast_in_dim.78), calls=%async_computation | async-start | bytes 2097152 | tf_op jit(solution)/shard_map/all_to_all | solution.py:38
  16.8 0.7 convert.7
  18.0 0.8 maximum_bitcast_fusion
  18.8 4.3 %collective-permute-start.1 = (bf16[1,144,256]{2,1,0:T(8,128)(2,1)S(1)}, bf16[1,144,256]{2,1,0:T(8,128)(2,1)S(1)}, u32[]{:S(2)}, u32[]{:S(2)}) collective-permute-start(bf16[1,144,256]{2,1,0:T(8,128)(2,1)S(1)} %maximum_bitcast_fusion), channel_id=1, source_target_pairs={{0,2},{2,4},{4,6},{6,8},{8,10},{10,12},{12,14},{14,16},{16,18},{18... | collective-permute-start | bytes 221192 | tf_op jit(solution)/shard_map/ppermute | solution.py:54
  23.1 3.1 %collective-permute-start = (bf16[1,144,256]{2,1,0:T(8,128)(2,1)S(1)}, bf16[1,144,256]{2,1,0:T(8,128)(2,1)S(1)}, u32[]{:S(2)}, u32[]{:S(2)}) collective-permute-start(bf16[1,144,256]{2,1,0:T(8,128)(2,1)S(1)} %maximum_bitcast_fusion), channel_id=1, source_target_pairs={{0,16},{2,18},{4,20},{6,22},{8,24},{10,26},{12,28},{14,30},{16,32}... | collective-permute-start | bytes 221192 | tf_op jit(solution)/shard_map/ppermute | solution.py:54
  26.2 8.4 %collective-permute-done.1 = bf16[1,144,256]{2,1,0:T(8,128)(2,1)S(1)} collective-permute-done((bf16[1,144,256]{2,1,0:T(8,128)(2,1)S(1)}, bf16[1,144,256]{2,1,0:T(8,128)(2,1)S(1)}, u32[]{:S(2)}, u32[]{:S(2)}) %collective-permute-start.1) | collective-permute-done | bytes 73760 | tf_op jit(solution)/shard_map/ppermute | solution.py:54
  34.6 5.8 %collective-permute-done = bf16[1,144,256]{2,1,0:T(8,128)(2,1)S(1)} collective-permute-done((bf16[1,144,256]{2,1,0:T(8,128)(2,1)S(1)}, bf16[1,144,256]{2,1,0:T(8,128)(2,1)S(1)}, u32[]{:S(2)}, u32[]{:S(2)}) %collective-permute-start) | collective-permute-done | bytes 73760 | tf_op jit(solution)/shard_map/ppermute | solution.py:54
  40.4 2.5 %all-to-all-done = bf16[32,8,2048]{2,1,0:T(8,128)(2,1)S(1)} async-done(((bf16[32,8,2048]{2,1,0:T(8,128)(2,1)}), bf16[32,8,2048]{2,1,0:T(8,128)(2,1)S(1)}, u32[]{:S(2)}, u32[]{:S(2)}) %all-to-all-start) | async-done | bytes 1048608 | tf_op jit(solution)/shard_map/all_to_all | solution.py:38
  42.9 1.1 broadcast_in_dim.79
  44.0 8.6 %all-to-all-start.1 = ((bf16[32,8,2048]{2,1,0:T(8,128)(2,1)}), bf16[32,8,2048]{2,1,0:T(8,128)(2,1)S(1)}, u32[]{:S(2)}, u32[]{:S(2)}) async-start(bf16[32,8,2048]{2,1,0:T(8,128)(2,1)} %broadcast_in_dim.79), calls=%async_computation.1 | async-start | bytes 2097152 | tf_op jit(solution)/shard_map/all_to_all | solution.py:38
  52.6 3.1 %collective-permute-start.2 = (bf16[256,2048]{1,0:T(8,128)(2,1)S(1)}, bf16[256,2048]{1,0:T(8,128)(2,1)S(1)}, u32[]{:S(2)}, u32[]{:S(2)}) collective-permute-start(bf16[256,2048]{1,0:T(8,128)(2,1)S(1)} %bitcast.139), channel_id=1, source_target_pairs={{0,2},{2,0},{4,6},{6,4},{8,10},{10,8},{12,14},{14,12},{16,18},{18,... | collective-permute-start | bytes 3145736 | tf_op jit(solution)/shard_map/ppermute | solution.py:29
  55.7 2.3 %collective-permute-done.2.theirs_ref = bf16[256,2048]{1,0:T(8,128)(2,1)S(1)} collective-permute-done((bf16[256,2048]{1,0:T(8,128)(2,1)S(1)}, bf16[256,2048]{1,0:T(8,128)(2,1)S(1)}, u32[]{:S(2)}, u32[]{:S(2)}) %collective-permute-start.2) | collective-permute-done | bytes 1048608 | tf_op jit(solution)/shard_map/ppermute | solution.py:29
  58.0 2.2 %copy-done = bf16[2048,1024]{1,0:T(8,128)(2,1)S(1)} copy-done((bf16[2048,1024]{1,0:T(8,128)(2,1)S(1)}, bf16[2048,1024]{1,0:T(8,128)(2,1)}, u32[]{:S(2)}) %copy-start) | copy-done | bytes 4194328
  60.2 3.7 %shard_map.129 = (f32[2,64,1024]{2,1,0:T(8,128)S(1)}, bf16[2,64,1024]{2,1,0:T(8,128)(2,1)S(1)}, bf16[2,64,1024]{2,1,0:T(8,128)(2,1)S(1)}, bf16[2,64,1024]{2,1,0:T(8,128)(2,1)S(1)}) custom-call(s32[1]{0:T(128)} %bitcast.section_ref, bf16[256,2048]{1,0:T(8,128)(2,1)S(1)} %bitcast.140, bf16[256,2048]{1,0:T(8,128)(2,1)S(1)} %collective-permute-done.2.theirs_ref, ...), custom_call_target="tpu_custom_call" | custom-call | flops 2147483648 | bytes 7602176 | tf_op jit(solution)/shard_map/pallas_call | solution.py:83
  63.9 4.4 %collective-permute-start.5 = (bf16[2,64,1024]{2,1,0:T(8,128)(2,1)S(1)}, bf16[2,64,1024]{2,1,0:T(8,128)(2,1)S(1)}, u32[]{:S(2)}, u32[]{:S(2)}) collective-permute-start(bf16[2,64,1024]{2,1,0:T(8,128)(2,1)S(1)} %get-tuple-element.33), channel_id=1, source_target_pairs={{0,384},{128,0},{256,128},{384,256},{1,385},{129,1},{257,129},{385... | collective-permute-start | bytes 786440 | tf_op jit(solution)/shard_map/ppermute | solution.py:58
  68.3 2.4 %collective-permute-start.4 = (bf16[2,64,1024]{2,1,0:T(8,128)(2,1)S(1)}, bf16[2,64,1024]{2,1,0:T(8,128)(2,1)S(1)}, u32[]{:S(2)}, u32[]{:S(2)}) collective-permute-start(bf16[2,64,1024]{2,1,0:T(8,128)(2,1)S(1)} %get-tuple-element.32), channel_id=1, source_target_pairs={{0,256},{128,384},{256,0},{384,128},{1,257},{129,385},{257,1},{385... | collective-permute-start | bytes 786440 | tf_op jit(solution)/shard_map/ppermute | solution.py:58
  70.7 2.5 %collective-permute-start.3 = (bf16[2,64,1024]{2,1,0:T(8,128)(2,1)S(1)}, bf16[2,64,1024]{2,1,0:T(8,128)(2,1)S(1)}, u32[]{:S(2)}, u32[]{:S(2)}) collective-permute-start(bf16[2,64,1024]{2,1,0:T(8,128)(2,1)S(1)} %get-tuple-element.31), channel_id=1, source_target_pairs={{0,128},{128,256},{256,384},{384,0},{1,129},{129,257},{257,385},{3... | collective-permute-start | bytes 786440 | tf_op jit(solution)/shard_map/ppermute | solution.py:58
  73.3 5.8 %collective-permute-done.5 = bf16[2,64,1024]{2,1,0:T(8,128)(2,1)S(1)} collective-permute-done((bf16[2,64,1024]{2,1,0:T(8,128)(2,1)S(1)}, bf16[2,64,1024]{2,1,0:T(8,128)(2,1)S(1)}, u32[]{:S(2)}, u32[]{:S(2)}) %collective-permute-start.5) | collective-permute-done | bytes 262176 | tf_op jit(solution)/shard_map/ppermute | solution.py:58
  79.1 6.5 %collective-permute-done.3 = bf16[2,64,1024]{2,1,0:T(8,128)(2,1)S(1)} collective-permute-done((bf16[2,64,1024]{2,1,0:T(8,128)(2,1)S(1)}, bf16[2,64,1024]{2,1,0:T(8,128)(2,1)S(1)}, u32[]{:S(2)}, u32[]{:S(2)}) %collective-permute-start.3) | collective-permute-done | bytes 262176 | tf_op jit(solution)/shard_map/ppermute | solution.py:58
  85.7 2.4 %collective-permute-start.6 = (bf16[256,2048]{1,0:T(8,128)(2,1)S(1)}, bf16[256,2048]{1,0:T(8,128)(2,1)S(1)}, u32[]{:S(2)}, u32[]{:S(2)}) collective-permute-start(bf16[256,2048]{1,0:T(8,128)(2,1)S(1)} %bitcast.137), channel_id=1, source_target_pairs={{0,2},{2,0},{4,6},{6,4},{8,10},{10,8},{12,14},{14,12},{16,18},{18,... | collective-permute-start | bytes 3145736 | tf_op jit(solution)/shard_map/ppermute | solution.py:29
  91.4 4.1 %collective-permute-start.11 = (bf16[2,144,256]{2,1,0:T(8,128)(2,1)S(1)}, bf16[2,144,256]{2,1,0:T(8,128)(2,1)}, u32[]{:S(2)}, u32[]{:S(2)}) collective-permute-start(bf16[2,144,256]{2,1,0:T(8,128)(2,1)S(1)} %pad_maximum_fusion.2), channel_id=1, source_target_pairs={{0,4},{2,6},{4,8},{6,10},{8,12},{10,14},{12,16},{14,18},{16,20},{1... | collective-permute-start | bytes 442376 | tf_op jit(solution)/shard_map/ppermute | solution.py:54
  95.5 0.7 fusion.30
  96.2 2.2 %copy-done.1 = bf16[2048,1024]{1,0:T(8,128)(2,1)S(1)} copy-done((bf16[2048,1024]{1,0:T(8,128)(2,1)S(1)}, bf16[2048,1024]{1,0:T(8,128)(2,1)}, u32[]{:S(2)}) %copy-start.1) | copy-done | bytes 4194328
  98.4 3.7 %shard_map.130 = (f32[2,64,1024]{2,1,0:T(8,128)S(1)}, bf16[2,64,1024]{2,1,0:T(8,128)(2,1)S(1)}, bf16[2,64,1024]{2,1,0:T(8,128)(2,1)S(1)}, bf16[2,64,1024]{2,1,0:T(8,128)(2,1)S(1)}) custom-call(s32[1]{0:T(128)} %bitcast.section_ref, bf16[256,2048]{1,0:T(8,128)(2,1)S(1)} %bitcast.138, bf16[256,2048]{1,0:T(8,128)(2,1)S(1)} %collective-permute-done.6.theirs_ref, ...), custom_call_target="tpu_custom_call" | custom-call | flops 2147483648 | bytes 7602176 | tf_op jit(solution)/shard_map/pallas_call | solution.py:83
  102.1 2.4 %collective-permute-start.10 = (bf16[2,64,1024]{2,1,0:T(8,128)(2,1)S(1)}, bf16[2,64,1024]{2,1,0:T(8,128)(2,1)}, u32[]{:S(2)}, u32[]{:S(2)}) collective-permute-start(bf16[2,64,1024]{2,1,0:T(8,128)(2,1)S(1)} %get-tuple-element.47), channel_id=1, source_target_pairs={{0,384},{128,0},{256,128},{384,256},{1,385},{129,1},{257,129},{385... | collective-permute-start | bytes 786440 | tf_op jit(solution)/shard_map/ppermute | solution.py:58
  104.5 2.4 %collective-permute-start.9 = (bf16[2,64,1024]{2,1,0:T(8,128)(2,1)S(1)}, bf16[2,64,1024]{2,1,0:T(8,128)(2,1)}, u32[]{:S(2)}, u32[]{:S(2)}) collective-permute-start(bf16[2,64,1024]{2,1,0:T(8,128)(2,1)S(1)} %get-tuple-element.46), channel_id=1, source_target_pairs={{0,256},{128,384},{256,0},{384,128},{1,257},{129,385},{257,1},{385... | collective-permute-start | bytes 786440 | tf_op jit(solution)/shard_map/ppermute | solution.py:58
  106.9 2.6 %collective-permute-start.8 = (bf16[2,64,1024]{2,1,0:T(8,128)(2,1)S(1)}, bf16[2,64,1024]{2,1,0:T(8,128)(2,1)}, u32[]{:S(2)}, u32[]{:S(2)}) collective-permute-start(bf16[2,64,1024]{2,1,0:T(8,128)(2,1)S(1)} %get-tuple-element.45), channel_id=1, source_target_pairs={{0,128},{128,256},{256,384},{384,0},{1,129},{129,257},{257,385},{3... | collective-permute-start | bytes 786440 | tf_op jit(solution)/shard_map/ppermute | solution.py:58
  110.1 0.7 copy.95
  111.4 1.3 copy.86
  112.7 1.0 copy.107
  113.9 0.8 reshape.221
  114.8 0.7 eq.59
  115.4 1.0 copy.109
  116.7 1.6 constant_dynamic-update-slice_fusion.2
  118.3 0.9 pad_maximum_fusion.1
  119.2 4.8 %collective-permute-start.7 = (bf16[2,32,1024]{2,1,0:T(8,128)(2,1)}, bf16[2,32,1024]{2,1,0:T(8,128)(2,1)S(1)}, u32[]{:S(2)}, u32[]{:S(2)}) collective-permute-start(bf16[2,32,1024]{2,1,0:T(8,128)(2,1)} %fusion.30), channel_id=1, source_target_pairs={{0,1},{1,0},{2,3},{3,2},{4,5},{5,4},{6,7},{7,6},{8,9},{9,8},{10,11... | collective-permute-start | bytes 393224 | tf_op jit(solution)/shard_map/ppermute | solution.py:62
  124.0 1.3 convert_add_fusion
  125.4 4.4 %collective-permute-start.12 = (bf16[2,32,1024]{2,1,0:T(8,128)(2,1)S(1)}, bf16[2,32,1024]{2,1,0:T(8,128)(2,1)S(1)}, u32[]{:S(2)}, u32[]{:S(2)}) collective-permute-start(bf16[2,32,1024]{2,1,0:T(8,128)(2,1)S(1)} %fusion.31), channel_id=1, source_target_pairs={{0,1},{1,0},{2,3},{3,2},{4,5},{5,4},{6,7},{7,6},{8,9},{9,8},{10,11... | collective-permute-start | bytes 393224 | tf_op jit(solution)/shard_map/ppermute | solution.py:62
  129.9 6.3 %collective-permute-start.13 = (bf16[4,144,256]{2,1,0:T(8,128)(2,1)S(1)}, bf16[4,144,256]{2,1,0:T(8,128)(2,1)S(1)}, u32[]{:S(2)}, u32[]{:S(2)}) collective-permute-start(bf16[4,144,256]{2,1,0:T(8,128)(2,1)S(1)} %pad_maximum_fusion.1), channel_id=1, source_target_pairs={{0,8},{2,10},{4,12},{6,14},{8,16},{10,18},{12,20},{14,22},{16,24},... | collective-permute-start | bytes 884744 | tf_op jit(solution)/shard_map/ppermute | solution.py:54
  136.2 4.0 %collective-permute-done.12 = bf16[2,32,1024]{2,1,0:T(8,128)(2,1)S(1)} collective-permute-done((bf16[2,32,1024]{2,1,0:T(8,128)(2,1)S(1)}, bf16[2,32,1024]{2,1,0:T(8,128)(2,1)S(1)}, u32[]{:S(2)}, u32[]{:S(2)}) %collective-permute-start.12) | collective-permute-done | bytes 131104 | tf_op jit(solution)/shard_map/ppermute | solution.py:62
  140.3 1.0 exponential_reduce_fusion
  141.5 0.7 broadcast_in_dim.83
  142.2 9.7 %all-to-all-start.2 = ((f32[64,3,128]{2,1,0:T(4,128)}), f32[64,3,128]{2,1,0:T(4,128)S(1)}, u32[]{:S(2)}, u32[]{:S(2)}) async-start(f32[64,3,128]{2,1,0:T(4,128)} %broadcast_in_dim.83), calls=%async_computation.2 | async-start | bytes 262144 | tf_op jit(solution)/shard_map/all_to_all | solution.py:198
  152.1 2.1 %and_and_fusion = pred[128,1152]{0,1:T(8,128)(4,1)S(1)} fusion(s32[128]{0:T(128)} %iota_add_fusion.2, s32[1152]{0:T(1024)} %iota_add_fusion, pred[1152]{0:T(1024)(128)(4,1)} %broadcast_compare_fusion, bf16[128]{0:T(256)(128)(2,1)} %copy-done.19, bf16[1152]{0:T(1024)(128)(2,1)S(1)} %bitcast.170), kind=kLoop, calls=%fused_computation.28 | loop fusion | flops 884736 | bytes 156288 | tf_op jit(solution)/shard_map/and | solution.py:231
  154.8 1.1 fusion.2
  156.0 1.3 fusion.3
  157.3 1.4 divide_convert_fusion
  159.4 3.3 %all-to-all-done.2 = f32[64,3,128]{2,1,0:T(4,128)S(1)} async-done(((f32[64,3,128]{2,1,0:T(4,128)}), f32[64,3,128]{2,1,0:T(4,128)S(1)}, u32[]{:S(2)}, u32[]{:S(2)}) %all-to-all-start.2) | async-done | bytes 98336 | tf_op jit(solution)/shard_map/all_to_all | solution.py:198
  163.4 7.1 %all-to-all-start.3 = ((f32[8,1,128]{2,1,0:T(1,128)}), f32[8,1,128]{2,1,0:T(1,128)S(1)}, u32[]{:S(2)}, u32[]{:S(2)}) async-start(f32[8,1,128]{2,1,0:T(1,128)} %broadcast_in_dim.86), calls=%async_computation.3 | async-start | bytes 8192 | tf_op jit(solution)/shard_map/all_to_all | solution.py:207
  170.5 3.3 %fusion.1 = bf16[1024,1152]{0,1:T(8,128)(2,1)} fusion(bf16[1024,1152]{0,1:T(8,128)(2,1)S(1)} %divide_convert_fusion, bf16[1152,128]{1,0:T(8,128)(2,1)} %bitcast.162, f32[1024]{0:T(1024)S(1)} %fusion.5, bf16[16,8,8,128]{3,2,1,0:T(8,128)(2,1)S(1)} %bitcast.151), kind=kOutput, calls=%fused_computation.4 | convolution fusion | flops 307888128 | bytes 5279744 | tf_op jit(solution)/shard_map/dot_general | solution.py:252
  173.8 5.5 %all-to-all-done.3 = f32[8,1,128]{2,1,0:T(1,128)S(1)} async-done(((f32[8,1,128]{2,1,0:T(1,128)}), f32[8,1,128]{2,1,0:T(1,128)S(1)}, u32[]{:S(2)}, u32[]{:S(2)}) %all-to-all-start.3) | async-done | bytes 4128 | tf_op jit(solution)/shard_map/all_to_all | solution.py:207
  179.6 1.9 fusion.16
  181.6 0.9 fusion.15
  182.5 1.0 fusion.12
  183.5 5.2 %all-to-all-start.4 = ((bf16[8,128,256]{1,2,0:T(8,128)(2,1)}), bf16[8,128,256]{1,2,0:T(8,128)(2,1)S(1)}, u32[]{:S(2)}, u32[]{:S(2)}) async-start(bf16[8,128,256]{1,2,0:T(8,128)(2,1)} %fusion.12), calls=%async_computation.4 | async-start | bytes 1048576 | tf_op jit(solution)/shard_map/all_to_all | solution.py:44
  188.9 2.2 %fusion.6 = bf16[16,8,8,128]{3,1,2,0:T(8,128)(2,1)S(1)} fusion(bf16[1024,1152]{0,1:T(8,128)(2,1)} %fusion.1, bf16[1152,128]{1,0:T(8,128)(2,1)S(1)} %bitcast.160, f32[1024]{0:T(1024)S(1)} %broadcast_bitcast_fusion), kind=kOutput, calls=%fused_computation.20 | convolution fusion | flops 302252032 | bytes 2920448 | tf_op jit(solution)/shard_map/dot_general | solution.py:256
  191.5 0.8 copy.148
  192.2 11.0 %all-to-all-done.4 = bf16[8,128,256]{1,2,0:T(8,128)(2,1)S(1)} async-done(((bf16[8,128,256]{1,2,0:T(8,128)(2,1)}), bf16[8,128,256]{1,2,0:T(8,128)(2,1)S(1)}, u32[]{:S(2)}, u32[]{:S(2)}) %all-to-all-start.4) | async-done | bytes 524320 | tf_op jit(solution)/shard_map/all_to_all | solution.py:44
  203.6 1.3 collective-permute-start.14
  205.5 3.1 %collective-permute-done.14 = bf16[128,256]{0,1:T(8,128)(2,1)S(1)} collective-permute-done((bf16[128,256]{0,1:T(8,128)(2,1)S(1)}, bf16[128,256]{0,1:T(8,128)(2,1)S(1)}, u32[]{:S(2)}, u32[]{:S(2)}) %collective-permute-start.14) | collective-permute-done | bytes 65568 | tf_op jit(solution)/shard_map/ppermute | solution.py:54
  208.6 0.7 copy.100
  209.4 0.7 copy.101
  (101 shorter events, 9.9 us)
Async XLA Ops:
  2.5 40.4 %all-to-all-start = ((bf16[32,8,2048]{2,1,0:T(8,128)(2,1)}), bf16[32,8,2048]{2,1,0:T(8,128)(2,1)S(1)}, u32[]{:S(2)}, u32[]{:S(2)}) async-start(bf16[32,8,2048]{2,1,0:T(8,128)(2,1)} %broadcast_in_dim.78), calls=%async_computation | async-start | bytes 2097152 | tf_op jit(solution)/shard_map/all_to_all | solution.py:38
  17.5 0.5 copy-start.19
  18.8 15.8 %collective-permute-start.1 = (bf16[1,144,256]{2,1,0:T(8,128)(2,1)S(1)}, bf16[1,144,256]{2,1,0:T(8,128)(2,1)S(1)}, u32[]{:S(2)}, u32[]{:S(2)}) collective-permute-start(bf16[1,144,256]{2,1,0:T(8,128)(2,1)S(1)} %maximum_bitcast_fusion), channel_id=1, source_target_pairs={{0,2},{2,4},{4,6},{6,8},{8,10},{10,12},{12,14},{14,16},{16,18},{18... | collective-permute-start | bytes 221192 | tf_op jit(solution)/shard_map/ppermute | solution.py:54
  23.1 17.3 %collective-permute-start = (bf16[1,144,256]{2,1,0:T(8,128)(2,1)S(1)}, bf16[1,144,256]{2,1,0:T(8,128)(2,1)S(1)}, u32[]{:S(2)}, u32[]{:S(2)}) collective-permute-start(bf16[1,144,256]{2,1,0:T(8,128)(2,1)S(1)} %maximum_bitcast_fusion), channel_id=1, source_target_pairs={{0,16},{2,18},{4,20},{6,22},{8,24},{10,26},{12,28},{14,30},{16,32}... | collective-permute-start | bytes 221192 | tf_op jit(solution)/shard_map/ppermute | solution.py:54
  40.4 3.6 %copy-start.12 = (bf16[1,144,256]{2,1,0:T(8,128)(2,1)}, bf16[1,144,256]{2,1,0:T(8,128)(2,1)S(1)}, u32[]{:S(2)}) copy-start(bf16[1,144,256]{2,1,0:T(8,128)(2,1)S(1)} %collective-permute-done) | copy-start | bytes 221188
  44.0 41.7 %all-to-all-start.1 = ((bf16[32,8,2048]{2,1,0:T(8,128)(2,1)}), bf16[32,8,2048]{2,1,0:T(8,128)(2,1)S(1)}, u32[]{:S(2)}, u32[]{:S(2)}) async-start(bf16[32,8,2048]{2,1,0:T(8,128)(2,1)} %broadcast_in_dim.79), calls=%async_computation.1 | async-start | bytes 2097152 | tf_op jit(solution)/shard_map/all_to_all | solution.py:38
  52.6 5.4 %collective-permute-start.2 = (bf16[256,2048]{1,0:T(8,128)(2,1)S(1)}, bf16[256,2048]{1,0:T(8,128)(2,1)S(1)}, u32[]{:S(2)}, u32[]{:S(2)}) collective-permute-start(bf16[256,2048]{1,0:T(8,128)(2,1)S(1)} %bitcast.139), channel_id=1, source_target_pairs={{0,2},{2,0},{4,6},{6,4},{8,10},{10,8},{12,14},{14,12},{16,18},{18,... | collective-permute-start | bytes 3145736 | tf_op jit(solution)/shard_map/ppermute | solution.py:29
  58.0 2.2 %copy-start = (bf16[2048,1024]{1,0:T(8,128)(2,1)S(1)}, bf16[2048,1024]{1,0:T(8,128)(2,1)}, u32[]{:S(2)}) copy-start(bf16[2048,1024]{1,0:T(8,128)(2,1)} %head_ref.3) | copy-start | bytes 12582916
  60.2 28.0 %copy-start.15 = (f32[1024]{0:T(1024)S(1)}, f32[1024]{0:T(1024)}, u32[]{:S(2)}) copy-start(f32[1024]{0:T(1024)} %param.13) | copy-start | bytes 12292
  60.2 28.1 %copy-start.16 = (s32[1024]{0:T(1024)S(1)}, s32[1024]{0:T(1024)}, u32[]{:S(2)}) copy-start(s32[1024]{0:T(1024)} %param.12) | copy-start | bytes 12292
  63.9 15.2 %collective-permute-start.5 = (bf16[2,64,1024]{2,1,0:T(8,128)(2,1)S(1)}, bf16[2,64,1024]{2,1,0:T(8,128)(2,1)S(1)}, u32[]{:S(2)}, u32[]{:S(2)}) collective-permute-start(bf16[2,64,1024]{2,1,0:T(8,128)(2,1)S(1)} %get-tuple-element.33), channel_id=1, source_target_pairs={{0,384},{128,0},{256,128},{384,256},{1,385},{129,1},{257,129},{385... | collective-permute-start | bytes 786440 | tf_op jit(solution)/shard_map/ppermute | solution.py:58
  68.3 10.8 %collective-permute-start.4 = (bf16[2,64,1024]{2,1,0:T(8,128)(2,1)S(1)}, bf16[2,64,1024]{2,1,0:T(8,128)(2,1)S(1)}, u32[]{:S(2)}, u32[]{:S(2)}) collective-permute-start(bf16[2,64,1024]{2,1,0:T(8,128)(2,1)S(1)} %get-tuple-element.32), channel_id=1, source_target_pairs={{0,256},{128,384},{256,0},{384,128},{1,257},{129,385},{257,1},{385... | collective-permute-start | bytes 786440 | tf_op jit(solution)/shard_map/ppermute | solution.py:58
  70.7 14.8 %collective-permute-start.3 = (bf16[2,64,1024]{2,1,0:T(8,128)(2,1)S(1)}, bf16[2,64,1024]{2,1,0:T(8,128)(2,1)S(1)}, u32[]{:S(2)}, u32[]{:S(2)}) collective-permute-start(bf16[2,64,1024]{2,1,0:T(8,128)(2,1)S(1)} %get-tuple-element.31), channel_id=1, source_target_pairs={{0,128},{128,256},{256,384},{384,0},{1,129},{129,257},{257,385},{3... | collective-permute-start | bytes 786440 | tf_op jit(solution)/shard_map/ppermute | solution.py:58
  85.7 10.5 %copy-start.3 = (f32[2,64,1024]{2,1,0:T(8,128)}, f32[2,64,1024]{2,1,0:T(8,128)S(1)}, u32[]{:S(2)}) copy-start(f32[2,64,1024]{2,1,0:T(8,128)S(1)} %convert_add_fusion.1) | copy-start | bytes 1572868
  85.7 10.5 %collective-permute-start.6 = (bf16[256,2048]{1,0:T(8,128)(2,1)S(1)}, bf16[256,2048]{1,0:T(8,128)(2,1)S(1)}, u32[]{:S(2)}, u32[]{:S(2)}) collective-permute-start(bf16[256,2048]{1,0:T(8,128)(2,1)S(1)} %bitcast.137), channel_id=1, source_target_pairs={{0,2},{2,0},{4,6},{6,4},{8,10},{10,8},{12,14},{14,12},{16,18},{18,... | collective-permute-start | bytes 3145736 | tf_op jit(solution)/shard_map/ppermute | solution.py:29
  91.4 26.8 %collective-permute-start.11 = (bf16[2,144,256]{2,1,0:T(8,128)(2,1)S(1)}, bf16[2,144,256]{2,1,0:T(8,128)(2,1)}, u32[]{:S(2)}, u32[]{:S(2)}) collective-permute-start(bf16[2,144,256]{2,1,0:T(8,128)(2,1)S(1)} %pad_maximum_fusion.2), channel_id=1, source_target_pairs={{0,4},{2,6},{4,8},{6,10},{8,12},{10,14},{12,16},{14,18},{16,20},{1... | collective-permute-start | bytes 442376 | tf_op jit(solution)/shard_map/ppermute | solution.py:54
  96.2 2.2 %copy-start.1 = (bf16[2048,1024]{1,0:T(8,128)(2,1)S(1)}, bf16[2048,1024]{1,0:T(8,128)(2,1)}, u32[]{:S(2)}) copy-start(bf16[2048,1024]{1,0:T(8,128)(2,1)} %head_ref.3) | copy-start | bytes 12582916
  102.1 27.7 %copy-start.4 = (f32[2,64,1024]{2,1,0:T(8,128)S(1)}, f32[2,64,1024]{2,1,0:T(8,128)}, u32[]{:S(2)}) copy-start(f32[2,64,1024]{2,1,0:T(8,128)} %copy-done.3) | copy-start | bytes 1572868
  102.1 21.9 %collective-permute-start.10 = (bf16[2,64,1024]{2,1,0:T(8,128)(2,1)S(1)}, bf16[2,64,1024]{2,1,0:T(8,128)(2,1)}, u32[]{:S(2)}, u32[]{:S(2)}) collective-permute-start(bf16[2,64,1024]{2,1,0:T(8,128)(2,1)S(1)} %get-tuple-element.47), channel_id=1, source_target_pairs={{0,384},{128,0},{256,128},{384,256},{1,385},{129,1},{257,129},{385... | collective-permute-start | bytes 786440 | tf_op jit(solution)/shard_map/ppermute | solution.py:58
  104.5 19.5 %collective-permute-start.9 = (bf16[2,64,1024]{2,1,0:T(8,128)(2,1)S(1)}, bf16[2,64,1024]{2,1,0:T(8,128)(2,1)}, u32[]{:S(2)}, u32[]{:S(2)}) collective-permute-start(bf16[2,64,1024]{2,1,0:T(8,128)(2,1)S(1)} %get-tuple-element.46), channel_id=1, source_target_pairs={{0,256},{128,384},{256,0},{384,128},{1,257},{129,385},{257,1},{385... | collective-permute-start | bytes 786440 | tf_op jit(solution)/shard_map/ppermute | solution.py:58
  106.9 17.1 %collective-permute-start.8 = (bf16[2,64,1024]{2,1,0:T(8,128)(2,1)S(1)}, bf16[2,64,1024]{2,1,0:T(8,128)(2,1)}, u32[]{:S(2)}, u32[]{:S(2)}) collective-permute-start(bf16[2,64,1024]{2,1,0:T(8,128)(2,1)S(1)} %get-tuple-element.45), channel_id=1, source_target_pairs={{0,128},{128,256},{256,384},{384,0},{1,129},{129,257},{257,385},{3... | collective-permute-start | bytes 786440 | tf_op jit(solution)/shard_map/ppermute | solution.py:58
  113.9 40.9 %copy-start.5 = (bf16[128,8,128]{0,1,2:T(8,128)(2,1)}, bf16[128,8,128]{0,1,2:T(8,128)(2,1)S(1)}, u32[]{:S(2)}) copy-start(bf16[128,8,128]{0,1,2:T(8,128)(2,1)S(1)} %copy.92) | copy-start | bytes 786436
  116.7 53.8 %copy-start.7 = (bf16[128,8,128]{0,1,2:T(8,128)(2,1)}, bf16[128,8,128]{0,1,2:T(8,128)(2,1)S(1)}, u32[]{:S(2)}) copy-start(bf16[128,8,128]{0,1,2:T(8,128)(2,1)S(1)} %copy.93) | copy-start | bytes 786436
  119.2 10.6 %collective-permute-start.7 = (bf16[2,32,1024]{2,1,0:T(8,128)(2,1)}, bf16[2,32,1024]{2,1,0:T(8,128)(2,1)S(1)}, u32[]{:S(2)}, u32[]{:S(2)}) collective-permute-start(bf16[2,32,1024]{2,1,0:T(8,128)(2,1)} %fusion.30), channel_id=1, source_target_pairs={{0,1},{1,0},{2,3},{3,2},{4,5},{5,4},{6,7},{7,6},{8,9},{9,8},{10,11... | collective-permute-start | bytes 393224 | tf_op jit(solution)/shard_map/ppermute | solution.py:62
  124.0 27.9 %copy-start.8 = (bf16[9,144,256]{2,1,0:T(8,128)(2,1)S(1)}, bf16[9,144,256]{2,1,0:T(8,128)(2,1)}, u32[]{:S(2)}) copy-start(bf16[9,144,256]{2,1,0:T(8,128)(2,1)} %constant_dynamic-update-slice_fusion.2) | copy-start | bytes 1990660
  125.4 14.8 %collective-permute-start.12 = (bf16[2,32,1024]{2,1,0:T(8,128)(2,1)S(1)}, bf16[2,32,1024]{2,1,0:T(8,128)(2,1)S(1)}, u32[]{:S(2)}, u32[]{:S(2)}) collective-permute-start(bf16[2,32,1024]{2,1,0:T(8,128)(2,1)S(1)} %fusion.31), channel_id=1, source_target_pairs={{0,1},{1,0},{2,3},{3,2},{4,5},{5,4},{6,7},{7,6},{8,9},{9,8},{10,11... | collective-permute-start | bytes 393224 | tf_op jit(solution)/shard_map/ppermute | solution.py:62
  129.9 22.0 %collective-permute-start.13 = (bf16[4,144,256]{2,1,0:T(8,128)(2,1)S(1)}, bf16[4,144,256]{2,1,0:T(8,128)(2,1)S(1)}, u32[]{:S(2)}, u32[]{:S(2)}) collective-permute-start(bf16[4,144,256]{2,1,0:T(8,128)(2,1)S(1)} %pad_maximum_fusion.1), channel_id=1, source_target_pairs={{0,8},{2,10},{4,12},{6,14},{8,16},{10,18},{12,20},{14,22},{16,24},... | collective-permute-start | bytes 884744 | tf_op jit(solution)/shard_map/ppermute | solution.py:54
  142.2 20.5 %all-to-all-start.2 = ((f32[64,3,128]{2,1,0:T(4,128)}), f32[64,3,128]{2,1,0:T(4,128)S(1)}, u32[]{:S(2)}, u32[]{:S(2)}) async-start(f32[64,3,128]{2,1,0:T(4,128)} %broadcast_in_dim.83), calls=%async_computation.2 | async-start | bytes 262144 | tf_op jit(solution)/shard_map/all_to_all | solution.py:198
  152.1 3.9 %copy-start.9 = (bf16[9,128,128]{2,1,0:T(8,128)(2,1)}, bf16[9,128,128]{2,1,0:T(8,128)(2,1)S(1)}, u32[]{:S(2)}) copy-start(bf16[9,128,128]{2,1,0:T(8,128)(2,1)S(1)} %get-tuple-element.87) | copy-start | bytes 884740
  152.1 6.7 %copy-start.11 = (bf16[9,128,128]{2,1,0:T(8,128)(2,1)}, bf16[9,128,128]{2,1,0:T(8,128)(2,1)S(1)}, u32[]{:S(2)}) copy-start(bf16[9,128,128]{2,1,0:T(8,128)(2,1)S(1)} %get-tuple-element.86) | copy-start | bytes 884740
  157.3 5.6 %copy-start.18 = (f32[128]{0:T(128)S(1)}, f32[128]{0:T(128)}, u32[]{:S(2)}) copy-start(f32[128]{0:T(128)} %reshape.222) | copy-start | bytes 1540
  158.7 20.6 %copy-start.14 = (s32[1024]{0:T(1024)S(1)}, s32[1024]{0:T(1024)}, u32[]{:S(2)}) copy-start(s32[1024]{0:T(1024)} %eq.59) | copy-start | bytes 12292
  158.8 20.6 %copy-start.17 = (s32[128]{0:T(128)S(1)}, s32[128]{0:T(128)}, u32[]{:S(2)}) copy-start(s32[128]{0:T(128)} %iota_add_fusion.2) | copy-start | bytes 1540
  163.4 15.9 %all-to-all-start.3 = ((f32[8,1,128]{2,1,0:T(1,128)}), f32[8,1,128]{2,1,0:T(1,128)S(1)}, u32[]{:S(2)}, u32[]{:S(2)}) async-start(f32[8,1,128]{2,1,0:T(1,128)} %broadcast_in_dim.86), calls=%async_computation.3 | async-start | bytes 8192 | tf_op jit(solution)/shard_map/all_to_all | solution.py:207
  170.5 11.0 %copy-start.6 = (bf16[128,8,128]{0,1,2:T(8,128)(2,1)S(1)}, bf16[128,8,128]{0,1,2:T(8,128)(2,1)}, u32[]{:S(2)}) copy-start(bf16[128,8,128]{0,1,2:T(8,128)(2,1)} %copy-done.5) | copy-start | bytes 786436
  179.3 2.2 %copy-start.2 = (bf16[1024,1152]{0,1:T(8,128)(2,1)S(1)}, bf16[1024,1152]{0,1:T(8,128)(2,1)}, u32[]{:S(2)}) copy-start(bf16[1024,1152]{0,1:T(8,128)(2,1)} %fusion.1) | copy-start | bytes 7077892
  181.5 7.2 %copy-start.13 = (f32[2,4,2,8]{3,2,0,1:T(2,128)S(1)}, f32[2,4,2,8]{3,2,0,1:T(2,128)}, u32[]{:S(2)}) copy-start(f32[2,4,2,8]{3,2,0,1:T(2,128)} %dynamic-slice_bitcast_fusion) | copy-start | bytes 1540
  181.6 7.4 %copy-start.10 = (bf16[9,128,128]{2,1,0:T(8,128)(2,1)S(1)}, bf16[9,128,128]{2,1,0:T(8,128)(2,1)}, u32[]{:S(2)}) copy-start(bf16[9,128,128]{2,1,0:T(8,128)(2,1)} %copy-done.9) | copy-start | bytes 884740
  183.5 19.7 %all-to-all-start.4 = ((bf16[8,128,256]{1,2,0:T(8,128)(2,1)}), bf16[8,128,256]{1,2,0:T(8,128)(2,1)S(1)}, u32[]{:S(2)}, u32[]{:S(2)}) async-start(bf16[8,128,256]{1,2,0:T(8,128)(2,1)} %fusion.12), calls=%async_computation.4 | async-start | bytes 1048576 | tf_op jit(solution)/shard_map/all_to_all | solution.py:44
  203.6 5.0 %collective-permute-start.14 = (bf16[128,256]{0,1:T(8,128)(2,1)S(1)}, bf16[128,256]{0,1:T(8,128)(2,1)S(1)}, u32[]{:S(2)}, u32[]{:S(2)}) collective-permute-start(bf16[128,256]{0,1:T(8,128)(2,1)S(1)} %get-tuple-element.85), channel_id=1, source_target_pairs={{16,0},{18,2},{20,4},{22,6},{24,8},{26,10},{28,12},{30,14},{32,16}... | collective-permute-start | bytes 196616 | tf_op jit(solution)/shard_map/ppermute | solution.py:54

commit v4 on v3

--- a/solution.py
+++ b/solution.py
@@ -1,10 +1,6 @@
-import functools
-
 import jax
 import jax.numpy as jnp
 from jax import lax
-from jax.experimental import pallas as pl
-from jax.experimental.pallas import tpu as pltpu
 from jax.sharding import PartitionSpec as P
 
 advantage_scale = 0.1
@@ -54,65 +50,41 @@
     return lax.ppermute(block, "ctx", route)
 
 
-def along_section(block, step):
-    return lax.ppermute(block, "section", [(s, (s + step) % SECTIONS) for s in range(SECTIONS)])
+def over_section(block, bits):
+    return lax.ppermute(block, "section", [(s, s ^ bits) for s in range(SECTIONS)])
 
 
 def to_other_tp(block):
     return lax.ppermute(block, "tp", [(0, 1), (1, 0)])
 
 
-def logits_kernel(section_ref, mine_ref, theirs_ref, head_ref, *refs):
-    outs, logits = refs[:SECTIONS], refs[SECTIONS]
-    count = outs[0].shape[1]
-    for part, rows in enumerate((mine_ref, theirs_ref)):
-        logits[part] = jnp.dot(rows[...], head_ref[...], preferred_element_type=jnp.float32)
-        for step, out in enumerate(outs):
-            place = lax.rem(section_ref[0] + step, SECTIONS)
-            kept = logits[part, pl.ds(pl.multiple_of(place * count, count), count), :]
-            out[part] = kept.astype(out.dtype)
-
-
-def section_parts(gathered, weight, section):
+def both_logits(gathered, weight):
     mine = gathered.reshape(-1, gathered.shape[2])
-    rows, depth = mine.shape
-    vocab, tile = weight.shape[1], 256
-    count = rows // SECTIONS
-    whole = pl.BlockSpec((rows, depth), lambda n: (0, 0))
-    kinds = [jnp.float32] + [jnp.bfloat16] * (SECTIONS - 1)
-    return pl.pallas_call(
-        logits_kernel,
-        grid=(vocab // tile,),
-        in_specs=[
-            pl.BlockSpec(memory_space=pltpu.SMEM),
-            whole,
-            whole,
-            pl.BlockSpec((depth, tile), lambda n: (0, n)),
-        ],
-        out_specs=[pl.BlockSpec((2, count, tile), lambda n: (0, 0, n))] * SECTIONS,
-        out_shape=[jax.ShapeDtypeStruct((2, count, vocab), kind) for kind in kinds],
-        scratch_shapes=[pltpu.VMEM((2, rows, tile), jnp.float32)],
-        compiler_params=pltpu.CompilerParams(vmem_limit_bytes=24 * 1024 * 1024),
-        cost_estimate=pl.CostEstimate(
-            flops=4 * rows * depth * vocab,
-            bytes_accessed=2 * depth * vocab + 4 * rows * depth + 5 * rows * vocab,
-            transcendentals=0,
-        ),
-    )(jnp.reshape(section, (1,)), mine, other_core(mine), weight)
-
-
-def section_arrivals(parts):
-    return [along_section(parts[step], step) for step in (1, 2, 3)]
-
-
-def section_sums(own, arrivals):
-    return functools.reduce(lambda total, part: total + part.astype(jnp.float32), arrivals, own)
+    for rows in (mine, other_core(mine)):
+        logits = jnp.dot(rows, weight, preferred_element_type=jnp.float32)
+        yield logits.reshape(SECTIONS, TPS, Y, gathered.shape[1], weight.shape[1])
+
+
+def of_section(logits, section):
+    return lax.dynamic_index_in_dim(logits, section, 0, keepdims=False)
+
+
+def first_round(logits, section, bits):
+    given = jnp.stack([of_section(logits, section ^ bits), of_section(logits, section ^ 2)])
+    return over_section(given.astype(jnp.bfloat16), bits)
+
+
+def second_round(logits, arrived, section, bits):
+    arrived = arrived.astype(jnp.float32)
+    given = of_section(logits, section ^ bits) + arrived[1]
+    return of_section(logits, section) + arrived[0] + over_section(
+        given.astype(jnp.bfloat16), bits
+    ).astype(jnp.float32)
 
 
 def tp_halves(total, tp):
-    halves = total.reshape(2, TPS, -1, total.shape[2])
-    keep = lax.dynamic_index_in_dim(halves, tp, 1, keepdims=False)
-    give = lax.dynamic_index_in_dim(halves, 1 - tp, 1, keepdims=False)
+    keep = lax.dynamic_index_in_dim(total, tp, 1, keepdims=False)
+    give = lax.dynamic_index_in_dim(total, 1 - tp, 1, keepdims=False)
     return keep, give.astype(jnp.bfloat16)
 
 
@@ -159,27 +131,62 @@
     tp = lax.axis_index("tp")
     place, core = lax.rem(ctx_index, Y * CORES), lax.rem(ctx_index, CORES)
 
+    seq_rows = queries.shape[0]
+    head_dim = keys.shape[1]
+    group = queries.shape[1] // head_dim
+    scaling = head_dim ** (-0.5)
+
+    query_position = ctx_index * seq_rows + jnp.arange(seq_rows, dtype=jnp.int32)
+    key_position = (ctx_index - FARTHEST) * seq_rows + jnp.arange(
+        (FARTHEST + 1) * seq_rows, dtype=jnp.int32
+    )
+    reached = (key_position[None, :] <= query_position[:, None]) & (key_position[None, :] >= 0)
+    owners = owner_map.reshape(SECTIONS * TPS, Y, CORES, PIECE).transpose(0, 2, 1, 3).reshape(-1)
+    routes = owners[None, :] == query_position[:, None]
+
+    def by_head(array):
+        return (
+            array.reshape(seq_rows, group, head_dim)
+            .transpose(1, 0, 2)
+            .reshape(group * seq_rows, head_dim)
+        )
+
+    query_rows, grad_rows = by_head(queries), by_head(grad_out)
+    own_window = packed_window(keys, values, segment_ids)
+    eighth = passed_along(own_window, 8)
+    two_windows = jnp.concatenate([passed_along(own_window, 1), own_window], axis=0)
+
     half = teacher_hidden.shape[0] // 2
     first = across_chips(copies_for_chips(teacher_hidden[:half]))
     copies = copies_for_chips(teacher_hidden[half:])
-    own_window = packed_window(keys, values, segment_ids)
-    eighth = passed_along(own_window, 8)
-    two_windows = jnp.concatenate([passed_along(own_window, 1), own_window], axis=0)
-    first, copies, eighth, two_windows = lax.optimization_barrier(
-        (first, copies, eighth, two_windows)
+    (
+        first, copies, eighth, two_windows, query_rows, grad_rows, reached, routes,
+    ) = lax.optimization_barrier(
+        (first, copies, eighth, two_windows, query_rows, grad_rows, reached, routes)
     )
     last = across_chips(copies)
-    first = section_parts(first, lm_head, section)
-    arrivals = section_arrivals(first)
-    arrivals[2], two_windows = lax.optimization_barrier((arrivals[2], two_windows))
+    mine, theirs = both_logits(first, lm_head)
+    arrived = [first_round(mine, section, 1), first_round(theirs, section, 3)]
+    arrived[1], two_windows = lax.optimization_barrier((arrived[1], two_windows))
     four_windows = jnp.concatenate([passed_along(two_windows, 2), two_windows], axis=0)
-    first, last = lax.optimization_barrier((section_sums(first[0], arrivals), last))
-    keep, give = tp_halves(first, tp)
-    last = section_parts(last, lm_head, section)
-    give, last = lax.optimization_barrier((give, last))
-    arrivals = section_arrivals(last)
-    first = tp_sums(keep, give)
-    last, four_windows = lax.optimization_barrier((section_sums(last[0], arrivals), four_windows))
+    first = jnp.stack(
+        [
+            second_round(mine, arrived[0], section, 3),
+            second_round(theirs, arrived[1], section, 1),
+        ]
+    )
+    first, last, four_windows = lax.optimization_barrier((first, last, four_windows))
+    first = tp_sums(*tp_halves(first, tp))
+    mine, theirs = both_logits(last, lm_head)
+    arrived = [first_round(mine, section, 1), first_round(theirs, section, 3)]
+    arrived[0], first = lax.optimization_barrier((arrived[0], first))
+    last = jnp.stack(
+        [
+            second_round(mine, arrived[0], section, 3),
+            second_round(theirs, arrived[1], section, 1),
+        ]
+    )
+    last, four_windows = lax.optimization_barrier((last, four_windows))
     last = tp_sums(*tp_halves(last, tp))
     window = jnp.concatenate([eighth, passed_along(four_windows, 4), four_windows], axis=0)
 
@@ -189,9 +196,7 @@
             rows, section * TPS + tp, 0, keepdims=False
         ).transpose(1, 0, 2, 3)
 
-    logits = jnp.stack(
-        [part.reshape(CORES, Y, half, -1) for part in (first, last)], axis=2
-    )
+    logits = jnp.stack([first, last], axis=2)
     columns = ctx_index * lm_head.shape[1] + jnp.arange(lm_head.shape[1], dtype=jnp.int32)
     stats = row_stats(logits, columns, cores_exchanged(kept_rows(sampled_ids), 0, core))
     stats = cores_exchanged(stats, 1, core).reshape(3, -1)
@@ -207,41 +212,19 @@
     everything = lax.all_to_all(
         jnp.broadcast_to(advantage, (count,) + advantage.shape), ("section", "tp"), 0, 0
     )
-    owners = owner_map.reshape(SECTIONS * TPS, Y, CORES, PIECE).transpose(0, 2, 1, 3).reshape(-1)
     advantage_own = advantage.reshape(CORES, Y, PIECE).transpose(1, 0, 2).reshape(-1)
     everything = everything.reshape(-1)
 
-    seq_rows = queries.shape[0]
-    head_dim = keys.shape[1]
-    group = queries.shape[1] // head_dim
-    scaling = head_dim ** (-0.5)
-    query_position = ctx_index * seq_rows + jnp.arange(seq_rows, dtype=jnp.int32)
-    routed = jnp.sum(
-        jnp.where(owners[None, :] == query_position[:, None], everything[None, :], 0.0), axis=1
-    )
+    routed = jnp.sum(jnp.where(routes, everything[None, :], 0.0), axis=1)
     weight = 1.0 + advantage_scale * routed
 
     key_window = window[:, :seq_rows, :head_dim].reshape(-1, head_dim)
     value_window = window[:, :seq_rows, head_dim:].reshape(-1, head_dim)
     key_segment = window[:, seq_rows, :seq_rows].reshape(-1)
-    key_position = (ctx_index - FARTHEST) * seq_rows + jnp.arange(
-        (FARTHEST + 1) * seq_rows, dtype=jnp.int32
-    )
-    allowed = (
-        (key_segment[None, :] == segment_ids.astype(jnp.bfloat16)[:, None])
-        & (key_position[None, :] <= query_position[:, None])
-        & (key_position[None, :] >= 0)
-    )
+    own_segment = segment_ids.astype(jnp.bfloat16)
+    allowed = (key_segment[None, :] == own_segment[:, None]) & reached
     allowed = jnp.tile(allowed, (group, 1))
 
-    def by_head(array):
-        return (
-            array.reshape(seq_rows, group, head_dim)
-            .transpose(1, 0, 2)
-            .reshape(group * seq_rows, head_dim)
-        )
-
-    query_rows, grad_rows = by_head(queries), by_head(grad_out)
     scores = jnp.dot(query_rows, key_window.T, preferred_element_type=jnp.float32) * scaling
     masked = jnp.where(allowed, scores, masked_value)
     top = jnp.max(masked, axis=1, keepdims=True)

time: 212 us -> 209 us (0.986)
  waiting for transfers between devices: 58.3 us -> 42.4 us
  starting transfers between devices: 95.2 us -> 111 us
  matrix products: 10 us -> 19.2 us
  Pallas kernels: 7.46 us -> 0 us
  local copies, waits for them, and re-layouts: 23.2 us -> 18 us
    dot_general x0 -> x4, matrix products: none -> 9.71 us  [both_logits(): logits = jnp.dot(rows, weight, preferred_element_type=jnp.float32)]
    ppermute x6 -> x8, starting transfers between devices: 16.7 us -> 26.2 us  [over_section(): lax.ppermute(block, 'section', [(s, s ^ bits) for s in range(SECTIONS)])]
    pallas_call x2 -> x0, Pallas kernels: 7.46 us -> none  [section_parts(): pl.pallas_call(logits_kernel, grid=(vocab // tile,), in_specs=[pl.BlockSp...]
    all_to_all x1, starting transfers between devices: 9.68 us -> 16.9 us  [body(): lax.all_to_all(jnp.broadcast_to(stats, (Z * Y * CORES,) + stats.shape), '...]
    ppermute x6 -> x8, waiting for transfers between devices: 12.3 us -> 7.67 us  [over_section(): lax.ppermute(block, 'section', [(s, s ^ bits) for s in range(SECTIONS)])]
    unnamed x48 -> x34, local copies, waits for them, and re-layouts: 10.8 us -> 6.64 us
    ppermute x2, waiting for transfers between devices: 4.04 us -> 0.01 us  [to_other_tp(): return lax.ppermute(block, 'tp', [(0, 1), (1, 0)])]
    ppermute x5, waiting for transfers between devices: 17.3 us -> 13.6 us  [passed_along(): return lax.ppermute(block, 'ctx', route)]
  transfers between devices with their start and end apart: 20 -> 22, of which waited for: 11 -> 14; matrix products, arithmetic and copies ran while one was open for 16% -> 19% of each run, Pallas kernels for 4% -> 0%
where the time goes in v4:
time: 209 us; the launch traced here: 208 us
  starting transfers between devices  111 us (53%)
  waiting for transfers between devices  42.4 us (20%)
  matrix products  19.2 us (9%)
  local copies, waits for them, and re-layouts  18 us (9%)
  other arithmetic  15.1 us (7%)
    ppermute x8, starting transfers between devices, over_section(): lax.ppermute(block, 'section', [(s, s ^ bits) for s in range(SECTIONS)])  26.2 us
    all_to_all x2, starting transfers between devices, across_chips(): return lax.all_to_all(copies, 'ctx', 0, 0, axis_index_groups=groups)  22.9 us
    ppermute x5, starting transfers between devices, passed_along(): return lax.ppermute(block, 'ctx', route)  17.8 us
    all_to_all x1, starting transfers between devices, body(): lax.all_to_all(jnp.broadcast_to(stats, (Z * Y * CORES,) + stats.shape), '...  16.9 us
    ppermute x5, waiting for transfers between devices, passed_along(): return lax.ppermute(block, 'ctx', route)  13.6 us
    all_to_all x1, waiting for transfers between devices, across_row(): return lax.all_to_all(blocks, 'ctx', 0, 0, axis_index_groups=groups)  10.3 us
    dot_general x4, matrix products, both_logits(): logits = jnp.dot(rows, weight, preferred_element_type=jnp.float32)  9.71 us
    ppermute x2, starting transfers between devices, to_other_tp(): return lax.ppermute(block, 'tp', [(0, 1), (1, 0)])  9.2 us
  transfers between devices with their start and end apart: 22, of which 14 were waited for; matrix products, arithmetic and copies ran while one was open for 19% of the time, Pallas kernels for 0%

profile of v4, /device:TPU:1, one launch (start us, length us, event | category | flops | bytes accessed | tf_op | source)
XLA Modules:
  0.0 207.6 jit_solution(3367935030316135882)
XLA Ops:
  0.7 0.8 fusion.57
  1.5 1.1 broadcast_in_dim.78
  2.6 14.3 %all-to-all-start = ((bf16[32,8,2048]{2,1,0:T(8,128)(2,1)}), bf16[32,8,2048]{2,1,0:T(8,128)(2,1)S(1)}, u32[]{:S(2)}, u32[]{:S(2)}) async-start(bf16[32,8,2048]{2,1,0:T(8,128)(2,1)} %broadcast_in_dim.78), calls=%async_computation | async-start | bytes 2097152 | tf_op jit(solution)/shard_map/all_to_all | solution.py:34
  17.5 0.8 maximum_bitcast_fusion
  18.3 4.3 %collective-permute-start.1 = (bf16[1,144,256]{2,1,0:T(8,128)(2,1)S(1)}, bf16[1,144,256]{2,1,0:T(8,128)(2,1)S(1)}, u32[]{:S(2)}, u32[]{:S(2)}) collective-permute-start(bf16[1,144,256]{2,1,0:T(8,128)(2,1)S(1)} %maximum_bitcast_fusion), channel_id=1, source_target_pairs={{0,2},{2,4},{4,6},{6,8},{8,10},{10,12},{12,14},{14,16},{16,18},{18... | collective-permute-start | bytes 221192 | tf_op jit(solution)/shard_map/ppermute | solution.py:50
  22.6 3.1 %collective-permute-start = (bf16[1,144,256]{2,1,0:T(8,128)(2,1)S(1)}, bf16[1,144,256]{2,1,0:T(8,128)(2,1)S(1)}, u32[]{:S(2)}, u32[]{:S(2)}) collective-permute-start(bf16[1,144,256]{2,1,0:T(8,128)(2,1)S(1)} %maximum_bitcast_fusion), channel_id=1, source_target_pairs={{0,16},{2,18},{4,20},{6,22},{8,24},{10,26},{12,28},{14,30},{16,32}... | collective-permute-start | bytes 221192 | tf_op jit(solution)/shard_map/ppermute | solution.py:50
  25.7 0.8 reshape.155
  26.6 0.8 reshape.160
  27.4 1.0 copy.107
  29.1 0.8 broadcast_compare_fusion
  30.2 0.8 reshape.162
  30.9 3.7 %collective-permute-done.1 = bf16[1,144,256]{2,1,0:T(8,128)(2,1)S(1)} collective-permute-done((bf16[1,144,256]{2,1,0:T(8,128)(2,1)S(1)}, bf16[1,144,256]{2,1,0:T(8,128)(2,1)S(1)}, u32[]{:S(2)}, u32[]{:S(2)}) %collective-permute-start.1) | collective-permute-done | bytes 73760 | tf_op jit(solution)/shard_map/ppermute | solution.py:50
  34.6 5.8 %collective-permute-done = bf16[1,144,256]{2,1,0:T(8,128)(2,1)S(1)} collective-permute-done((bf16[1,144,256]{2,1,0:T(8,128)(2,1)S(1)}, bf16[1,144,256]{2,1,0:T(8,128)(2,1)S(1)}, u32[]{:S(2)}, u32[]{:S(2)}) %collective-permute-start) | collective-permute-done | bytes 73760 | tf_op jit(solution)/shard_map/ppermute | solution.py:50
  40.4 2.5 %all-to-all-done = bf16[32,8,2048]{2,1,0:T(8,128)(2,1)S(1)} async-done(((bf16[32,8,2048]{2,1,0:T(8,128)(2,1)}), bf16[32,8,2048]{2,1,0:T(8,128)(2,1)S(1)}, u32[]{:S(2)}, u32[]{:S(2)}) %all-to-all-start) | async-done | bytes 1048608 | tf_op jit(solution)/shard_map/all_to_all | solution.py:34
  42.9 1.1 broadcast_in_dim.79
  44.0 8.6 %all-to-all-start.1 = ((bf16[32,8,2048]{2,1,0:T(8,128)(2,1)}), bf16[32,8,2048]{2,1,0:T(8,128)(2,1)S(1)}, u32[]{:S(2)}, u32[]{:S(2)}) async-start(bf16[32,8,2048]{2,1,0:T(8,128)(2,1)} %broadcast_in_dim.79), calls=%async_computation.1 | async-start | bytes 2097152 | tf_op jit(solution)/shard_map/all_to_all | solution.py:34
  52.7 3.1 %collective-permute-start.4 = (bf16[256,2048]{1,0:T(8,128)(2,1)S(1)}, bf16[256,2048]{1,0:T(8,128)(2,1)S(1)}, u32[]{:S(2)}, u32[]{:S(2)}) collective-permute-start(bf16[256,2048]{1,0:T(8,128)(2,1)S(1)} %bitcast.162), channel_id=1, source_target_pairs={{0,2},{2,0},{4,6},{6,4},{8,10},{10,8},{12,14},{14,12},{16,18},{18,... | collective-permute-start | bytes 3145736 | tf_op jit(solution)/shard_map/ppermute | solution.py:25
  55.8 3.6 %fusion.4 = f32[4,2,4,8,1024]{4,3,2,1,0:T(8,128)S(1)} fusion(bf16[4,2,4,8,2048]{4,3,2,1,0:T(8,128)(2,1)S(1)} %bitcast.163, bf16[2048,1024]{1,0:T(8,128)(2,1)} %param.11), kind=kOutput, calls=%fused_computation.9 | convolution fusion | flops 1073741824 | bytes 6291456 | tf_op jit(solution)/shard_map/dot_general | solution.py:64
  59.4 0.8 pad_maximum_fusion.4
  60.2 3.1 %collective-permute-start.2 = (bf16[2,2,4,8,1024]{4,3,2,1,0:T(8,128)(2,1)}, bf16[2,2,4,8,1024]{4,3,2,1,0:T(8,128)(2,1)S(1)}, u32[]{:S(2)}, u32[]{:S(2)}) collective-permute-start(bf16[2,2,4,8,1024]{4,3,2,1,0:T(8,128)(2,1)} %pad_maximum_fusion.4), channel_id=1, source_target_pairs={{0,128},{128,0},{256,384},{384,256},{1,129},{129,1},{257,385},{385... | collective-permute-start | bytes 786440 | tf_op jit(solution)/shard_map/ppermute | solution.py:54
  63.4 1.3 fusion.59
  64.7 1.0 copy-done.5
  65.7 3.7 %collective-permute-start.5 = (bf16[2,2,4,8,1024]{4,3,2,1,0:T(8,128)(2,1)S(1)}, bf16[2,2,4,8,1024]{4,3,2,1,0:T(8,128)(2,1)S(1)}, u32[]{:S(2)}, u32[]{:S(2)}) collective-permute-start(bf16[2,2,4,8,1024]{4,3,2,1,0:T(8,128)(2,1)S(1)} %pad_maximum_fusion.5), channel_id=1, source_target_pairs={{0,384},{128,256},{256,128},{384,0},{1,385},{129,257},{257,129},{3... | collective-permute-start | bytes 786440 | tf_op jit(solution)/shard_map/ppermute | solution.py:54
  70.3 1.0 fusion.43
  71.3 4.4 %collective-permute-start.3 = (bf16[2,4,8,1024]{3,2,1,0:T(8,128)(2,1)S(1)}, bf16[2,4,8,1024]{3,2,1,0:T(8,128)(2,1)S(1)}, u32[]{:S(2)}, u32[]{:S(2)}) collective-permute-start(bf16[2,4,8,1024]{3,2,1,0:T(8,128)(2,1)S(1)} %fusion.43), channel_id=1, source_target_pairs={{0,384},{128,256},{256,128},{384,0},{1,385},{129,257},{257,129},{3... | collective-permute-start | bytes 393224 | tf_op jit(solution)/shard_map/ppermute | solution.py:54
  76.5 1.0 fusion.44
  77.5 1.9 collective-permute-start.6
  79.4 1.0 fusion.37
  80.4 3.4 %collective-permute-start.7 = (bf16[2,144,256]{2,1,0:T(8,128)(2,1)S(1)}, bf16[2,144,256]{2,1,0:T(8,128)(2,1)S(1)}, u32[]{:S(2)}, u32[]{:S(2)}) collective-permute-start(bf16[2,144,256]{2,1,0:T(8,128)(2,1)S(1)} %pad_maximum_fusion.8), channel_id=1, source_target_pairs={{0,4},{2,6},{4,8},{6,10},{8,12},{10,14},{12,16},{14,18},{16,20},{1... | collective-permute-start | bytes 442376 | tf_op jit(solution)/shard_map/ppermute | solution.py:50
  83.9 1.0 fusion.33
  84.9 1.0 collective-permute-done.7
  86.0 4.8 %collective-permute-start.9 = (bf16[2,4,8,1024]{3,2,1,0:T(8,128)(2,1)S(1)}, bf16[2,4,8,1024]{3,2,1,0:T(8,128)(2,1)S(1)}, u32[]{:S(2)}, u32[]{:S(2)}) collective-permute-start(bf16[2,4,8,1024]{3,2,1,0:T(8,128)(2,1)S(1)} %fusion.41), channel_id=1, source_target_pairs={{0,1},{1,0},{2,3},{3,2},{4,5},{5,4},{6,7},{7,6},{8,9},{9,8},{10,11... | collective-permute-start | bytes 393224 | tf_op jit(solution)/shard_map/ppermute | solution.py:58
  90.8 4.2 %collective-permute-start.11 = (bf16[256,2048]{1,0:T(8,128)(2,1)S(1)}, bf16[256,2048]{1,0:T(8,128)(2,1)S(1)}, u32[]{:S(2)}, u32[]{:S(2)}) collective-permute-start(bf16[256,2048]{1,0:T(8,128)(2,1)S(1)} %bitcast.164), channel_id=1, source_target_pairs={{0,2},{2,0},{4,6},{6,4},{8,10},{10,8},{12,14},{14,12},{16,18},{18,... | collective-permute-start | bytes 3145736 | tf_op jit(solution)/shard_map/ppermute | solution.py:25
  94.9 3.6 %fusion.2 = f32[4,2,4,8,1024]{4,3,2,1,0:T(8,128)S(1)} fusion(bf16[4,2,4,8,2048]{4,3,2,1,0:T(8,128)(2,1)S(1)} %bitcast.165, bf16[2048,1024]{1,0:T(8,128)(2,1)} %param.11), kind=kOutput, calls=%fused_computation.7 | convolution fusion | flops 1073741824 | bytes 6291456 | tf_op jit(solution)/shard_map/dot_general | solution.py:64
  98.6 3.6 %collective-permute-start.8 = (bf16[2,2,4,8,1024]{4,3,2,1,0:T(8,128)(2,1)S(1)}, bf16[2,2,4,8,1024]{4,3,2,1,0:T(8,128)(2,1)S(1)}, u32[]{:S(2)}, u32[]{:S(2)}) collective-permute-start(bf16[2,2,4,8,1024]{4,3,2,1,0:T(8,128)(2,1)S(1)} %pad_maximum_fusion.6), channel_id=1, source_target_pairs={{0,128},{128,0},{256,384},{384,256},{1,129},{129,1},{257,385},{385... | collective-permute-start | bytes 786440 | tf_op jit(solution)/shard_map/ppermute | solution.py:54
  102.3 1.3 fusion.60
  103.6 3.7 %collective-permute-start.12 = (bf16[2,2,4,8,1024]{4,3,2,1,0:T(8,128)(2,1)S(1)}, bf16[2,2,4,8,1024]{4,3,2,1,0:T(8,128)(2,1)S(1)}, u32[]{:S(2)}, u32[]{:S(2)}) collective-permute-start(bf16[2,2,4,8,1024]{4,3,2,1,0:T(8,128)(2,1)S(1)} %pad_maximum_fusion.7), channel_id=1, source_target_pairs={{0,384},{128,256},{256,128},{384,0},{1,385},{129,257},{257,129},{3... | collective-permute-start | bytes 786440 | tf_op jit(solution)/shard_map/ppermute | solution.py:54
  107.4 1.5 collective-permute-done.8
  109.0 3.7 %collective-permute-start.10 = (bf16[2,4,8,1024]{3,2,1,0:T(8,128)(2,1)S(1)}, bf16[2,4,8,1024]{3,2,1,0:T(8,128)(2,1)S(1)}, u32[]{:S(2)}, u32[]{:S(2)}) collective-permute-start(bf16[2,4,8,1024]{3,2,1,0:T(8,128)(2,1)S(1)} %fusion.45), channel_id=1, source_target_pairs={{0,384},{128,256},{256,128},{384,0},{1,385},{129,257},{257,129},{3... | collective-permute-start | bytes 393224 | tf_op jit(solution)/shard_map/ppermute | solution.py:54
  112.7 1.6 collective-permute-done.12
  114.4 1.9 collective-permute-start.13
  117.1 3.0 %collective-permute-done.13 = bf16[2,4,8,1024]{3,2,1,0:T(8,128)(2,1)S(1)} collective-permute-done((bf16[2,4,8,1024]{3,2,1,0:T(8,128)(2,1)S(1)}, bf16[2,4,8,1024]{3,2,1,0:T(8,128)(2,1)S(1)}, u32[]{:S(2)}, u32[]{:S(2)}) %collective-permute-start.13) | collective-permute-done | bytes 131104 | tf_op jit(solution)/shard_map/ppermute | solution.py:54
  120.3 4.4 %collective-permute-start.14 = (bf16[2,4,8,1024]{3,2,1,0:T(8,128)(2,1)S(1)}, bf16[2,4,8,1024]{3,2,1,0:T(8,128)(2,1)S(1)}, u32[]{:S(2)}, u32[]{:S(2)}) collective-permute-start(bf16[2,4,8,1024]{3,2,1,0:T(8,128)(2,1)S(1)} %fusion.42), channel_id=1, source_target_pairs={{0,1},{1,0},{2,3},{3,2},{4,5},{5,4},{6,7},{7,6},{8,9},{9,8},{10,11... | collective-permute-start | bytes 393224 | tf_op jit(solution)/shard_map/ppermute | solution.py:58
  124.9 5.7 %collective-permute-start.15 = (bf16[4,144,256]{2,1,0:T(8,128)(2,1)S(1)}, bf16[4,144,256]{2,1,0:T(8,128)(2,1)}, u32[]{:S(2)}, u32[]{:S(2)}) collective-permute-start(bf16[4,144,256]{2,1,0:T(8,128)(2,1)S(1)} %pad_maximum_fusion.3), channel_id=1, source_target_pairs={{0,8},{2,10},{4,12},{6,14},{8,16},{10,18},{12,20},{14,22},{16,24},... | collective-permute-start | bytes 884744 | tf_op jit(solution)/shard_map/ppermute | solution.py:50
  131.9 16.9 %all-to-all-start.2 = ((f32[64,3,128]{2,1,0:T(4,128)}), f32[64,3,128]{2,1,0:T(4,128)S(1)}, u32[]{:S(2)}, u32[]{:S(2)}) async-start(f32[64,3,128]{2,1,0:T(4,128)} %broadcast_in_dim.83), calls=%async_computation.2 | async-start | bytes 262144 | tf_op jit(solution)/shard_map/all_to_all | solution.py:203
  148.8 1.0 constant_dynamic-update-slice_fusion.1
  149.8 0.8 copy-done.3
  150.7 1.1 fusion.55
  152.5 1.2 fusion.58
  153.7 1.2 fusion.6
  154.9 1.7 divide_convert_fusion
  156.6 0.9 fusion.9
  157.5 2.1 %all-to-all-done.2 = f32[64,3,128]{2,1,0:T(4,128)S(1)} async-done(((f32[64,3,128]{2,1,0:T(4,128)}), f32[64,3,128]{2,1,0:T(4,128)S(1)}, u32[]{:S(2)}, u32[]{:S(2)}) %all-to-all-start.2) | async-done | bytes 98336 | tf_op jit(solution)/shard_map/all_to_all | solution.py:203
  160.9 5.3 %all-to-all-start.3 = ((f32[8,1,128]{2,1,0:T(1,128)}), f32[8,1,128]{2,1,0:T(1,128)S(1)}, u32[]{:S(2)}, u32[]{:S(2)}) async-start(f32[8,1,128]{2,1,0:T(1,128)} %broadcast_in_dim.86), calls=%async_computation.3 | async-start | bytes 8192 | tf_op jit(solution)/shard_map/all_to_all | solution.py:212
  166.2 2.6 %fusion.7 = bf16[1024,1152]{1,0:T(8,128)(2,1)} fusion(bf16[1024,128]{0,1:T(8,128)(2,1)S(1)} %get-tuple-element.38, bf16[1152,128]{1,0:T(8,128)(2,1)S(1)} %bitcast.161, bf16[1024,1152]{1,0:T(8,128)(2,1)S(1)} %divide_convert_fusion, f32[1024]{0:T(1024)S(1)} %fusion.9), kind=kOutput, calls=%fused_computation.12 | convolution fusion | flops 307888128 | bytes 5279744 | tf_op jit(solution)/shard_map/dot_general | solution.py:235
  168.8 6.3 %all-to-all-done.3 = f32[8,1,128]{2,1,0:T(1,128)S(1)} async-done(((f32[8,1,128]{2,1,0:T(1,128)}), f32[8,1,128]{2,1,0:T(1,128)S(1)}, u32[]{:S(2)}, u32[]{:S(2)}) %all-to-all-start.3) | async-done | bytes 4128 | tf_op jit(solution)/shard_map/all_to_all | solution.py:212
  175.7 2.4 %fusion.19 = f32[1152,128]{0,1:T(8,128)S(1)} fusion(bf16[1024,1152]{1,0:T(8,128)(2,1)} %fusion.7, bf16[1024,128]{0,1:T(8,128)(2,1)} %copy-done.2, f32[1024]{0:T(1024)S(1)} %broadcast_bitcast_fusion), kind=kOutput, calls=%fused_computation.46 | convolution fusion | flops 302383104 | bytes 3215360 | tf_op jit(solution)/shard_map/dot_general | solution.py:245
  178.2 1.0 fusion.16
  179.2 5.9 %all-to-all-start.4 = ((bf16[8,128,256]{1,2,0:T(8,128)(2,1)}), bf16[8,128,256]{1,2,0:T(8,128)(2,1)}, u32[]{:S(2)}, u32[]{:S(2)}) async-start(bf16[8,128,256]{1,2,0:T(8,128)(2,1)} %fusion.16), calls=%async_computation.4 | async-start | bytes 1048576 | tf_op jit(solution)/shard_map/all_to_all | solution.py:40
  186.4 1.9 fusion.10
  189.4 10.3 %all-to-all-done.4 = bf16[8,128,256]{1,2,0:T(8,128)(2,1)} async-done(((bf16[8,128,256]{1,2,0:T(8,128)(2,1)}), bf16[8,128,256]{1,2,0:T(8,128)(2,1)}, u32[]{:S(2)}, u32[]{:S(2)}) %all-to-all-start.4) | async-done | bytes 524320 | tf_op jit(solution)/shard_map/all_to_all | solution.py:40
  199.7 1.3 fusion.11
  201.1 1.3 collective-permute-start.16
  203.0 3.1 %collective-permute-done.16 = bf16[128,256]{0,1:T(8,128)(2,1)S(1)} collective-permute-done((bf16[128,256]{0,1:T(8,128)(2,1)S(1)}, bf16[128,256]{0,1:T(8,128)(2,1)S(1)}, u32[]{:S(2)}, u32[]{:S(2)}) %collective-permute-start.16) | collective-permute-done | bytes 65568 | tf_op jit(solution)/shard_map/ppermute | solution.py:50
  (116 shorter events, 13.3 us)
Async XLA Ops:
  0.6 28.1 %copy-start.7 = (bf16[128,1024]{1,0:T(8,128)(2,1)S(1)}, bf16[128,1024]{1,0:T(8,128)(2,1)}, u32[]{:S(2)}) copy-start(bf16[128,1024]{1,0:T(8,128)(2,1)} %param.18) | copy-start | bytes 786436
  0.6 29.5 %copy-start.10 = (f32[1024]{0:T(1024)S(1)}, f32[1024]{0:T(1024)}, u32[]{:S(2)}) copy-start(f32[1024]{0:T(1024)} %param.13) | copy-start | bytes 12292
  2.6 40.4 %all-to-all-start = ((bf16[32,8,2048]{2,1,0:T(8,128)(2,1)}), bf16[32,8,2048]{2,1,0:T(8,128)(2,1)S(1)}, u32[]{:S(2)}, u32[]{:S(2)}) async-start(bf16[32,8,2048]{2,1,0:T(8,128)(2,1)} %broadcast_in_dim.78), calls=%async_computation | async-start | bytes 2097152 | tf_op jit(solution)/shard_map/all_to_all | solution.py:34
  18.3 16.3 %collective-permute-start.1 = (bf16[1,144,256]{2,1,0:T(8,128)(2,1)S(1)}, bf16[1,144,256]{2,1,0:T(8,128)(2,1)S(1)}, u32[]{:S(2)}, u32[]{:S(2)}) collective-permute-start(bf16[1,144,256]{2,1,0:T(8,128)(2,1)S(1)} %maximum_bitcast_fusion), channel_id=1, source_target_pairs={{0,2},{2,4},{4,6},{6,8},{8,10},{10,12},{12,14},{14,16},{16,18},{18... | collective-permute-start | bytes 221192 | tf_op jit(solution)/shard_map/ppermute | solution.py:50
  22.6 17.8 %collective-permute-start = (bf16[1,144,256]{2,1,0:T(8,128)(2,1)S(1)}, bf16[1,144,256]{2,1,0:T(8,128)(2,1)S(1)}, u32[]{:S(2)}, u32[]{:S(2)}) collective-permute-start(bf16[1,144,256]{2,1,0:T(8,128)(2,1)S(1)} %maximum_bitcast_fusion), channel_id=1, source_target_pairs={{0,16},{2,18},{4,20},{6,22},{8,24},{10,26},{12,28},{14,30},{16,32}... | collective-permute-start | bytes 221192 | tf_op jit(solution)/shard_map/ppermute | solution.py:50
  29.9 122.1 %copy-start.2 = (bf16[1024,128]{0,1:T(8,128)(2,1)}, bf16[1024,128]{0,1:T(8,128)(2,1)S(1)}, u32[]{:S(2)}) copy-start(bf16[1024,128]{0,1:T(8,128)(2,1)S(1)} %get-tuple-element.37) | copy-start | bytes 786436
  40.4 3.6 %copy-start.8 = (bf16[1,144,256]{2,1,0:T(8,128)(2,1)}, bf16[1,144,256]{2,1,0:T(8,128)(2,1)S(1)}, u32[]{:S(2)}) copy-start(bf16[1,144,256]{2,1,0:T(8,128)(2,1)S(1)} %collective-permute-done) | copy-start | bytes 221188
  44.0 41.9 %all-to-all-start.1 = ((bf16[32,8,2048]{2,1,0:T(8,128)(2,1)}), bf16[32,8,2048]{2,1,0:T(8,128)(2,1)S(1)}, u32[]{:S(2)}, u32[]{:S(2)}) async-start(bf16[32,8,2048]{2,1,0:T(8,128)(2,1)} %broadcast_in_dim.79), calls=%async_computation.1 | async-start | bytes 2097152 | tf_op jit(solution)/shard_map/all_to_all | solution.py:34
  52.7 10.7 %collective-permute-start.4 = (bf16[256,2048]{1,0:T(8,128)(2,1)S(1)}, bf16[256,2048]{1,0:T(8,128)(2,1)S(1)}, u32[]{:S(2)}, u32[]{:S(2)}) collective-permute-start(bf16[256,2048]{1,0:T(8,128)(2,1)S(1)} %bitcast.162), channel_id=1, source_target_pairs={{0,2},{2,0},{4,6},{6,4},{8,10},{10,8},{12,14},{14,12},{16,18},{18,... | collective-permute-start | bytes 3145736 | tf_op jit(solution)/shard_map/ppermute | solution.py:25
  55.8 7.6 %copy-start.11 = (bf16[2048,1024]{1,0:T(8,128)(2,1)S(1)}, bf16[2048,1024]{1,0:T(8,128)(2,1)}, u32[]{:S(2)}) copy-start(bf16[2048,1024]{1,0:T(8,128)(2,1)} %param.11) | copy-start | bytes 12582916
  59.4 5.3 %copy-start.4 = (f32[4,2,4,8,1024]{4,3,2,1,0:T(8,128)}, f32[4,2,4,8,1024]{4,3,2,1,0:T(8,128)S(1)}, u32[]{:S(2)}) copy-start(f32[4,2,4,8,1024]{4,3,2,1,0:T(8,128)S(1)} %fusion.4) | copy-start | bytes 3145732
  60.2 10.0 %collective-permute-start.2 = (bf16[2,2,4,8,1024]{4,3,2,1,0:T(8,128)(2,1)}, bf16[2,2,4,8,1024]{4,3,2,1,0:T(8,128)(2,1)S(1)}, u32[]{:S(2)}, u32[]{:S(2)}) collective-permute-start(bf16[2,2,4,8,1024]{4,3,2,1,0:T(8,128)(2,1)} %pad_maximum_fusion.4), channel_id=1, source_target_pairs={{0,128},{128,0},{256,384},{384,256},{1,129},{129,1},{257,385},{385... | collective-permute-start | bytes 786440 | tf_op jit(solution)/shard_map/ppermute | solution.py:54
  64.7 1.0 copy-start.5
  65.7 10.7 %collective-permute-start.5 = (bf16[2,2,4,8,1024]{4,3,2,1,0:T(8,128)(2,1)S(1)}, bf16[2,2,4,8,1024]{4,3,2,1,0:T(8,128)(2,1)S(1)}, u32[]{:S(2)}, u32[]{:S(2)}) collective-permute-start(bf16[2,2,4,8,1024]{4,3,2,1,0:T(8,128)(2,1)S(1)} %pad_maximum_fusion.5), channel_id=1, source_target_pairs={{0,384},{128,256},{256,128},{384,0},{1,385},{129,257},{257,129},{3... | collective-permute-start | bytes 786440 | tf_op jit(solution)/shard_map/ppermute | solution.py:54
  71.3 8.1 %collective-permute-start.3 = (bf16[2,4,8,1024]{3,2,1,0:T(8,128)(2,1)S(1)}, bf16[2,4,8,1024]{3,2,1,0:T(8,128)(2,1)S(1)}, u32[]{:S(2)}, u32[]{:S(2)}) collective-permute-start(bf16[2,4,8,1024]{3,2,1,0:T(8,128)(2,1)S(1)} %fusion.43), channel_id=1, source_target_pairs={{0,384},{128,256},{256,128},{384,0},{1,385},{129,257},{257,129},{3... | collective-permute-start | bytes 393224 | tf_op jit(solution)/shard_map/ppermute | solution.py:54
  77.5 6.4 %collective-permute-start.6 = (bf16[2,4,8,1024]{3,2,1,0:T(8,128)(2,1)S(1)}, bf16[2,4,8,1024]{3,2,1,0:T(8,128)(2,1)S(1)}, u32[]{:S(2)}, u32[]{:S(2)}) collective-permute-start(bf16[2,4,8,1024]{3,2,1,0:T(8,128)(2,1)S(1)} %fusion.44), channel_id=1, source_target_pairs={{0,128},{128,0},{256,384},{384,256},{1,129},{129,1},{257,385},{385... | collective-permute-start | bytes 393224 | tf_op jit(solution)/shard_map/ppermute | solution.py:54
  80.4 5.5 %collective-permute-start.7 = (bf16[2,144,256]{2,1,0:T(8,128)(2,1)S(1)}, bf16[2,144,256]{2,1,0:T(8,128)(2,1)S(1)}, u32[]{:S(2)}, u32[]{:S(2)}) collective-permute-start(bf16[2,144,256]{2,1,0:T(8,128)(2,1)S(1)} %pad_maximum_fusion.8), channel_id=1, source_target_pairs={{0,4},{2,6},{4,8},{6,10},{8,12},{10,14},{12,16},{14,18},{16,20},{1... | collective-permute-start | bytes 442376 | tf_op jit(solution)/shard_map/ppermute | solution.py:50
  86.0 21.4 %collective-permute-start.9 = (bf16[2,4,8,1024]{3,2,1,0:T(8,128)(2,1)S(1)}, bf16[2,4,8,1024]{3,2,1,0:T(8,128)(2,1)S(1)}, u32[]{:S(2)}, u32[]{:S(2)}) collective-permute-start(bf16[2,4,8,1024]{3,2,1,0:T(8,128)(2,1)S(1)} %fusion.41), channel_id=1, source_target_pairs={{0,1},{1,0},{2,3},{3,2},{4,5},{5,4},{6,7},{7,6},{8,9},{9,8},{10,11... | collective-permute-start | bytes 393224 | tf_op jit(solution)/shard_map/ppermute | solution.py:58
  90.8 11.5 %collective-permute-start.11 = (bf16[256,2048]{1,0:T(8,128)(2,1)S(1)}, bf16[256,2048]{1,0:T(8,128)(2,1)S(1)}, u32[]{:S(2)}, u32[]{:S(2)}) collective-permute-start(bf16[256,2048]{1,0:T(8,128)(2,1)S(1)} %bitcast.164), channel_id=1, source_target_pairs={{0,2},{2,0},{4,6},{6,4},{8,10},{10,8},{12,14},{14,12},{16,18},{18,... | collective-permute-start | bytes 3145736 | tf_op jit(solution)/shard_map/ppermute | solution.py:25
  94.9 7.3 %copy-start.12 = (bf16[2048,1024]{1,0:T(8,128)(2,1)S(1)}, bf16[2048,1024]{1,0:T(8,128)(2,1)}, u32[]{:S(2)}) copy-start(bf16[2048,1024]{1,0:T(8,128)(2,1)} %param.11) | copy-start | bytes 12582916
  98.6 10.3 %collective-permute-start.8 = (bf16[2,2,4,8,1024]{4,3,2,1,0:T(8,128)(2,1)S(1)}, bf16[2,2,4,8,1024]{4,3,2,1,0:T(8,128)(2,1)S(1)}, u32[]{:S(2)}, u32[]{:S(2)}) collective-permute-start(bf16[2,2,4,8,1024]{4,3,2,1,0:T(8,128)(2,1)S(1)} %pad_maximum_fusion.6), channel_id=1, source_target_pairs={{0,128},{128,0},{256,384},{384,256},{1,129},{129,1},{257,385},{385... | collective-permute-start | bytes 786440 | tf_op jit(solution)/shard_map/ppermute | solution.py:54
  103.5 21.3 %copy-start.9 = (bf16[1,144,256]{2,1,0:T(8,128)(2,1)S(1)}, bf16[1,144,256]{2,1,0:T(8,128)(2,1)}, u32[]{:S(2)}) copy-start(bf16[1,144,256]{2,1,0:T(8,128)(2,1)} %copy-done.8) | copy-start | bytes 221188
  103.6 10.7 %collective-permute-start.12 = (bf16[2,2,4,8,1024]{4,3,2,1,0:T(8,128)(2,1)S(1)}, bf16[2,2,4,8,1024]{4,3,2,1,0:T(8,128)(2,1)S(1)}, u32[]{:S(2)}, u32[]{:S(2)}) collective-permute-start(bf16[2,2,4,8,1024]{4,3,2,1,0:T(8,128)(2,1)S(1)} %pad_maximum_fusion.7), channel_id=1, source_target_pairs={{0,384},{128,256},{256,128},{384,0},{1,385},{129,257},{257,129},{3... | collective-permute-start | bytes 786440 | tf_op jit(solution)/shard_map/ppermute | solution.py:54
  109.0 8.1 %collective-permute-start.10 = (bf16[2,4,8,1024]{3,2,1,0:T(8,128)(2,1)S(1)}, bf16[2,4,8,1024]{3,2,1,0:T(8,128)(2,1)S(1)}, u32[]{:S(2)}, u32[]{:S(2)}) collective-permute-start(bf16[2,4,8,1024]{3,2,1,0:T(8,128)(2,1)S(1)} %fusion.45), channel_id=1, source_target_pairs={{0,384},{128,256},{256,128},{384,0},{1,385},{129,257},{257,129},{3... | collective-permute-start | bytes 393224 | tf_op jit(solution)/shard_map/ppermute | solution.py:54
  114.4 5.7 %collective-permute-start.13 = (bf16[2,4,8,1024]{3,2,1,0:T(8,128)(2,1)S(1)}, bf16[2,4,8,1024]{3,2,1,0:T(8,128)(2,1)S(1)}, u32[]{:S(2)}, u32[]{:S(2)}) collective-permute-start(bf16[2,4,8,1024]{3,2,1,0:T(8,128)(2,1)S(1)} %fusion.46), channel_id=1, source_target_pairs={{0,128},{128,0},{256,384},{384,256},{1,129},{129,1},{257,385},{385... | collective-permute-start | bytes 393224 | tf_op jit(solution)/shard_map/ppermute | solution.py:54
  120.3 10.3 %collective-permute-start.14 = (bf16[2,4,8,1024]{3,2,1,0:T(8,128)(2,1)S(1)}, bf16[2,4,8,1024]{3,2,1,0:T(8,128)(2,1)S(1)}, u32[]{:S(2)}, u32[]{:S(2)}) collective-permute-start(bf16[2,4,8,1024]{3,2,1,0:T(8,128)(2,1)S(1)} %fusion.42), channel_id=1, source_target_pairs={{0,1},{1,0},{2,3},{3,2},{4,5},{5,4},{6,7},{7,6},{8,9},{9,8},{10,11... | collective-permute-start | bytes 393224 | tf_op jit(solution)/shard_map/ppermute | solution.py:58
  124.9 23.9 %collective-permute-start.15 = (bf16[4,144,256]{2,1,0:T(8,128)(2,1)S(1)}, bf16[4,144,256]{2,1,0:T(8,128)(2,1)}, u32[]{:S(2)}, u32[]{:S(2)}) collective-permute-start(bf16[4,144,256]{2,1,0:T(8,128)(2,1)S(1)} %pad_maximum_fusion.3), channel_id=1, source_target_pairs={{0,8},{2,10},{4,12},{6,14},{8,16},{10,18},{12,20},{14,22},{16,24},... | collective-permute-start | bytes 884744 | tf_op jit(solution)/shard_map/ppermute | solution.py:50
  131.9 27.7 %all-to-all-start.2 = ((f32[64,3,128]{2,1,0:T(4,128)}), f32[64,3,128]{2,1,0:T(4,128)S(1)}, u32[]{:S(2)}, u32[]{:S(2)}) async-start(f32[64,3,128]{2,1,0:T(4,128)} %broadcast_in_dim.83), calls=%async_computation.2 | async-start | bytes 262144 | tf_op jit(solution)/shard_map/all_to_all | solution.py:203
  149.8 0.8 copy-start.3
  151.8 0.7 copy-start.1
  156.6 18.4 %copy-start.6 = (pred[128,1024]{1,0:T(8,128)(4,1)S(1)}, pred[128,1024]{1,0:T(8,128)(4,1)}, u32[]{:S(2)}) copy-start(pred[128,1024]{1,0:T(8,128)(4,1)} %broadcast_compare_fusion) | copy-start | bytes 393220
  160.9 14.1 %all-to-all-start.3 = ((f32[8,1,128]{2,1,0:T(1,128)}), f32[8,1,128]{2,1,0:T(1,128)S(1)}, u32[]{:S(2)}, u32[]{:S(2)}) async-start(f32[8,1,128]{2,1,0:T(1,128)} %broadcast_in_dim.86), calls=%async_computation.3 | async-start | bytes 8192 | tf_op jit(solution)/shard_map/all_to_all | solution.py:212
  175.7 10.7 %copy-start = (bf16[1024,1152]{1,0:T(8,128)(2,1)S(1)}, bf16[1024,1152]{1,0:T(8,128)(2,1)}, u32[]{:S(2)}) copy-start(bf16[1024,1152]{1,0:T(8,128)(2,1)} %fusion.7) | copy-start | bytes 7077892
  179.2 20.5 %all-to-all-start.4 = ((bf16[8,128,256]{1,2,0:T(8,128)(2,1)}), bf16[8,128,256]{1,2,0:T(8,128)(2,1)}, u32[]{:S(2)}, u32[]{:S(2)}) async-start(bf16[8,128,256]{1,2,0:T(8,128)(2,1)} %fusion.16), calls=%async_computation.4 | async-start | bytes 1048576 | tf_op jit(solution)/shard_map/all_to_all | solution.py:40
  201.1 5.0 %collective-permute-start.16 = (bf16[128,256]{0,1:T(8,128)(2,1)S(1)}, bf16[128,256]{0,1:T(8,128)(2,1)S(1)}, u32[]{:S(2)}, u32[]{:S(2)}) collective-permute-start(bf16[128,256]{0,1:T(8,128)(2,1)S(1)} %get-tuple-element.73), channel_id=1, source_target_pairs={{16,0},{18,2},{20,4},{22,6},{24,8},{26,10},{28,12},{30,14},{32,16}... | collective-permute-start | bytes 196616 | tf_op jit(solution)/shard_map/ppermute | solution.py:50

commit v5 on v3

--- a/solution.py
+++ b/solution.py
@@ -3,8 +3,6 @@
 import jax
 import jax.numpy as jnp
 from jax import lax
-from jax.experimental import pallas as pl
-from jax.experimental.pallas import tpu as pltpu
 from jax.sharding import PartitionSpec as P
 
 advantage_scale = 0.1
@@ -62,43 +60,20 @@
     return lax.ppermute(block, "tp", [(0, 1), (1, 0)])
 
 
-def logits_kernel(section_ref, mine_ref, theirs_ref, head_ref, *refs):
-    outs, logits = refs[:SECTIONS], refs[SECTIONS]
-    count = outs[0].shape[1]
-    for part, rows in enumerate((mine_ref, theirs_ref)):
-        logits[part] = jnp.dot(rows[...], head_ref[...], preferred_element_type=jnp.float32)
-        for step, out in enumerate(outs):
-            place = lax.rem(section_ref[0] + step, SECTIONS)
-            kept = logits[part, pl.ds(pl.multiple_of(place * count, count), count), :]
-            out[part] = kept.astype(out.dtype)
-
-
 def section_parts(gathered, weight, section):
     mine = gathered.reshape(-1, gathered.shape[2])
-    rows, depth = mine.shape
-    vocab, tile = weight.shape[1], 256
-    count = rows // SECTIONS
-    whole = pl.BlockSpec((rows, depth), lambda n: (0, 0))
-    kinds = [jnp.float32] + [jnp.bfloat16] * (SECTIONS - 1)
-    return pl.pallas_call(
-        logits_kernel,
-        grid=(vocab // tile,),
-        in_specs=[
-            pl.BlockSpec(memory_space=pltpu.SMEM),
-            whole,
-            whole,
-            pl.BlockSpec((depth, tile), lambda n: (0, n)),
-        ],
-        out_specs=[pl.BlockSpec((2, count, tile), lambda n: (0, 0, n))] * SECTIONS,
-        out_shape=[jax.ShapeDtypeStruct((2, count, vocab), kind) for kind in kinds],
-        scratch_shapes=[pltpu.VMEM((2, rows, tile), jnp.float32)],
-        compiler_params=pltpu.CompilerParams(vmem_limit_bytes=24 * 1024 * 1024),
-        cost_estimate=pl.CostEstimate(
-            flops=4 * rows * depth * vocab,
-            bytes_accessed=2 * depth * vocab + 4 * rows * depth + 5 * rows * vocab,
-            transcendentals=0,
-        ),
-    )(jnp.reshape(section, (1,)), mine, other_core(mine), weight)
+    parts = []
+    for rows in (mine, other_core(mine)):
+        part = jnp.dot(rows, weight, preferred_element_type=jnp.float32)
+        parts.append(part.reshape(SECTIONS, TPS, Y, gathered.shape[1], weight.shape[1]))
+
+    def rows_for(step):
+        place = lax.rem(section + step, SECTIONS)
+        return jnp.stack(
+            [lax.dynamic_index_in_dim(part, place, 0, keepdims=False) for part in parts]
+        )
+
+    return [rows_for(0)] + [rows_for(step).astype(jnp.bfloat16) for step in (1, 2, 3)]
 
 
 def section_arrivals(parts):
@@ -110,9 +85,8 @@
 
 
 def tp_halves(total, tp):
-    halves = total.reshape(2, TPS, -1, total.shape[2])
-    keep = lax.dynamic_index_in_dim(halves, tp, 1, keepdims=False)
-    give = lax.dynamic_index_in_dim(halves, 1 - tp, 1, keepdims=False)
+    keep = lax.dynamic_index_in_dim(total, tp, 1, keepdims=False)
+    give = lax.dynamic_index_in_dim(total, 1 - tp, 1, keepdims=False)
     return keep, give.astype(jnp.bfloat16)
 
 
@@ -173,13 +147,16 @@
     arrivals = section_arrivals(first)
     arrivals[2], two_windows = lax.optimization_barrier((arrivals[2], two_windows))
     four_windows = jnp.concatenate([passed_along(two_windows, 2), two_windows], axis=0)
-    first, last = lax.optimization_barrier((section_sums(first[0], arrivals), last))
+    first, last, four_windows = lax.optimization_barrier(
+        (section_sums(first[0], arrivals), last, four_windows)
+    )
     keep, give = tp_halves(first, tp)
     last = section_parts(last, lm_head, section)
     give, last = lax.optimization_barrier((give, last))
-    arrivals = section_arrivals(last)
     first = tp_sums(keep, give)
-    last, four_windows = lax.optimization_barrier((section_sums(last[0], arrivals), four_windows))
+    last, four_windows = lax.optimization_barrier(
+        (section_sums(last[0], section_arrivals(last)), four_windows)
+    )
     last = tp_sums(*tp_halves(last, tp))
     window = jnp.concatenate([eighth, passed_along(four_windows, 4), four_windows], axis=0)
 
@@ -189,9 +166,7 @@
             rows, section * TPS + tp, 0, keepdims=False
         ).transpose(1, 0, 2, 3)
 
-    logits = jnp.stack(
-        [part.reshape(CORES, Y, half, -1) for part in (first, last)], axis=2
-    )
+    logits = jnp.stack([first, last], axis=2)
     columns = ctx_index * lm_head.shape[1] + jnp.arange(lm_head.shape[1], dtype=jnp.int32)
     stats = row_stats(logits, columns, cores_exchanged(kept_rows(sampled_ids), 0, core))
     stats = cores_exchanged(stats, 1, core).reshape(3, -1)
@@ -264,22 +239,21 @@
     both = jnp.concatenate([grad_key, grad_value], axis=1).reshape(
         FARTHEST + 1, seq_rows, 2 * head_dim
     )
-    d_queries = (
-        grad_query.reshape(group, seq_rows, head_dim)
-        .transpose(1, 0, 2)
-        .reshape(seq_rows, group * head_dim)
-    )
     cyclic = both[1:].astype(jnp.bfloat16)
     cyclic = jnp.concatenate([cyclic, cyclic], axis=0)
     given = lax.dynamic_slice_in_dim(cyclic, Y * CORES - 1 - place, Y * CORES, 0)
-    arrived, d_queries = lax.optimization_barrier((across_row(given), d_queries))
-    arrived = arrived.astype(jnp.float32)
+    arrived = across_row(given).astype(jnp.float32)
     sender = jnp.arange(Y * CORES, dtype=jnp.int32)[:, None, None]
     back = both[0] + jnp.sum(jnp.where(sender < place, arrived, 0.0), axis=0)
     back = passed_along(back.astype(jnp.bfloat16), -Y * CORES).astype(jnp.float32)
     here = both[FARTHEST] + jnp.sum(jnp.where(sender > place, arrived, 0.0), axis=0)
     d_keys = (here[:, :head_dim] + back[:, :head_dim]).astype(jnp.bfloat16)
     d_values = (here[:, head_dim:] + back[:, head_dim:]).astype(jnp.bfloat16)
+    d_queries = (
+        grad_query.reshape(group, seq_rows, head_dim)
+        .transpose(1, 0, 2)
+        .reshape(seq_rows, group * head_dim)
+    )
     return (advantage_own, d_queries, d_keys, d_values)
 
 

time: 212 us -> 202 us (0.953)
  local copies, waits for them, and re-layouts: 23.2 us -> 13.3 us
  matrix products: 10 us -> 19.2 us
  Pallas kernels: 7.46 us -> 0 us
  waiting for transfers between devices: 58.3 us -> 55.6 us
  starting transfers between devices: 95.2 us -> 97.4 us
    dot_general x0 -> x4, matrix products: none -> 11.3 us  [section_parts(): part = jnp.dot(rows, weight, preferred_element_type=jnp.float32)]
    pallas_call x2 -> x0, Pallas kernels: 7.46 us -> none  [section_parts(): pl.pallas_call(logits_kernel, grid=(vocab // tile,), in_specs=[pl.BlockSp...]
    unnamed x48 -> x35, local copies, waits for them, and re-layouts: 10.8 us -> 3.52 us
    all_to_all x1, starting transfers between devices: 9.68 us -> 16 us  [body(): lax.all_to_all(jnp.broadcast_to(stats, (Z * Y * CORES,) + stats.shape), '...]
    ppermute x5, waiting for transfers between devices: 17.3 us -> 13.5 us  [passed_along(): return lax.ppermute(block, 'ctx', route)]
    ppermute x5, starting transfers between devices: 19 us -> 15.2 us  [passed_along(): return lax.ppermute(block, 'ctx', route)]
    another operation x3 -> x10, other arithmetic: 0.72 us -> 4.4 us  [the longest x7 3.69 us: rows_for(): jnp.stack([lax.dynamic_index_in_dim(part, place, 0, keepdims=False) for p...]
    ppermute x2, waiting for transfers between devices: 4.04 us -> 0.56 us  [to_other_tp(): return lax.ppermute(block, 'tp', [(0, 1), (1, 0)])]
  transfers between devices with their start and end apart: 20 -> 20, of which waited for: 11 -> 12; matrix products, arithmetic and copies ran while one was open for 16% -> 16% of each run, Pallas kernels for 4% -> 0%
where the time goes in v5:
time: 202 us; the launch traced here: 201 us
  starting transfers between devices  97.4 us (48%)
  waiting for transfers between devices  55.6 us (28%)
  matrix products  19.2 us (10%)
  other arithmetic  13.6 us (7%)
  local copies, waits for them, and re-layouts  13.3 us (7%)
    all_to_all x2, starting transfers between devices, across_chips(): return lax.all_to_all(copies, 'ctx', 0, 0, axis_index_groups=groups)  19.8 us
    ppermute x6, starting transfers between devices, along_section(): lax.ppermute(block, 'section', [(s, (s + step) % SECTIONS) for s in range...  18.9 us
    all_to_all x1, starting transfers between devices, body(): lax.all_to_all(jnp.broadcast_to(stats, (Z * Y * CORES,) + stats.shape), '...  16 us
    ppermute x6, waiting for transfers between devices, along_section(): lax.ppermute(block, 'section', [(s, (s + step) % SECTIONS) for s in range...  15.4 us
    ppermute x5, starting transfers between devices, passed_along(): return lax.ppermute(block, 'ctx', route)  15.2 us
    all_to_all x1, waiting for transfers between devices, across_row(): return lax.all_to_all(blocks, 'ctx', 0, 0, axis_index_groups=groups)  13.7 us
    ppermute x5, waiting for transfers between devices, passed_along(): return lax.ppermute(block, 'ctx', route)  13.5 us
    dot_general x4, matrix products, section_parts(): part = jnp.dot(rows, weight, preferred_element_type=jnp.float32)  11.3 us
  transfers between devices with their start and end apart: 20, of which 12 were waited for; matrix products, arithmetic and copies ran while one was open for 16% of the time, Pallas kernels for 0%

profile of v5, /device:TPU:1, one launch (start us, length us, event | category | flops | bytes accessed | tf_op | source)
XLA Modules:
  0.0 200.6 jit_solution(9115536651672814844)
XLA Ops:
  0.6 0.8 fusion.49
  1.4 1.1 broadcast_in_dim.78
  2.5 14.3 %all-to-all-start = ((bf16[32,8,2048]{2,1,0:T(8,128)(2,1)}), bf16[32,8,2048]{2,1,0:T(8,128)(2,1)S(1)}, u32[]{:S(2)}, u32[]{:S(2)}) async-start(bf16[32,8,2048]{2,1,0:T(8,128)(2,1)} %broadcast_in_dim.78), calls=%async_computation | async-start | bytes 2097152 | tf_op jit(solution)/shard_map/all_to_all | solution.py:36
  16.8 0.7 convert.43
  18.0 0.8 maximum_bitcast_fusion
  18.8 3.1 %collective-permute-start = (bf16[1,144,256]{2,1,0:T(8,128)(2,1)S(1)}, bf16[1,144,256]{2,1,0:T(8,128)(2,1)S(1)}, u32[]{:S(2)}, u32[]{:S(2)}) collective-permute-start(bf16[1,144,256]{2,1,0:T(8,128)(2,1)S(1)} %maximum_bitcast_fusion), channel_id=1, source_target_pairs={{0,16},{2,18},{4,20},{6,22},{8,24},{10,26},{12,28},{14,30},{16,32}... | collective-permute-start | bytes 221192 | tf_op jit(solution)/shard_map/ppermute | solution.py:52
  21.9 4.5 %collective-permute-start.1 = (bf16[1,144,256]{2,1,0:T(8,128)(2,1)S(1)}, bf16[1,144,256]{2,1,0:T(8,128)(2,1)S(1)}, u32[]{:S(2)}, u32[]{:S(2)}) collective-permute-start(bf16[1,144,256]{2,1,0:T(8,128)(2,1)S(1)} %maximum_bitcast_fusion), channel_id=1, source_target_pairs={{0,2},{2,4},{4,6},{6,8},{8,10},{10,12},{12,14},{14,16},{16,18},{18... | collective-permute-start | bytes 221192 | tf_op jit(solution)/shard_map/ppermute | solution.py:52
  26.4 0.8 reshape.211
  27.3 7.2 %collective-permute-done.1 = bf16[1,144,256]{2,1,0:T(8,128)(2,1)S(1)} collective-permute-done((bf16[1,144,256]{2,1,0:T(8,128)(2,1)S(1)}, bf16[1,144,256]{2,1,0:T(8,128)(2,1)S(1)}, u32[]{:S(2)}, u32[]{:S(2)}) %collective-permute-start.1) | collective-permute-done | bytes 73760 | tf_op jit(solution)/shard_map/ppermute | solution.py:52
  34.6 5.8 %collective-permute-done = bf16[1,144,256]{2,1,0:T(8,128)(2,1)S(1)} collective-permute-done((bf16[1,144,256]{2,1,0:T(8,128)(2,1)S(1)}, bf16[1,144,256]{2,1,0:T(8,128)(2,1)S(1)}, u32[]{:S(2)}, u32[]{:S(2)}) %collective-permute-start) | collective-permute-done | bytes 73760 | tf_op jit(solution)/shard_map/ppermute | solution.py:52
  40.4 2.5 %all-to-all-done = bf16[32,8,2048]{2,1,0:T(8,128)(2,1)S(1)} async-done(((bf16[32,8,2048]{2,1,0:T(8,128)(2,1)}), bf16[32,8,2048]{2,1,0:T(8,128)(2,1)S(1)}, u32[]{:S(2)}, u32[]{:S(2)}) %all-to-all-start) | async-done | bytes 1048608 | tf_op jit(solution)/shard_map/all_to_all | solution.py:36
  42.9 1.1 broadcast_in_dim.79
  44.0 5.9 %collective-permute-start.2 = (bf16[256,2048]{1,0:T(8,128)(2,1)S(1)}, bf16[256,2048]{1,0:T(8,128)(2,1)}, u32[]{:S(2)}, u32[]{:S(2)}) collective-permute-start(bf16[256,2048]{1,0:T(8,128)(2,1)S(1)} %bitcast.170), channel_id=1, source_target_pairs={{0,2},{2,0},{4,6},{6,4},{8,10},{10,8},{12,14},{14,12},{16,18},{18,... | collective-permute-start | bytes 3145736 | tf_op jit(solution)/shard_map/ppermute | solution.py:27
  49.9 5.5 %all-to-all-start.1 = ((bf16[32,8,2048]{2,1,0:T(8,128)(2,1)}), bf16[32,8,2048]{2,1,0:T(8,128)(2,1)S(1)}, u32[]{:S(2)}, u32[]{:S(2)}) async-start(bf16[32,8,2048]{2,1,0:T(8,128)(2,1)} %broadcast_in_dim.79), calls=%async_computation.1 | async-start | bytes 2097152 | tf_op jit(solution)/shard_map/all_to_all | solution.py:36
  55.4 3.6 %fusion.5 = f32[4,2,4,8,1024]{4,3,2,1,0:T(8,128)S(1)} fusion(bf16[4,2,4,8,2048]{4,3,2,1,0:T(8,128)(2,1)S(1)} %bitcast.171, bf16[2048,1024]{1,0:T(8,128)(2,1)} %param.11), kind=kOutput, calls=%fused_computation.11 | convolution fusion | flops 1073741824 | bytes 6291456 | tf_op jit(solution)/shard_map/dot_general | solution.py:67
  59.0 2.9 %fusion.50 = f32[256,1024]{1,0:T(8,128)S(1)} fusion(bf16[256,2048]{1,0:T(8,128)(2,1)} %collective-permute-done.2, bf16[2048,1024]{1,0:T(8,128)(2,1)S(1)} %copy-done.11), kind=kOutput, calls=%fused_computation.133 | convolution fusion | flops 1073741824 | bytes 6291456 | tf_op jit(solution)/shard_map/dot_general | solution.py:67
  62.1 0.7 pad_maximum_fusion.5
  62.8 4.4 %collective-permute-start.5 = (bf16[2,2,4,8,1024]{4,3,2,1,0:T(8,128)(2,1)}, bf16[2,2,4,8,1024]{4,3,2,1,0:T(8,128)(2,1)S(1)}, u32[]{:S(2)}, u32[]{:S(2)}) collective-permute-start(bf16[2,2,4,8,1024]{4,3,2,1,0:T(8,128)(2,1)} %pad_maximum_fusion.5), channel_id=1, source_target_pairs={{0,384},{128,0},{256,128},{384,256},{1,385},{129,1},{257,129},{385... | collective-permute-start | bytes 786440 | tf_op jit(solution)/shard_map/ppermute | solution.py:56
  67.2 2.4 %collective-permute-start.4 = (bf16[2,2,4,8,1024]{4,3,2,1,0:T(8,128)(2,1)S(1)}, bf16[2,2,4,8,1024]{4,3,2,1,0:T(8,128)(2,1)S(1)}, u32[]{:S(2)}, u32[]{:S(2)}) collective-permute-start(bf16[2,2,4,8,1024]{4,3,2,1,0:T(8,128)(2,1)S(1)} %pad_maximum_fusion.4), channel_id=1, source_target_pairs={{0,256},{128,384},{256,0},{384,128},{1,257},{129,385},{257,1},{385... | collective-permute-start | bytes 786440 | tf_op jit(solution)/shard_map/ppermute | solution.py:56
  69.7 0.7 pad_maximum_fusion.3
  70.4 2.5 %collective-permute-start.3 = (bf16[2,2,4,8,1024]{4,3,2,1,0:T(8,128)(2,1)}, bf16[2,2,4,8,1024]{4,3,2,1,0:T(8,128)(2,1)S(1)}, u32[]{:S(2)}, u32[]{:S(2)}) collective-permute-start(bf16[2,2,4,8,1024]{4,3,2,1,0:T(8,128)(2,1)} %pad_maximum_fusion.3), channel_id=1, source_target_pairs={{0,128},{128,256},{256,384},{384,0},{1,129},{129,257},{257,385},{3... | collective-permute-start | bytes 786440 | tf_op jit(solution)/shard_map/ppermute | solution.py:56
  73.1 1.0 constant_dynamic-slice_fusion.1
  74.1 4.3 %collective-permute-done.5 = bf16[2,2,4,8,1024]{4,3,2,1,0:T(8,128)(2,1)S(1)} collective-permute-done((bf16[2,2,4,8,1024]{4,3,2,1,0:T(8,128)(2,1)}, bf16[2,2,4,8,1024]{4,3,2,1,0:T(8,128)(2,1)S(1)}, u32[]{:S(2)}, u32[]{:S(2)}) %collective-permute-start.5) | collective-permute-done | bytes 262176 | tf_op jit(solution)/shard_map/ppermute | solution.py:56
  78.4 1.3 collective-permute-start.6
  79.7 4.8 %collective-permute-done.3 = bf16[2,2,4,8,1024]{4,3,2,1,0:T(8,128)(2,1)S(1)} collective-permute-done((bf16[2,2,4,8,1024]{4,3,2,1,0:T(8,128)(2,1)}, bf16[2,2,4,8,1024]{4,3,2,1,0:T(8,128)(2,1)S(1)}, u32[]{:S(2)}, u32[]{:S(2)}) %collective-permute-start.3) | collective-permute-done | bytes 262176 | tf_op jit(solution)/shard_map/ppermute | solution.py:56
  84.7 3.0 %collective-permute-start.7 = (bf16[256,2048]{1,0:T(8,128)(2,1)S(1)}, bf16[256,2048]{1,0:T(8,128)(2,1)S(1)}, u32[]{:S(2)}, u32[]{:S(2)}) collective-permute-start(bf16[256,2048]{1,0:T(8,128)(2,1)S(1)} %bitcast.172), channel_id=1, source_target_pairs={{0,2},{2,0},{4,6},{6,4},{8,10},{10,8},{12,14},{14,12},{16,18},{18,... | collective-permute-start | bytes 3145736 | tf_op jit(solution)/shard_map/ppermute | solution.py:27
  87.7 0.6 broadcast_compare_fusion
  88.3 3.6 %fusion.3 = f32[4,2,4,8,1024]{4,3,2,0,1:T(8,128)S(1)} fusion(bf16[2048,1024]{1,0:T(8,128)(2,1)} %param.11, bf16[4,2,4,8,2048]{4,3,2,1,0:T(8,128)(2,1)S(1)} %bitcast.173), kind=kOutput, calls=%fused_computation.9 | convolution fusion | flops 1073741824 | bytes 6291456 | tf_op jit(solution)/shard_map/dot_general | solution.py:67
  92.0 1.3 fusion.51
  93.5 0.7 pad_maximum_fusion.6
  94.2 0.7 pad_maximum_fusion.7
  94.9 0.7 pad_maximum_fusion.8
  95.6 5.2 %collective-permute-start.11 = (bf16[2,2,4,8,1024]{4,3,2,0,1:T(8,128)(2,1)}, bf16[2,2,4,8,1024]{4,3,2,0,1:T(8,128)(2,1)S(1)}, u32[]{:S(2)}, u32[]{:S(2)}) collective-permute-start(bf16[2,2,4,8,1024]{4,3,2,0,1:T(8,128)(2,1)} %pad_maximum_fusion.8), channel_id=1, source_target_pairs={{0,384},{128,0},{256,128},{384,256},{1,385},{129,1},{257,129},{385... | collective-permute-start | bytes 786440 | tf_op jit(solution)/shard_map/ppermute | solution.py:56
  100.8 1.9 collective-permute-start.10
  102.7 2.5 %collective-permute-start.9 = (bf16[2,2,4,8,1024]{4,3,2,0,1:T(8,128)(2,1)}, bf16[2,2,4,8,1024]{4,3,2,0,1:T(8,128)(2,1)S(1)}, u32[]{:S(2)}, u32[]{:S(2)}) collective-permute-start(bf16[2,2,4,8,1024]{4,3,2,0,1:T(8,128)(2,1)} %pad_maximum_fusion.6), channel_id=1, source_target_pairs={{0,128},{128,256},{256,384},{384,0},{1,129},{129,257},{257,385},{3... | collective-permute-start | bytes 786440 | tf_op jit(solution)/shard_map/ppermute | solution.py:56
  105.8 0.6 reshape.217
  107.2 4.8 %collective-permute-start.8 = (bf16[2,4,8,1024]{3,2,1,0:T(8,128)(2,1)S(1)}, bf16[2,4,8,1024]{3,2,1,0:T(8,128)(2,1)S(1)}, u32[]{:S(2)}, u32[]{:S(2)}) collective-permute-start(bf16[2,4,8,1024]{3,2,1,0:T(8,128)(2,1)S(1)} %fusion.37), channel_id=1, source_target_pairs={{0,1},{1,0},{2,3},{3,2},{4,5},{5,4},{6,7},{7,6},{8,9},{9,8},{10,11... | collective-permute-start | bytes 393224 | tf_op jit(solution)/shard_map/ppermute | solution.py:60
  112.4 5.8 %collective-permute-done.9 = bf16[2,2,4,8,1024]{4,3,2,0,1:T(8,128)(2,1)S(1)} collective-permute-done((bf16[2,2,4,8,1024]{4,3,2,0,1:T(8,128)(2,1)}, bf16[2,2,4,8,1024]{4,3,2,0,1:T(8,128)(2,1)S(1)}, u32[]{:S(2)}, u32[]{:S(2)}) %collective-permute-start.9) | collective-permute-done | bytes 262176 | tf_op jit(solution)/shard_map/ppermute | solution.py:56
  118.5 4.8 %collective-permute-start.12 = (bf16[2,4,8,1024]{3,2,1,0:T(8,128)(2,1)S(1)}, bf16[2,4,8,1024]{3,2,1,0:T(8,128)(2,1)S(1)}, u32[]{:S(2)}, u32[]{:S(2)}) collective-permute-start(bf16[2,4,8,1024]{3,2,1,0:T(8,128)(2,1)S(1)} %fusion.38), channel_id=1, source_target_pairs={{0,1},{1,0},{2,3},{3,2},{4,5},{5,4},{6,7},{7,6},{8,9},{9,8},{10,11... | collective-permute-start | bytes 393224 | tf_op jit(solution)/shard_map/ppermute | solution.py:60
  123.3 5.0 %collective-permute-start.13 = (bf16[4,144,256]{2,1,0:T(8,128)(2,1)S(1)}, bf16[4,144,256]{2,1,0:T(8,128)(2,1)S(1)}, u32[]{:S(2)}, u32[]{:S(2)}) collective-permute-start(bf16[4,144,256]{2,1,0:T(8,128)(2,1)S(1)} %pad_maximum_fusion.2), channel_id=1, source_target_pairs={{0,8},{2,10},{4,12},{6,14},{8,16},{10,18},{12,20},{14,22},{16,24},... | collective-permute-start | bytes 884744 | tf_op jit(solution)/shard_map/ppermute | solution.py:52
  129.5 0.7 broadcast_in_dim.83
  130.2 16.0 %all-to-all-start.2 = ((f32[64,3,128]{2,1,0:T(4,128)}), f32[64,3,128]{2,1,0:T(4,128)S(1)}, u32[]{:S(2)}, u32[]{:S(2)}) async-start(f32[64,3,128]{2,1,0:T(4,128)} %broadcast_in_dim.83), calls=%async_computation.2 | async-start | bytes 262144 | tf_op jit(solution)/shard_map/all_to_all | solution.py:173
  146.4 2.1 %and_and_fusion = pred[128,1152]{0,1:T(8,128)(4,1)S(1)} fusion(s32[128]{0:T(128)} %iota_add_fusion.2, s32[1152]{0:T(1024)S(1)} %iota_add_fusion, pred[1152]{0:T(1024)(128)(4,1)} %broadcast_compare_fusion, bf16[128]{0:T(256)(128)(2,1)} %copy-done.10, bf16[1152]{0:T(1024)(128)(2,1)S(1)} %bitcast.197), kind=kLoop, calls=%fused_computation.33 | loop fusion | flops 884736 | bytes 156288 | tf_op jit(solution)/shard_map/and | solution.py:206
  148.5 0.6 tile.7
  149.1 1.1 fusion.2
  150.2 1.3 fusion.7
  151.6 1.4 divide_convert_fusion
  153.0 0.6 fusion.9
  153.6 3.4 %all-to-all-done.2 = f32[64,3,128]{2,1,0:T(4,128)S(1)} async-done(((f32[64,3,128]{2,1,0:T(4,128)}), f32[64,3,128]{2,1,0:T(4,128)S(1)}, u32[]{:S(2)}, u32[]{:S(2)}) %all-to-all-start.2) | async-done | bytes 98336 | tf_op jit(solution)/shard_map/all_to_all | solution.py:173
  157.2 0.6 broadcast_in_dim.84
  157.8 3.8 %all-to-all-start.3 = ((f32[8,1,128]{2,1,0:T(1,128)}), f32[8,1,128]{2,1,0:T(1,128)S(1)}, u32[]{:S(2)}, u32[]{:S(2)}) async-start(f32[8,1,128]{2,1,0:T(1,128)} %broadcast_in_dim.84), calls=%async_computation.3 | async-start | bytes 8192 | tf_op jit(solution)/shard_map/all_to_all | solution.py:182
  161.6 2.3 %fusion.1 = bf16[1024,1152]{0,1:T(8,128)(2,1)} fusion(bf16[1024,1152]{0,1:T(8,128)(2,1)S(1)} %divide_convert_fusion, bf16[1152,128]{1,0:T(8,128)(2,1)S(1)} %bitcast.187, f32[1024]{0:T(1024)S(1)} %fusion.9, bf16[16,8,8,128]{3,2,1,0:T(8,128)(2,1)S(1)} %bitcast.168), kind=kOutput, calls=%fused_computation.4 | convolution fusion | flops 307888128 | bytes 5279744 | tf_op jit(solution)/shard_map/dot_general | solution.py:227
  163.8 6.6 %all-to-all-done.3 = f32[8,1,128]{2,1,0:T(1,128)S(1)} async-done(((f32[8,1,128]{2,1,0:T(1,128)}), f32[8,1,128]{2,1,0:T(1,128)S(1)}, u32[]{:S(2)}, u32[]{:S(2)}) %all-to-all-start.3) | async-done | bytes 4128 | tf_op jit(solution)/shard_map/all_to_all | solution.py:182
  170.6 0.9 fusion.23
  172.1 0.9 fusion.22
  173.0 1.0 fusion.17
  174.1 5.2 %all-to-all-start.4 = ((bf16[8,128,256]{1,2,0:T(8,128)(2,1)}), bf16[8,128,256]{1,2,0:T(8,128)(2,1)S(1)}, u32[]{:S(2)}, u32[]{:S(2)}) async-start(bf16[8,128,256]{1,2,0:T(8,128)(2,1)} %fusion.17), calls=%async_computation.4 | async-start | bytes 1048576 | tf_op jit(solution)/shard_map/all_to_all | solution.py:42
  179.5 0.6 reshape.215
  180.1 13.7 %all-to-all-done.4 = bf16[8,128,256]{1,2,0:T(8,128)(2,1)S(1)} async-done(((bf16[8,128,256]{1,2,0:T(8,128)(2,1)}), bf16[8,128,256]{1,2,0:T(8,128)(2,1)S(1)}, u32[]{:S(2)}, u32[]{:S(2)}) %all-to-all-start.4) | async-done | bytes 524320 | tf_op jit(solution)/shard_map/all_to_all | solution.py:42
  194.1 1.3 collective-permute-start.14
  195.4 2.2 %fusion.10 = bf16[16,8,8,128]{3,1,2,0:T(8,128)(2,1)S(1)} fusion(bf16[1024,1152]{0,1:T(8,128)(2,1)} %fusion.1, bf16[1152,128]{1,0:T(8,128)(2,1)S(1)} %bitcast.185, f32[1024]{0:T(1024)S(1)} %broadcast_bitcast_fusion), kind=kOutput, calls=%fused_computation.24 | convolution fusion | flops 302252032 | bytes 2920448 | tf_op jit(solution)/shard_map/dot_general | solution.py:231
  197.9 0.8 copy.202
  199.2 0.7 copy.144
  199.9 0.7 copy.145
  (103 shorter events, 6.8 us)
Async XLA Ops:
  2.5 40.4 %all-to-all-start = ((bf16[32,8,2048]{2,1,0:T(8,128)(2,1)}), bf16[32,8,2048]{2,1,0:T(8,128)(2,1)S(1)}, u32[]{:S(2)}, u32[]{:S(2)}) async-start(bf16[32,8,2048]{2,1,0:T(8,128)(2,1)} %broadcast_in_dim.78), calls=%async_computation | async-start | bytes 2097152 | tf_op jit(solution)/shard_map/all_to_all | solution.py:36
  17.5 0.5 copy-start.10
  18.8 21.6 %collective-permute-start = (bf16[1,144,256]{2,1,0:T(8,128)(2,1)S(1)}, bf16[1,144,256]{2,1,0:T(8,128)(2,1)S(1)}, u32[]{:S(2)}, u32[]{:S(2)}) collective-permute-start(bf16[1,144,256]{2,1,0:T(8,128)(2,1)S(1)} %maximum_bitcast_fusion), channel_id=1, source_target_pairs={{0,16},{2,18},{4,20},{6,22},{8,24},{10,26},{12,28},{14,30},{16,32}... | collective-permute-start | bytes 221192 | tf_op jit(solution)/shard_map/ppermute | solution.py:52
  21.9 12.6 %collective-permute-start.1 = (bf16[1,144,256]{2,1,0:T(8,128)(2,1)S(1)}, bf16[1,144,256]{2,1,0:T(8,128)(2,1)S(1)}, u32[]{:S(2)}, u32[]{:S(2)}) collective-permute-start(bf16[1,144,256]{2,1,0:T(8,128)(2,1)S(1)} %maximum_bitcast_fusion), channel_id=1, source_target_pairs={{0,2},{2,4},{4,6},{6,8},{8,10},{10,12},{12,14},{14,16},{16,18},{18... | collective-permute-start | bytes 221192 | tf_op jit(solution)/shard_map/ppermute | solution.py:52
  44.0 15.1 %collective-permute-start.2 = (bf16[256,2048]{1,0:T(8,128)(2,1)S(1)}, bf16[256,2048]{1,0:T(8,128)(2,1)}, u32[]{:S(2)}, u32[]{:S(2)}) collective-permute-start(bf16[256,2048]{1,0:T(8,128)(2,1)S(1)} %bitcast.170), channel_id=1, source_target_pairs={{0,2},{2,0},{4,6},{6,4},{8,10},{10,8},{12,14},{14,12},{16,18},{18,... | collective-permute-start | bytes 3145736 | tf_op jit(solution)/shard_map/ppermute | solution.py:27
  49.9 34.8 %all-to-all-start.1 = ((bf16[32,8,2048]{2,1,0:T(8,128)(2,1)}), bf16[32,8,2048]{2,1,0:T(8,128)(2,1)S(1)}, u32[]{:S(2)}, u32[]{:S(2)}) async-start(bf16[32,8,2048]{2,1,0:T(8,128)(2,1)} %broadcast_in_dim.79), calls=%async_computation.1 | async-start | bytes 2097152 | tf_op jit(solution)/shard_map/all_to_all | solution.py:36
  55.4 3.6 %copy-start.11 = (bf16[2048,1024]{1,0:T(8,128)(2,1)S(1)}, bf16[2048,1024]{1,0:T(8,128)(2,1)}, u32[]{:S(2)}) copy-start(bf16[2048,1024]{1,0:T(8,128)(2,1)} %param.11) | copy-start | bytes 12582916
  59.0 3.1 %copy-start.1 = (f32[4,2,4,8,1024]{4,3,2,1,0:T(8,128)}, f32[4,2,4,8,1024]{4,3,2,1,0:T(8,128)S(1)}, u32[]{:S(2)}) copy-start(f32[4,2,4,8,1024]{4,3,2,1,0:T(8,128)S(1)} %fusion.5) | copy-start | bytes 3145732
  59.0 13.9 %copy-start.6 = (f32[1024]{0:T(1024)S(1)}, f32[1024]{0:T(1024)}, u32[]{:S(2)}) copy-start(f32[1024]{0:T(1024)} %param.13) | copy-start | bytes 12292
  62.8 15.6 %collective-permute-start.5 = (bf16[2,2,4,8,1024]{4,3,2,1,0:T(8,128)(2,1)}, bf16[2,2,4,8,1024]{4,3,2,1,0:T(8,128)(2,1)S(1)}, u32[]{:S(2)}, u32[]{:S(2)}) collective-permute-start(bf16[2,2,4,8,1024]{4,3,2,1,0:T(8,128)(2,1)} %pad_maximum_fusion.5), channel_id=1, source_target_pairs={{0,384},{128,0},{256,128},{384,256},{1,385},{129,1},{257,129},{385... | collective-permute-start | bytes 786440 | tf_op jit(solution)/shard_map/ppermute | solution.py:56
  67.2 12.4 %collective-permute-start.4 = (bf16[2,2,4,8,1024]{4,3,2,1,0:T(8,128)(2,1)S(1)}, bf16[2,2,4,8,1024]{4,3,2,1,0:T(8,128)(2,1)S(1)}, u32[]{:S(2)}, u32[]{:S(2)}) collective-permute-start(bf16[2,2,4,8,1024]{4,3,2,1,0:T(8,128)(2,1)S(1)} %pad_maximum_fusion.4), channel_id=1, source_target_pairs={{0,256},{128,384},{256,0},{384,128},{1,257},{129,385},{257,1},{385... | collective-permute-start | bytes 786440 | tf_op jit(solution)/shard_map/ppermute | solution.py:56
  70.4 14.1 %collective-permute-start.3 = (bf16[2,2,4,8,1024]{4,3,2,1,0:T(8,128)(2,1)}, bf16[2,2,4,8,1024]{4,3,2,1,0:T(8,128)(2,1)S(1)}, u32[]{:S(2)}, u32[]{:S(2)}) collective-permute-start(bf16[2,2,4,8,1024]{4,3,2,1,0:T(8,128)(2,1)} %pad_maximum_fusion.3), channel_id=1, source_target_pairs={{0,128},{128,256},{256,384},{384,0},{1,129},{129,257},{257,385},{3... | collective-permute-start | bytes 786440 | tf_op jit(solution)/shard_map/ppermute | solution.py:56
  78.4 6.2 %collective-permute-start.6 = (bf16[2,144,256]{2,1,0:T(8,128)(2,1)S(1)}, bf16[2,144,256]{2,1,0:T(8,128)(2,1)S(1)}, u32[]{:S(2)}, u32[]{:S(2)}) collective-permute-start(bf16[2,144,256]{2,1,0:T(8,128)(2,1)S(1)} %pad_maximum_fusion.9), channel_id=1, source_target_pairs={{0,4},{2,6},{4,8},{6,10},{8,12},{10,14},{12,16},{14,18},{16,20},{1... | collective-permute-start | bytes 442376 | tf_op jit(solution)/shard_map/ppermute | solution.py:52
  84.7 7.3 %collective-permute-start.7 = (bf16[256,2048]{1,0:T(8,128)(2,1)S(1)}, bf16[256,2048]{1,0:T(8,128)(2,1)S(1)}, u32[]{:S(2)}, u32[]{:S(2)}) collective-permute-start(bf16[256,2048]{1,0:T(8,128)(2,1)S(1)} %bitcast.172), channel_id=1, source_target_pairs={{0,2},{2,0},{4,6},{6,4},{8,10},{10,8},{12,14},{14,12},{16,18},{18,... | collective-permute-start | bytes 3145736 | tf_op jit(solution)/shard_map/ppermute | solution.py:27
  88.3 3.7 %copy-start.12 = (bf16[2048,1024]{1,0:T(8,128)(2,1)S(1)}, bf16[2048,1024]{1,0:T(8,128)(2,1)}, u32[]{:S(2)}) copy-start(bf16[2048,1024]{1,0:T(8,128)(2,1)} %param.11) | copy-start | bytes 12582916
  92.0 14.4 %copy-start.4 = (bf16[128,1024]{1,0:T(8,128)(2,1)S(1)}, bf16[128,1024]{1,0:T(8,128)(2,1)}, u32[]{:S(2)}) copy-start(bf16[128,1024]{1,0:T(8,128)(2,1)} %param.15) | copy-start | bytes 786436
  93.3 13.4 %copy-start.5 = (bf16[128,1024]{1,0:T(8,128)(2,1)S(1)}, bf16[128,1024]{1,0:T(8,128)(2,1)}, u32[]{:S(2)}) copy-start(bf16[128,1024]{1,0:T(8,128)(2,1)} %param.18) | copy-start | bytes 786436
  93.3 13.7 %copy-start.7 = (s32[1024]{0:T(1024)S(1)}, s32[1024]{0:T(1024)}, u32[]{:S(2)}) copy-start(s32[1024]{0:T(1024)} %param.14) | copy-start | bytes 12292
  95.6 16.8 %collective-permute-start.11 = (bf16[2,2,4,8,1024]{4,3,2,0,1:T(8,128)(2,1)}, bf16[2,2,4,8,1024]{4,3,2,0,1:T(8,128)(2,1)S(1)}, u32[]{:S(2)}, u32[]{:S(2)}) collective-permute-start(bf16[2,2,4,8,1024]{4,3,2,0,1:T(8,128)(2,1)} %pad_maximum_fusion.8), channel_id=1, source_target_pairs={{0,384},{128,0},{256,128},{384,256},{1,385},{129,1},{257,129},{385... | collective-permute-start | bytes 786440 | tf_op jit(solution)/shard_map/ppermute | solution.py:56
  100.8 11.6 %collective-permute-start.10 = (bf16[2,2,4,8,1024]{4,3,2,0,1:T(8,128)(2,1)}, bf16[2,2,4,8,1024]{4,3,2,0,1:T(8,128)(2,1)S(1)}, u32[]{:S(2)}, u32[]{:S(2)}) collective-permute-start(bf16[2,2,4,8,1024]{4,3,2,0,1:T(8,128)(2,1)} %pad_maximum_fusion.7), channel_id=1, source_target_pairs={{0,256},{128,384},{256,0},{384,128},{1,257},{129,385},{257,1},{385... | collective-permute-start | bytes 786440 | tf_op jit(solution)/shard_map/ppermute | solution.py:56
  102.7 15.6 %collective-permute-start.9 = (bf16[2,2,4,8,1024]{4,3,2,0,1:T(8,128)(2,1)}, bf16[2,2,4,8,1024]{4,3,2,0,1:T(8,128)(2,1)S(1)}, u32[]{:S(2)}, u32[]{:S(2)}) collective-permute-start(bf16[2,2,4,8,1024]{4,3,2,0,1:T(8,128)(2,1)} %pad_maximum_fusion.6), channel_id=1, source_target_pairs={{0,128},{128,256},{256,384},{384,0},{1,129},{129,257},{257,385},{3... | collective-permute-start | bytes 786440 | tf_op jit(solution)/shard_map/ppermute | solution.py:56
  107.2 16.0 %collective-permute-start.8 = (bf16[2,4,8,1024]{3,2,1,0:T(8,128)(2,1)S(1)}, bf16[2,4,8,1024]{3,2,1,0:T(8,128)(2,1)S(1)}, u32[]{:S(2)}, u32[]{:S(2)}) collective-permute-start(bf16[2,4,8,1024]{3,2,1,0:T(8,128)(2,1)S(1)} %fusion.37), channel_id=1, source_target_pairs={{0,1},{1,0},{2,3},{3,2},{4,5},{5,4},{6,7},{7,6},{8,9},{9,8},{10,11... | collective-permute-start | bytes 393224 | tf_op jit(solution)/shard_map/ppermute | solution.py:60
  118.5 10.4 %collective-permute-start.12 = (bf16[2,4,8,1024]{3,2,1,0:T(8,128)(2,1)S(1)}, bf16[2,4,8,1024]{3,2,1,0:T(8,128)(2,1)S(1)}, u32[]{:S(2)}, u32[]{:S(2)}) collective-permute-start(bf16[2,4,8,1024]{3,2,1,0:T(8,128)(2,1)S(1)} %fusion.38), channel_id=1, source_target_pairs={{0,1},{1,0},{2,3},{3,2},{4,5},{5,4},{6,7},{7,6},{8,9},{9,8},{10,11... | collective-permute-start | bytes 393224 | tf_op jit(solution)/shard_map/ppermute | solution.py:60
  123.3 22.9 %collective-permute-start.13 = (bf16[4,144,256]{2,1,0:T(8,128)(2,1)S(1)}, bf16[4,144,256]{2,1,0:T(8,128)(2,1)S(1)}, u32[]{:S(2)}, u32[]{:S(2)}) collective-permute-start(bf16[4,144,256]{2,1,0:T(8,128)(2,1)S(1)} %pad_maximum_fusion.2), channel_id=1, source_target_pairs={{0,8},{2,10},{4,12},{6,14},{8,16},{10,18},{12,20},{14,22},{16,24},... | collective-permute-start | bytes 884744 | tf_op jit(solution)/shard_map/ppermute | solution.py:52
  130.2 26.8 %all-to-all-start.2 = ((f32[64,3,128]{2,1,0:T(4,128)}), f32[64,3,128]{2,1,0:T(4,128)S(1)}, u32[]{:S(2)}, u32[]{:S(2)}) async-start(f32[64,3,128]{2,1,0:T(4,128)} %broadcast_in_dim.83), calls=%async_computation.2 | async-start | bytes 262144 | tf_op jit(solution)/shard_map/all_to_all | solution.py:173
  146.4 3.8 %copy-start.2 = (bf16[9,128,128]{2,1,0:T(8,128)(2,1)}, bf16[9,128,128]{2,1,0:T(8,128)(2,1)S(1)}, u32[]{:S(2)}) copy-start(bf16[9,128,128]{2,1,0:T(8,128)(2,1)S(1)} %get-tuple-element.81) | copy-start | bytes 884740
  153.0 4.2 %copy-start.9 = (f32[128]{0:T(128)S(1)}, f32[128]{0:T(128)}, u32[]{:S(2)}) copy-start(f32[128]{0:T(128)} %reshape.217) | copy-start | bytes 1540
  153.0 17.4 %copy-start.8 = (s32[128]{0:T(128)S(1)}, s32[128]{0:T(128)}, u32[]{:S(2)}) copy-start(s32[128]{0:T(128)} %iota_add_fusion.2) | copy-start | bytes 1540
  157.8 12.6 %all-to-all-start.3 = ((f32[8,1,128]{2,1,0:T(1,128)}), f32[8,1,128]{2,1,0:T(1,128)S(1)}, u32[]{:S(2)}, u32[]{:S(2)}) async-start(f32[8,1,128]{2,1,0:T(1,128)} %broadcast_in_dim.84), calls=%async_computation.3 | async-start | bytes 8192 | tf_op jit(solution)/shard_map/all_to_all | solution.py:182
  170.4 1.7 copy-start
  172.9 22.5 %copy-start.3 = (bf16[9,128,128]{2,1,0:T(8,128)(2,1)S(1)}, bf16[9,128,128]{2,1,0:T(8,128)(2,1)}, u32[]{:S(2)}) copy-start(bf16[9,128,128]{2,1,0:T(8,128)(2,1)} %copy-done.2) | copy-start | bytes 884740
  174.1 19.7 %all-to-all-start.4 = ((bf16[8,128,256]{1,2,0:T(8,128)(2,1)}), bf16[8,128,256]{1,2,0:T(8,128)(2,1)S(1)}, u32[]{:S(2)}, u32[]{:S(2)}) async-start(bf16[8,128,256]{1,2,0:T(8,128)(2,1)} %fusion.17), calls=%async_computation.4 | async-start | bytes 1048576 | tf_op jit(solution)/shard_map/all_to_all | solution.py:42
  194.1 5.0 %collective-permute-start.14 = (bf16[128,256]{0,1:T(8,128)(2,1)S(1)}, bf16[128,256]{0,1:T(8,128)(2,1)S(1)}, u32[]{:S(2)}, u32[]{:S(2)}) collective-permute-start(bf16[128,256]{0,1:T(8,128)(2,1)S(1)} %get-tuple-element.67), channel_id=1, source_target_pairs={{16,0},{18,2},{20,4},{22,6},{24,8},{26,10},{28,12},{30,14},{32,16}... | collective-permute-start | bytes 196616 | tf_op jit(solution)/shard_map/ppermute | solution.py:52

commit v6 on v5

--- a/solution.py
+++ b/solution.py
@@ -77,7 +77,7 @@
 
 
 def section_arrivals(parts):
-    return [along_section(parts[step], step) for step in (1, 2, 3)]
+    return [along_section(parts[step], step) for step in (3, 1, 2)]
 
 
 def section_sums(own, arrivals):
@@ -135,17 +135,16 @@
 
     half = teacher_hidden.shape[0] // 2
     first = across_chips(copies_for_chips(teacher_hidden[:half]))
-    copies = copies_for_chips(teacher_hidden[half:])
     own_window = packed_window(keys, values, segment_ids)
     eighth = passed_along(own_window, 8)
     two_windows = jnp.concatenate([passed_along(own_window, 1), own_window], axis=0)
-    first, copies, eighth, two_windows = lax.optimization_barrier(
-        (first, copies, eighth, two_windows)
-    )
-    last = across_chips(copies)
+    first, teacher_hidden, eighth, two_windows = lax.optimization_barrier(
+        (first, teacher_hidden, eighth, two_windows)
+    )
+    last = across_chips(copies_for_chips(teacher_hidden[half:]))
     first = section_parts(first, lm_head, section)
     arrivals = section_arrivals(first)
-    arrivals[2], two_windows = lax.optimization_barrier((arrivals[2], two_windows))
+    arrivals[0], two_windows = lax.optimization_barrier((arrivals[0], two_windows))
     four_windows = jnp.concatenate([passed_along(two_windows, 2), two_windows], axis=0)
     first, last, four_windows = lax.optimization_barrier(
         (section_sums(first[0], arrivals), last, four_windows)
@@ -239,21 +238,22 @@
     both = jnp.concatenate([grad_key, grad_value], axis=1).reshape(
         FARTHEST + 1, seq_rows, 2 * head_dim
     )
+    d_queries = (
+        grad_query.reshape(group, seq_rows, head_dim)
+        .transpose(1, 0, 2)
+        .reshape(seq_rows, group * head_dim)
+    )
     cyclic = both[1:].astype(jnp.bfloat16)
     cyclic = jnp.concatenate([cyclic, cyclic], axis=0)
     given = lax.dynamic_slice_in_dim(cyclic, Y * CORES - 1 - place, Y * CORES, 0)
-    arrived = across_row(given).astype(jnp.float32)
+    arrived, d_queries = lax.optimization_barrier((across_row(given), d_queries))
+    arrived = arrived.astype(jnp.float32)
     sender = jnp.arange(Y * CORES, dtype=jnp.int32)[:, None, None]
     back = both[0] + jnp.sum(jnp.where(sender < place, arrived, 0.0), axis=0)
     back = passed_along(back.astype(jnp.bfloat16), -Y * CORES).astype(jnp.float32)
     here = both[FARTHEST] + jnp.sum(jnp.where(sender > place, arrived, 0.0), axis=0)
     d_keys = (here[:, :head_dim] + back[:, :head_dim]).astype(jnp.bfloat16)
     d_values = (here[:, head_dim:] + back[:, head_dim:]).astype(jnp.bfloat16)
-    d_queries = (
-        grad_query.reshape(group, seq_rows, head_dim)
-        .transpose(1, 0, 2)
-        .reshape(seq_rows, group * head_dim)
-    )
     return (advantage_own, d_queries, d_keys, d_values)
 
 

time: 202 us -> 205 us (1.015)
  waiting for transfers between devices: 55.6 us -> 45.5 us
  starting transfers between devices: 97.4 us -> 105 us
  local copies, waits for them, and re-layouts: 13.3 us -> 16 us
  other arithmetic: 13.6 us -> 16.2 us
    ppermute x6, waiting for transfers between devices: 15.4 us -> 3.3 us  [along_section(): lax.ppermute(block, 'section', [(s, (s + step) % SECTIONS) for s in range...]
    ppermute x5, starting transfers between devices: 15.2 us -> 20.6 us  [passed_along(): return lax.ppermute(block, 'ctx', route)]
    ppermute x5, waiting for transfers between devices: 13.5 us -> 17.9 us  [passed_along(): return lax.ppermute(block, 'ctx', route)]
    all_to_all x1, starting transfers between devices: 16 us -> 13.1 us  [body(): lax.all_to_all(jnp.broadcast_to(stats, (Z * Y * CORES,) + stats.shape), '...]
    all_to_all x1, waiting for transfers between devices: 13.7 us -> 11 us  [across_row(): return lax.all_to_all(blocks, 'ctx', 0, 0, axis_index_groups=groups)]
    ppermute x6, starting transfers between devices: 18.9 us -> 21.3 us  [along_section(): lax.ppermute(block, 'section', [(s, (s + step) % SECTIONS) for s in range...]
  transfers between devices with their start and end apart: 20 -> 20, of which waited for: 12 -> 10; matrix products, arithmetic and copies ran while one was open for 16% -> 19% of each run, Pallas kernels for 0% -> 0%
where the time goes in v6:
time: 205 us; the launch traced here: 204 us
  starting transfers between devices  105 us (51%)
  waiting for transfers between devices  45.5 us (22%)
  matrix products  19.3 us (9%)
  other arithmetic  16.2 us (8%)
  local copies, waits for them, and re-layouts  16 us (8%)
    ppermute x6, starting transfers between devices, along_section(): lax.ppermute(block, 'section', [(s, (s + step) % SECTIONS) for s in range...  21.3 us
    ppermute x5, starting transfers between devices, passed_along(): return lax.ppermute(block, 'ctx', route)  20.6 us
    all_to_all x2, starting transfers between devices, across_chips(): return lax.all_to_all(copies, 'ctx', 0, 0, axis_index_groups=groups)  19.8 us
    ppermute x5, waiting for transfers between devices, passed_along(): return lax.ppermute(block, 'ctx', route)  17.9 us
    all_to_all x1, starting transfers between devices, body(): lax.all_to_all(jnp.broadcast_to(stats, (Z * Y * CORES,) + stats.shape), '...  13.1 us
    dot_general x4, matrix products, section_parts(): part = jnp.dot(rows, weight, preferred_element_type=jnp.float32)  11.3 us
    all_to_all x1, waiting for transfers between devices, across_row(): return lax.all_to_all(blocks, 'ctx', 0, 0, axis_index_groups=groups)  11 us
    ppermute x2, starting transfers between devices, ctx_move(): return lax.ppermute(block, 'ctx', route)  10.7 us
  transfers between devices with their start and end apart: 20, of which 10 were waited for; matrix products, arithmetic and copies ran while one was open for 19% of the time, Pallas kernels for 0%

profile of v6, /device:TPU:1, one launch (start us, length us, event | category | flops | bytes accessed | tf_op | source)
XLA Modules:
  0.0 203.9 jit_solution(9971614197529099238)
XLA Ops:
  0.6 0.8 slice.50
  1.4 1.1 broadcast_in_dim.78
  2.5 14.3 %all-to-all-start = ((bf16[32,8,2048]{2,1,0:T(8,128)(2,1)}), bf16[32,8,2048]{2,1,0:T(8,128)(2,1)S(1)}, u32[]{:S(2)}, u32[]{:S(2)}) async-start(bf16[32,8,2048]{2,1,0:T(8,128)(2,1)} %broadcast_in_dim.78), calls=%async_computation | async-start | bytes 2097152 | tf_op jit(solution)/shard_map/all_to_all | solution.py:36
  16.8 0.7 convert.43
  18.1 0.8 maximum_bitcast_fusion
  18.8 3.1 %collective-permute-start = (bf16[1,144,256]{2,1,0:T(8,128)(2,1)S(1)}, bf16[1,144,256]{2,1,0:T(8,128)(2,1)S(1)}, u32[]{:S(2)}, u32[]{:S(2)}) collective-permute-start(bf16[1,144,256]{2,1,0:T(8,128)(2,1)S(1)} %maximum_bitcast_fusion), channel_id=1, source_target_pairs={{0,16},{2,18},{4,20},{6,22},{8,24},{10,26},{12,28},{14,30},{16,32}... | collective-permute-start | bytes 221192 | tf_op jit(solution)/shard_map/ppermute | solution.py:52
  22.0 4.5 %collective-permute-start.1 = (bf16[1,144,256]{2,1,0:T(8,128)(2,1)S(1)}, bf16[1,144,256]{2,1,0:T(8,128)(2,1)S(1)}, u32[]{:S(2)}, u32[]{:S(2)}) collective-permute-start(bf16[1,144,256]{2,1,0:T(8,128)(2,1)S(1)} %maximum_bitcast_fusion), channel_id=1, source_target_pairs={{0,2},{2,4},{4,6},{6,8},{8,10},{10,12},{12,14},{14,16},{16,18},{18... | collective-permute-start | bytes 221192 | tf_op jit(solution)/shard_map/ppermute | solution.py:52
  26.5 0.8 reshape.211
  27.4 7.1 %collective-permute-done.1 = bf16[1,144,256]{2,1,0:T(8,128)(2,1)S(1)} collective-permute-done((bf16[1,144,256]{2,1,0:T(8,128)(2,1)S(1)}, bf16[1,144,256]{2,1,0:T(8,128)(2,1)S(1)}, u32[]{:S(2)}, u32[]{:S(2)}) %collective-permute-start.1) | collective-permute-done | bytes 73760 | tf_op jit(solution)/shard_map/ppermute | solution.py:52
  34.6 5.8 %collective-permute-done = bf16[1,144,256]{2,1,0:T(8,128)(2,1)S(1)} collective-permute-done((bf16[1,144,256]{2,1,0:T(8,128)(2,1)S(1)}, bf16[1,144,256]{2,1,0:T(8,128)(2,1)S(1)}, u32[]{:S(2)}, u32[]{:S(2)}) %collective-permute-start) | collective-permute-done | bytes 73760 | tf_op jit(solution)/shard_map/ppermute | solution.py:52
  40.4 2.5 %all-to-all-done = bf16[32,8,2048]{2,1,0:T(8,128)(2,1)S(1)} async-done(((bf16[32,8,2048]{2,1,0:T(8,128)(2,1)}), bf16[32,8,2048]{2,1,0:T(8,128)(2,1)S(1)}, u32[]{:S(2)}, u32[]{:S(2)}) %all-to-all-start) | async-done | bytes 1048608 | tf_op jit(solution)/shard_map/all_to_all | solution.py:36
  42.9 5.9 %collective-permute-start.2 = (bf16[256,2048]{1,0:T(8,128)(2,1)S(1)}, bf16[256,2048]{1,0:T(8,128)(2,1)}, u32[]{:S(2)}, u32[]{:S(2)}) collective-permute-start(bf16[256,2048]{1,0:T(8,128)(2,1)S(1)} %bitcast.170), channel_id=1, source_target_pairs={{0,2},{2,0},{4,6},{6,4},{8,10},{10,8},{12,14},{14,12},{16,18},{18,... | collective-permute-start | bytes 3145736 | tf_op jit(solution)/shard_map/ppermute | solution.py:27
  48.8 0.8 slice.51
  49.6 1.1 broadcast_in_dim.81
  50.7 5.5 %all-to-all-start.1 = ((bf16[32,8,2048]{2,1,0:T(8,128)(2,1)}), bf16[32,8,2048]{2,1,0:T(8,128)(2,1)S(1)}, u32[]{:S(2)}, u32[]{:S(2)}) async-start(bf16[32,8,2048]{2,1,0:T(8,128)(2,1)} %broadcast_in_dim.81), calls=%async_computation.1 | async-start | bytes 2097152 | tf_op jit(solution)/shard_map/all_to_all | solution.py:36
  56.2 3.6 %fusion.5 = f32[4,2,4,8,1024]{4,3,2,1,0:T(8,128)S(1)} fusion(bf16[4,2,4,8,2048]{4,3,2,1,0:T(8,128)(2,1)S(1)} %bitcast.171, bf16[2048,1024]{1,0:T(8,128)(2,1)} %param.11), kind=kOutput, calls=%fused_computation.11 | convolution fusion | flops 1073741824 | bytes 6291456 | tf_op jit(solution)/shard_map/dot_general | solution.py:67
  59.8 2.9 %fusion.49 = f32[256,1024]{1,0:T(8,128)S(1)} fusion(bf16[256,2048]{1,0:T(8,128)(2,1)} %collective-permute-done.2, bf16[2048,1024]{1,0:T(8,128)(2,1)S(1)} %copy-done.14), kind=kOutput, calls=%fused_computation.132 | convolution fusion | flops 1073741824 | bytes 6291456 | tf_op jit(solution)/shard_map/dot_general | solution.py:67
  62.8 0.7 pad_maximum_fusion.5
  63.6 4.6 %collective-permute-start.5 = (bf16[2,2,4,8,1024]{4,3,2,1,0:T(8,128)(2,1)}, bf16[2,2,4,8,1024]{4,3,2,1,0:T(8,128)(2,1)S(1)}, u32[]{:S(2)}, u32[]{:S(2)}) collective-permute-start(bf16[2,2,4,8,1024]{4,3,2,1,0:T(8,128)(2,1)} %pad_maximum_fusion.5), channel_id=1, source_target_pairs={{0,256},{128,384},{256,0},{384,128},{1,257},{129,385},{257,1},{385... | collective-permute-start | bytes 786440 | tf_op jit(solution)/shard_map/ppermute | solution.py:56
  68.2 0.7 pad_maximum_fusion.4
  68.9 2.2 %collective-permute-start.4 = (bf16[2,2,4,8,1024]{4,3,2,1,0:T(8,128)(2,1)}, bf16[2,2,4,8,1024]{4,3,2,1,0:T(8,128)(2,1)S(1)}, u32[]{:S(2)}, u32[]{:S(2)}) collective-permute-start(bf16[2,2,4,8,1024]{4,3,2,1,0:T(8,128)(2,1)} %pad_maximum_fusion.4), channel_id=1, source_target_pairs={{0,128},{128,256},{256,384},{384,0},{1,129},{129,257},{257,385},{3... | collective-permute-start | bytes 786440 | tf_op jit(solution)/shard_map/ppermute | solution.py:56
  71.2 0.7 pad_maximum_fusion.3
  71.9 4.3 %collective-permute-start.3 = (bf16[2,2,4,8,1024]{4,3,2,1,0:T(8,128)(2,1)}, bf16[2,2,4,8,1024]{4,3,2,1,0:T(8,128)(2,1)S(1)}, u32[]{:S(2)}, u32[]{:S(2)}) collective-permute-start(bf16[2,2,4,8,1024]{4,3,2,1,0:T(8,128)(2,1)} %pad_maximum_fusion.3), channel_id=1, source_target_pairs={{0,384},{128,0},{256,128},{384,256},{1,385},{129,1},{257,129},{385... | collective-permute-start | bytes 786440 | tf_op jit(solution)/shard_map/ppermute | solution.py:56
  76.9 1.0 constant_dynamic-slice_fusion.1
  77.9 3.3 %collective-permute-done.3 = bf16[2,2,4,8,1024]{4,3,2,1,0:T(8,128)(2,1)S(1)} collective-permute-done((bf16[2,2,4,8,1024]{4,3,2,1,0:T(8,128)(2,1)}, bf16[2,2,4,8,1024]{4,3,2,1,0:T(8,128)(2,1)S(1)}, u32[]{:S(2)}, u32[]{:S(2)}) %collective-permute-start.3) | collective-permute-done | bytes 262176 | tf_op jit(solution)/shard_map/ppermute | solution.py:56
  81.2 2.8 %collective-permute-start.6 = (bf16[2,144,256]{2,1,0:T(8,128)(2,1)S(1)}, bf16[2,144,256]{2,1,0:T(8,128)(2,1)S(1)}, u32[]{:S(2)}, u32[]{:S(2)}) collective-permute-start(bf16[2,144,256]{2,1,0:T(8,128)(2,1)S(1)} %pad_maximum_fusion.9), channel_id=1, source_target_pairs={{0,4},{2,6},{4,8},{6,10},{8,12},{10,14},{12,16},{14,18},{16,20},{1... | collective-permute-start | bytes 442376 | tf_op jit(solution)/shard_map/ppermute | solution.py:52
  84.2 1.9 collective-permute-done.6
  86.2 4.8 %collective-permute-start.7 = (bf16[256,2048]{1,0:T(8,128)(2,1)S(1)}, bf16[256,2048]{1,0:T(8,128)(2,1)S(1)}, u32[]{:S(2)}, u32[]{:S(2)}) collective-permute-start(bf16[256,2048]{1,0:T(8,128)(2,1)S(1)} %bitcast.172), channel_id=1, source_target_pairs={{0,2},{2,0},{4,6},{6,4},{8,10},{10,8},{12,14},{14,12},{16,18},{18,... | collective-permute-start | bytes 3145736 | tf_op jit(solution)/shard_map/ppermute | solution.py:27
  91.6 0.7 fusion.37
  92.2 3.6 %fusion.3 = f32[4,2,4,8,1024]{4,3,2,0,1:T(8,128)S(1)} fusion(bf16[2048,1024]{1,0:T(8,128)(2,1)} %param.11, bf16[4,2,4,8,2048]{4,3,2,1,0:T(8,128)(2,1)S(1)} %bitcast.173), kind=kOutput, calls=%fused_computation.9 | convolution fusion | flops 1073741824 | bytes 6291456 | tf_op jit(solution)/shard_map/dot_general | solution.py:67
  96.0 1.3 fusion.50
  97.4 0.7 pad_maximum_fusion.6
  98.1 0.7 pad_maximum_fusion.7
  98.9 0.7 pad_maximum_fusion.8
  99.6 3.7 %collective-permute-start.11 = (bf16[2,2,4,8,1024]{4,3,2,0,1:T(8,128)(2,1)}, bf16[2,2,4,8,1024]{4,3,2,0,1:T(8,128)(2,1)S(1)}, u32[]{:S(2)}, u32[]{:S(2)}) collective-permute-start(bf16[2,2,4,8,1024]{4,3,2,0,1:T(8,128)(2,1)} %pad_maximum_fusion.7), channel_id=1, source_target_pairs={{0,256},{128,384},{256,0},{384,128},{1,257},{129,385},{257,1},{385... | collective-permute-start | bytes 786440 | tf_op jit(solution)/shard_map/ppermute | solution.py:56
  103.3 4.0 %collective-permute-start.10 = (bf16[2,2,4,8,1024]{4,3,2,0,1:T(8,128)(2,1)}, bf16[2,2,4,8,1024]{4,3,2,0,1:T(8,128)(2,1)S(1)}, u32[]{:S(2)}, u32[]{:S(2)}) collective-permute-start(bf16[2,2,4,8,1024]{4,3,2,0,1:T(8,128)(2,1)} %pad_maximum_fusion.6), channel_id=1, source_target_pairs={{0,128},{128,256},{256,384},{384,0},{1,129},{129,257},{257,385},{3... | collective-permute-start | bytes 786440 | tf_op jit(solution)/shard_map/ppermute | solution.py:56
  107.3 2.5 %collective-permute-start.9 = (bf16[2,2,4,8,1024]{4,3,2,0,1:T(8,128)(2,1)}, bf16[2,2,4,8,1024]{4,3,2,0,1:T(8,128)(2,1)S(1)}, u32[]{:S(2)}, u32[]{:S(2)}) collective-permute-start(bf16[2,2,4,8,1024]{4,3,2,0,1:T(8,128)(2,1)} %pad_maximum_fusion.8), channel_id=1, source_target_pairs={{0,384},{128,0},{256,128},{384,256},{1,385},{129,1},{257,129},{385... | collective-permute-start | bytes 786440 | tf_op jit(solution)/shard_map/ppermute | solution.py:56
  112.0 0.7 eq.59
  113.6 4.8 %collective-permute-start.8 = (bf16[2,4,8,1024]{3,2,1,0:T(8,128)(2,1)}, bf16[2,4,8,1024]{3,2,1,0:T(8,128)(2,1)S(1)}, u32[]{:S(2)}, u32[]{:S(2)}) collective-permute-start(bf16[2,4,8,1024]{3,2,1,0:T(8,128)(2,1)} %fusion.37), channel_id=1, source_target_pairs={{0,1},{1,0},{2,3},{3,2},{4,5},{5,4},{6,7},{7,6},{8,9},{9,8},{10,11... | collective-permute-start | bytes 393224 | tf_op jit(solution)/shard_map/ppermute | solution.py:60
  118.6 4.4 %collective-permute-start.12 = (bf16[2,4,8,1024]{3,2,1,0:T(8,128)(2,1)S(1)}, bf16[2,4,8,1024]{3,2,1,0:T(8,128)(2,1)S(1)}, u32[]{:S(2)}, u32[]{:S(2)}) collective-permute-start(bf16[2,4,8,1024]{3,2,1,0:T(8,128)(2,1)S(1)} %fusion.38), channel_id=1, source_target_pairs={{0,1},{1,0},{2,3},{3,2},{4,5},{5,4},{6,7},{7,6},{8,9},{9,8},{10,11... | collective-permute-start | bytes 393224 | tf_op jit(solution)/shard_map/ppermute | solution.py:60
  123.0 0.8 collective-permute-done.8
  123.8 8.9 %collective-permute-start.13 = (bf16[4,144,256]{2,1,0:T(8,128)(2,1)S(1)}, bf16[4,144,256]{2,1,0:T(8,128)(2,1)S(1)}, u32[]{:S(2)}, u32[]{:S(2)}) collective-permute-start(bf16[4,144,256]{2,1,0:T(8,128)(2,1)S(1)} %pad_maximum_fusion.2), channel_id=1, source_target_pairs={{0,8},{2,10},{4,12},{6,14},{8,16},{10,18},{12,20},{14,22},{16,24},... | collective-permute-start | bytes 884744 | tf_op jit(solution)/shard_map/ppermute | solution.py:52
  132.9 0.9 exponential_reduce_fusion
  134.0 0.7 broadcast_in_dim.83
  134.7 13.1 %all-to-all-start.2 = ((f32[64,3,128]{2,1,0:T(4,128)}), f32[64,3,128]{2,1,0:T(4,128)S(1)}, u32[]{:S(2)}, u32[]{:S(2)}) async-start(f32[64,3,128]{2,1,0:T(4,128)} %broadcast_in_dim.83), calls=%async_computation.2 | async-start | bytes 262144 | tf_op jit(solution)/shard_map/all_to_all | solution.py:172
  148.0 2.1 %and_and_fusion = pred[128,1152]{0,1:T(8,128)(4,1)S(1)} fusion(s32[128]{0:T(128)} %iota_add_fusion.2, s32[1152]{0:T(1024)S(1)} %copy-done.7, pred[1152]{0:T(1024)(128)(4,1)} %broadcast_compare_fusion, bf16[128]{0:T(256)(128)(2,1)} %copy-done.13, bf16[1152]{0:T(1024)(128)(2,1)S(1)} %bitcast.197), kind=kLoop, calls=%fused_computation.33 | loop fusion | flops 884736 | bytes 156288 | tf_op jit(solution)/shard_map/and | solution.py:205
  150.7 1.1 fusion.2
  151.9 1.3 fusion.7
  153.2 1.4 divide_convert_fusion
  155.2 3.4 %all-to-all-done.2 = f32[64,3,128]{2,1,0:T(4,128)S(1)} async-done(((f32[64,3,128]{2,1,0:T(4,128)}), f32[64,3,128]{2,1,0:T(4,128)S(1)}, u32[]{:S(2)}, u32[]{:S(2)}) %all-to-all-start.2) | async-done | bytes 98336 | tf_op jit(solution)/shard_map/all_to_all | solution.py:172
  159.4 5.5 %all-to-all-start.3 = ((f32[8,1,128]{2,1,0:T(1,128)}), f32[8,1,128]{2,1,0:T(1,128)S(1)}, u32[]{:S(2)}, u32[]{:S(2)}) async-start(f32[8,1,128]{2,1,0:T(1,128)} %broadcast_in_dim.86), calls=%async_computation.3 | async-start | bytes 8192 | tf_op jit(solution)/shard_map/all_to_all | solution.py:181
  164.9 2.3 %fusion.1 = bf16[1024,1152]{0,1:T(8,128)(2,1)} fusion(bf16[1024,1152]{0,1:T(8,128)(2,1)S(1)} %divide_convert_fusion, bf16[1152,128]{1,0:T(8,128)(2,1)S(1)} %bitcast.187, f32[1024]{0:T(1024)S(1)} %fusion.9, bf16[16,8,8,128]{3,2,1,0:T(8,128)(2,1)S(1)} %bitcast.168), kind=kOutput, calls=%fused_computation.4 | convolution fusion | flops 307888128 | bytes 5279744 | tf_op jit(solution)/shard_map/dot_general | solution.py:226
  167.2 6.6 %all-to-all-done.3 = f32[8,1,128]{2,1,0:T(1,128)S(1)} async-done(((f32[8,1,128]{2,1,0:T(1,128)}), f32[8,1,128]{2,1,0:T(1,128)S(1)}, u32[]{:S(2)}, u32[]{:S(2)}) %all-to-all-start.3) | async-done | bytes 4128 | tf_op jit(solution)/shard_map/all_to_all | solution.py:181
  173.9 0.9 fusion.23
  175.4 0.9 fusion.22
  176.3 1.0 fusion.17
  177.4 5.2 %all-to-all-start.4 = ((bf16[8,128,256]{1,2,0:T(8,128)(2,1)}), bf16[8,128,256]{1,2,0:T(8,128)(2,1)S(1)}, u32[]{:S(2)}, u32[]{:S(2)}) async-start(bf16[8,128,256]{1,2,0:T(8,128)(2,1)} %fusion.17), calls=%async_computation.4 | async-start | bytes 1048576 | tf_op jit(solution)/shard_map/all_to_all | solution.py:42
  182.8 2.2 %fusion.10 = bf16[16,8,8,128]{3,1,2,0:T(8,128)(2,1)S(1)} fusion(bf16[1024,1152]{0,1:T(8,128)(2,1)} %fusion.1, bf16[1152,128]{1,0:T(8,128)(2,1)S(1)} %bitcast.185, f32[1024]{0:T(1024)S(1)} %broadcast_bitcast_fusion), kind=kOutput, calls=%fused_computation.24 | convolution fusion | flops 302252032 | bytes 2920448 | tf_op jit(solution)/shard_map/dot_general | solution.py:230
  185.3 0.8 copy.202
  186.1 11.0 %all-to-all-done.4 = bf16[8,128,256]{1,2,0:T(8,128)(2,1)S(1)} async-done(((bf16[8,128,256]{1,2,0:T(8,128)(2,1)}), bf16[8,128,256]{1,2,0:T(8,128)(2,1)S(1)}, u32[]{:S(2)}, u32[]{:S(2)}) %all-to-all-start.4) | async-done | bytes 524320 | tf_op jit(solution)/shard_map/all_to_all | solution.py:42
  197.4 1.3 collective-permute-start.14
  199.3 3.1 %collective-permute-done.14 = bf16[128,256]{0,1:T(8,128)(2,1)S(1)} collective-permute-done((bf16[128,256]{0,1:T(8,128)(2,1)S(1)}, bf16[128,256]{0,1:T(8,128)(2,1)S(1)}, u32[]{:S(2)}, u32[]{:S(2)}) %collective-permute-start.14) | collective-permute-done | bytes 65568 | tf_op jit(solution)/shard_map/ppermute | solution.py:52
  202.5 0.7 copy.144
  203.2 0.7 copy.145
  (110 shorter events, 10.4 us)
Async XLA Ops:
  2.5 40.4 %all-to-all-start = ((bf16[32,8,2048]{2,1,0:T(8,128)(2,1)}), bf16[32,8,2048]{2,1,0:T(8,128)(2,1)S(1)}, u32[]{:S(2)}, u32[]{:S(2)}) async-start(bf16[32,8,2048]{2,1,0:T(8,128)(2,1)} %broadcast_in_dim.78), calls=%async_computation | async-start | bytes 2097152 | tf_op jit(solution)/shard_map/all_to_all | solution.py:36
  17.5 0.6 copy-start.13
  18.8 21.5 %collective-permute-start = (bf16[1,144,256]{2,1,0:T(8,128)(2,1)S(1)}, bf16[1,144,256]{2,1,0:T(8,128)(2,1)S(1)}, u32[]{:S(2)}, u32[]{:S(2)}) collective-permute-start(bf16[1,144,256]{2,1,0:T(8,128)(2,1)S(1)} %maximum_bitcast_fusion), channel_id=1, source_target_pairs={{0,16},{2,18},{4,20},{6,22},{8,24},{10,26},{12,28},{14,30},{16,32}... | collective-permute-start | bytes 221192 | tf_op jit(solution)/shard_map/ppermute | solution.py:52
  22.0 12.6 %collective-permute-start.1 = (bf16[1,144,256]{2,1,0:T(8,128)(2,1)S(1)}, bf16[1,144,256]{2,1,0:T(8,128)(2,1)S(1)}, u32[]{:S(2)}, u32[]{:S(2)}) collective-permute-start(bf16[1,144,256]{2,1,0:T(8,128)(2,1)S(1)} %maximum_bitcast_fusion), channel_id=1, source_target_pairs={{0,2},{2,4},{4,6},{6,8},{8,10},{10,12},{12,14},{14,16},{16,18},{18... | collective-permute-start | bytes 221192 | tf_op jit(solution)/shard_map/ppermute | solution.py:52
  42.9 16.9 %collective-permute-start.2 = (bf16[256,2048]{1,0:T(8,128)(2,1)S(1)}, bf16[256,2048]{1,0:T(8,128)(2,1)}, u32[]{:S(2)}, u32[]{:S(2)}) collective-permute-start(bf16[256,2048]{1,0:T(8,128)(2,1)S(1)} %bitcast.170), channel_id=1, source_target_pairs={{0,2},{2,0},{4,6},{6,4},{8,10},{10,8},{12,14},{14,12},{16,18},{18,... | collective-permute-start | bytes 3145736 | tf_op jit(solution)/shard_map/ppermute | solution.py:27
  50.7 35.5 %all-to-all-start.1 = ((bf16[32,8,2048]{2,1,0:T(8,128)(2,1)}), bf16[32,8,2048]{2,1,0:T(8,128)(2,1)S(1)}, u32[]{:S(2)}, u32[]{:S(2)}) async-start(bf16[32,8,2048]{2,1,0:T(8,128)(2,1)} %broadcast_in_dim.81), calls=%async_computation.1 | async-start | bytes 2097152 | tf_op jit(solution)/shard_map/all_to_all | solution.py:36
  56.2 3.6 %copy-start.14 = (bf16[2048,1024]{1,0:T(8,128)(2,1)S(1)}, bf16[2048,1024]{1,0:T(8,128)(2,1)}, u32[]{:S(2)}) copy-start(bf16[2048,1024]{1,0:T(8,128)(2,1)} %param.11) | copy-start | bytes 12582916
  59.8 12.1 %copy-start.1 = (f32[4,2,4,8,1024]{4,3,2,1,0:T(8,128)}, f32[4,2,4,8,1024]{4,3,2,1,0:T(8,128)S(1)}, u32[]{:S(2)}) copy-start(f32[4,2,4,8,1024]{4,3,2,1,0:T(8,128)S(1)} %fusion.5) | copy-start | bytes 3145732
  59.8 17.0 %copy-start.9 = (f32[1024]{0:T(1024)S(1)}, f32[1024]{0:T(1024)}, u32[]{:S(2)}) copy-start(f32[1024]{0:T(1024)} %param.13) | copy-start | bytes 12292
  63.6 20.5 %collective-permute-start.5 = (bf16[2,2,4,8,1024]{4,3,2,1,0:T(8,128)(2,1)}, bf16[2,2,4,8,1024]{4,3,2,1,0:T(8,128)(2,1)S(1)}, u32[]{:S(2)}, u32[]{:S(2)}) collective-permute-start(bf16[2,2,4,8,1024]{4,3,2,1,0:T(8,128)(2,1)} %pad_maximum_fusion.5), channel_id=1, source_target_pairs={{0,256},{128,384},{256,0},{384,128},{1,257},{129,385},{257,1},{385... | collective-permute-start | bytes 786440 | tf_op jit(solution)/shard_map/ppermute | solution.py:56
  68.9 15.1 %collective-permute-start.4 = (bf16[2,2,4,8,1024]{4,3,2,1,0:T(8,128)(2,1)}, bf16[2,2,4,8,1024]{4,3,2,1,0:T(8,128)(2,1)S(1)}, u32[]{:S(2)}, u32[]{:S(2)}) collective-permute-start(bf16[2,2,4,8,1024]{4,3,2,1,0:T(8,128)(2,1)} %pad_maximum_fusion.4), channel_id=1, source_target_pairs={{0,128},{128,256},{256,384},{384,0},{1,129},{129,257},{257,385},{3... | collective-permute-start | bytes 786440 | tf_op jit(solution)/shard_map/ppermute | solution.py:56
  71.9 9.3 %collective-permute-start.3 = (bf16[2,2,4,8,1024]{4,3,2,1,0:T(8,128)(2,1)}, bf16[2,2,4,8,1024]{4,3,2,1,0:T(8,128)(2,1)S(1)}, u32[]{:S(2)}, u32[]{:S(2)}) collective-permute-start(bf16[2,2,4,8,1024]{4,3,2,1,0:T(8,128)(2,1)} %pad_maximum_fusion.3), channel_id=1, source_target_pairs={{0,384},{128,0},{256,128},{384,256},{1,385},{129,1},{257,129},{385... | collective-permute-start | bytes 786440 | tf_op jit(solution)/shard_map/ppermute | solution.py:56
  81.2 4.9 %collective-permute-start.6 = (bf16[2,144,256]{2,1,0:T(8,128)(2,1)S(1)}, bf16[2,144,256]{2,1,0:T(8,128)(2,1)S(1)}, u32[]{:S(2)}, u32[]{:S(2)}) collective-permute-start(bf16[2,144,256]{2,1,0:T(8,128)(2,1)S(1)} %pad_maximum_fusion.9), channel_id=1, source_target_pairs={{0,4},{2,6},{4,8},{6,10},{8,12},{10,14},{12,16},{14,18},{16,20},{1... | collective-permute-start | bytes 442376 | tf_op jit(solution)/shard_map/ppermute | solution.py:52
  86.2 9.8 %collective-permute-start.7 = (bf16[256,2048]{1,0:T(8,128)(2,1)S(1)}, bf16[256,2048]{1,0:T(8,128)(2,1)S(1)}, u32[]{:S(2)}, u32[]{:S(2)}) collective-permute-start(bf16[256,2048]{1,0:T(8,128)(2,1)S(1)} %bitcast.172), channel_id=1, source_target_pairs={{0,2},{2,0},{4,6},{6,4},{8,10},{10,8},{12,14},{14,12},{16,18},{18,... | collective-permute-start | bytes 3145736 | tf_op jit(solution)/shard_map/ppermute | solution.py:27
  92.2 3.7 %copy-start.15 = (bf16[2048,1024]{1,0:T(8,128)(2,1)S(1)}, bf16[2048,1024]{1,0:T(8,128)(2,1)}, u32[]{:S(2)}) copy-start(bf16[2048,1024]{1,0:T(8,128)(2,1)} %param.11) | copy-start | bytes 12582916
  95.9 15.6 %copy-start.4 = (bf16[128,1024]{1,0:T(8,128)(2,1)S(1)}, bf16[128,1024]{1,0:T(8,128)(2,1)}, u32[]{:S(2)}) copy-start(bf16[128,1024]{1,0:T(8,128)(2,1)} %param.15) | copy-start | bytes 786436
  97.2 14.7 %copy-start.10 = (s32[1024]{0:T(1024)S(1)}, s32[1024]{0:T(1024)}, u32[]{:S(2)}) copy-start(s32[1024]{0:T(1024)} %param.14) | copy-start | bytes 12292
  97.3 15.4 %copy-start.5 = (bf16[128,1024]{1,0:T(8,128)(2,1)S(1)}, bf16[128,1024]{1,0:T(8,128)(2,1)}, u32[]{:S(2)}) copy-start(bf16[128,1024]{1,0:T(8,128)(2,1)} %param.18) | copy-start | bytes 786436
  99.6 18.8 %collective-permute-start.11 = (bf16[2,2,4,8,1024]{4,3,2,0,1:T(8,128)(2,1)}, bf16[2,2,4,8,1024]{4,3,2,0,1:T(8,128)(2,1)S(1)}, u32[]{:S(2)}, u32[]{:S(2)}) collective-permute-start(bf16[2,2,4,8,1024]{4,3,2,0,1:T(8,128)(2,1)} %pad_maximum_fusion.7), channel_id=1, source_target_pairs={{0,256},{128,384},{256,0},{384,128},{1,257},{129,385},{257,1},{385... | collective-permute-start | bytes 786440 | tf_op jit(solution)/shard_map/ppermute | solution.py:56
  103.3 15.1 %collective-permute-start.10 = (bf16[2,2,4,8,1024]{4,3,2,0,1:T(8,128)(2,1)}, bf16[2,2,4,8,1024]{4,3,2,0,1:T(8,128)(2,1)S(1)}, u32[]{:S(2)}, u32[]{:S(2)}) collective-permute-start(bf16[2,2,4,8,1024]{4,3,2,0,1:T(8,128)(2,1)} %pad_maximum_fusion.6), channel_id=1, source_target_pairs={{0,128},{128,256},{256,384},{384,0},{1,129},{129,257},{257,385},{3... | collective-permute-start | bytes 786440 | tf_op jit(solution)/shard_map/ppermute | solution.py:56
  107.3 11.1 %collective-permute-start.9 = (bf16[2,2,4,8,1024]{4,3,2,0,1:T(8,128)(2,1)}, bf16[2,2,4,8,1024]{4,3,2,0,1:T(8,128)(2,1)S(1)}, u32[]{:S(2)}, u32[]{:S(2)}) collective-permute-start(bf16[2,2,4,8,1024]{4,3,2,0,1:T(8,128)(2,1)} %pad_maximum_fusion.8), channel_id=1, source_target_pairs={{0,384},{128,0},{256,128},{384,256},{1,385},{129,1},{257,129},{385... | collective-permute-start | bytes 786440 | tf_op jit(solution)/shard_map/ppermute | solution.py:56
  111.6 21.2 %copy-start.6 = (s32[2,4,2,8]{3,1,0,2:T(4,128)S(1)}, s32[2,4,2,8]{3,1,0,2:T(4,128)}, u32[]{:S(2)}) copy-start(s32[2,4,2,8]{3,1,0,2:T(4,128)} %copy.130) | copy-start | bytes 1540
  113.6 34.4 %copy-start.7 = (s32[1152]{0:T(1024)S(1)}, s32[1152]{0:T(1024)}, u32[]{:S(2)}) copy-start(s32[1152]{0:T(1024)} %iota_add_fusion) | copy-start | bytes 13828
  113.6 10.2 %collective-permute-start.8 = (bf16[2,4,8,1024]{3,2,1,0:T(8,128)(2,1)}, bf16[2,4,8,1024]{3,2,1,0:T(8,128)(2,1)S(1)}, u32[]{:S(2)}, u32[]{:S(2)}) collective-permute-start(bf16[2,4,8,1024]{3,2,1,0:T(8,128)(2,1)} %fusion.37), channel_id=1, source_target_pairs={{0,1},{1,0},{2,3},{3,2},{4,5},{5,4},{6,7},{7,6},{8,9},{9,8},{10,11... | collective-permute-start | bytes 393224 | tf_op jit(solution)/shard_map/ppermute | solution.py:60
  118.6 14.1 %collective-permute-start.12 = (bf16[2,4,8,1024]{3,2,1,0:T(8,128)(2,1)S(1)}, bf16[2,4,8,1024]{3,2,1,0:T(8,128)(2,1)S(1)}, u32[]{:S(2)}, u32[]{:S(2)}) collective-permute-start(bf16[2,4,8,1024]{3,2,1,0:T(8,128)(2,1)S(1)} %fusion.38), channel_id=1, source_target_pairs={{0,1},{1,0},{2,3},{3,2},{4,5},{5,4},{6,7},{7,6},{8,9},{9,8},{10,11... | collective-permute-start | bytes 393224 | tf_op jit(solution)/shard_map/ppermute | solution.py:60
  123.8 24.0 %collective-permute-start.13 = (bf16[4,144,256]{2,1,0:T(8,128)(2,1)S(1)}, bf16[4,144,256]{2,1,0:T(8,128)(2,1)S(1)}, u32[]{:S(2)}, u32[]{:S(2)}) collective-permute-start(bf16[4,144,256]{2,1,0:T(8,128)(2,1)S(1)} %pad_maximum_fusion.2), channel_id=1, source_target_pairs={{0,8},{2,10},{4,12},{6,14},{8,16},{10,18},{12,20},{14,22},{16,24},... | collective-permute-start | bytes 884744 | tf_op jit(solution)/shard_map/ppermute | solution.py:52
  134.7 24.0 %all-to-all-start.2 = ((f32[64,3,128]{2,1,0:T(4,128)}), f32[64,3,128]{2,1,0:T(4,128)S(1)}, u32[]{:S(2)}, u32[]{:S(2)}) async-start(f32[64,3,128]{2,1,0:T(4,128)} %broadcast_in_dim.83), calls=%async_computation.2 | async-start | bytes 262144 | tf_op jit(solution)/shard_map/all_to_all | solution.py:172
  148.0 3.8 %copy-start.2 = (bf16[9,128,128]{2,1,0:T(8,128)(2,1)}, bf16[9,128,128]{2,1,0:T(8,128)(2,1)S(1)}, u32[]{:S(2)}) copy-start(bf16[9,128,128]{2,1,0:T(8,128)(2,1)S(1)} %get-tuple-element.85) | copy-start | bytes 884740
  154.6 4.2 %copy-start.12 = (f32[128]{0:T(128)S(1)}, f32[128]{0:T(128)}, u32[]{:S(2)}) copy-start(f32[128]{0:T(128)} %reshape.223) | copy-start | bytes 1540
  154.6 19.1 %copy-start.8 = (s32[1024]{0:T(1024)S(1)}, s32[1024]{0:T(1024)}, u32[]{:S(2)}) copy-start(s32[1024]{0:T(1024)} %eq.59) | copy-start | bytes 12292
  154.6 19.1 %copy-start.11 = (s32[128]{0:T(128)S(1)}, s32[128]{0:T(128)}, u32[]{:S(2)}) copy-start(s32[128]{0:T(128)} %iota_add_fusion.2) | copy-start | bytes 1540
  159.4 14.3 %all-to-all-start.3 = ((f32[8,1,128]{2,1,0:T(1,128)}), f32[8,1,128]{2,1,0:T(1,128)S(1)}, u32[]{:S(2)}, u32[]{:S(2)}) async-start(f32[8,1,128]{2,1,0:T(1,128)} %broadcast_in_dim.86), calls=%async_computation.3 | async-start | bytes 8192 | tf_op jit(solution)/shard_map/all_to_all | solution.py:181
  173.7 1.7 copy-start
  175.4 7.4 %copy-start.3 = (bf16[9,128,128]{2,1,0:T(8,128)(2,1)S(1)}, bf16[9,128,128]{2,1,0:T(8,128)(2,1)}, u32[]{:S(2)}) copy-start(bf16[9,128,128]{2,1,0:T(8,128)(2,1)} %copy-done.2) | copy-start | bytes 884740
  177.4 19.7 %all-to-all-start.4 = ((bf16[8,128,256]{1,2,0:T(8,128)(2,1)}), bf16[8,128,256]{1,2,0:T(8,128)(2,1)S(1)}, u32[]{:S(2)}, u32[]{:S(2)}) async-start(bf16[8,128,256]{1,2,0:T(8,128)(2,1)} %fusion.17), calls=%async_computation.4 | async-start | bytes 1048576 | tf_op jit(solution)/shard_map/all_to_all | solution.py:42
  197.4 5.0 %collective-permute-start.14 = (bf16[128,256]{0,1:T(8,128)(2,1)S(1)}, bf16[128,256]{0,1:T(8,128)(2,1)S(1)}, u32[]{:S(2)}, u32[]{:S(2)}) collective-permute-start(bf16[128,256]{0,1:T(8,128)(2,1)S(1)} %get-tuple-element.71), channel_id=1, source_target_pairs={{16,0},{18,2},{20,4},{22,6},{24,8},{26,10},{28,12},{30,14},{32,16}... | collective-permute-start | bytes 196616 | tf_op jit(solution)/shard_map/ppermute | solution.py:52
